TPU v7x, 32 devices: a whole 2x2x4 slice. The times are simulated.
32 devices in a mesh: seq: 8 (over z, y), head: 4 (over x, core).
Axes of the slice: x: 2, y: 2, z: 4, core: 2. Of those that a mesh axis runs over, the one named last changes fastest.
Arguments:
- tokens: bfloat16 [4096, 2048], P('seq'), may hold values from -6 to 6
- w_query: bfloat16 [2048, 2048], P('seq', 'head'), may hold values from -0.125 to 0.125
- w_key: bfloat16 [2048, 2048], P('seq', 'head'), may hold values from -0.125 to 0.125
- w_value: bfloat16 [2048, 2048], P('seq', 'head'), may hold values from -0.125 to 0.125
- w_out: bfloat16 [2048, 2048], P('head', 'seq'), may hold values from -0.125 to 0.125
- level_weights: float32 [16, 13, 4096], P('head', None, 'seq'), may hold values from 0.2 to 2
Outputs:
- layer_output: bfloat16 [4096, 2048], P('seq', 'head')
All inputs are finite; a program needn't handle non-finite values.
Results may differ from a plain program's by a relative error of at most 0.017.
Values may be sent and summed in bfloat16 or wider, within the bound.
No kernel may reach another device: no remote copies, remote signals or barrier semaphores. Data moves between devices by JAX's collectives and lax.ppermute only.
A program may use at most 128 MiB of HBM per device.

v0:
```python
import jax
import jax.numpy as jnp
from jax import lax
from jax.sharding import PartitionSpec as P


def from_partner(array, axis, stride):
    return lax.ppermute(array, axis, [(i, i ^ 1 << stride) for i in range(lax.axis_size(axis))])


def bit_length(numbers, bit_count):
    total_bits = jnp.zeros(numbers.shape, jnp.int32)
    for bit_index in range(bit_count):
        total_bits = total_bits + (numbers >= 1 << bit_index).astype(jnp.int32)
    return total_bits


def per_device(tokens, w_query, w_key, w_value, w_out, level_weights):
    highest = lax.Precision.HIGHEST
    tok_rows = tokens.shape[0]
    local_bits = tok_rows.bit_length() - 1
    heads_here = level_weights.shape[0]
    head_dim = w_query.shape[1] // heads_here

    def add_rows(weight_piece):
        return jnp.dot(tokens, weight_piece, preferred_element_type=jnp.float32)

    query_sums = add_rows(lax.all_gather(w_query, "seq", axis=0, tiled=True))
    key_sums = add_rows(lax.all_gather(w_key, "seq", axis=0, tiled=True))
    value_sums = add_rows(lax.all_gather(w_value, "seq", axis=0, tiled=True))
    block_shape = (tok_rows, heads_here, head_dim)
    query_vectors = query_sums.astype(jnp.bfloat16).reshape(block_shape)
    key_vectors = key_sums.astype(jnp.bfloat16).reshape(block_shape)
    value_vectors = value_sums.astype(jnp.bfloat16).reshape(block_shape)
    states = jnp.einsum(
        "chd,che->hde", key_vectors, value_vectors, preferred_element_type=jnp.float32
    )
    query_float = query_vectors.astype(jnp.float32)
    device_index = lax.axis_index("seq")
    device_bits = lax.axis_size("seq").bit_length() - 1
    running = states
    scaled_list = []
    state_list = []
    for bit_index in range(device_bits):
        partner = from_partner(running.astype(jnp.bfloat16), "seq", bit_index).astype(running.dtype)
        upper_half = jnp.bitwise_and(jnp.right_shift(device_index, bit_index), 1).astype(
            jnp.float32
        )
        level_column = level_weights[:, local_bits + bit_index + 1, :].T[:, :, None]
        scaled_list.append(level_column * query_float)
        state_list.append(upper_half * partner)
        running = running + partner
    scaled_stack = jnp.stack(scaled_list, axis=2)
    state_stack = jnp.stack(state_list, axis=1)
    remote_part = jnp.einsum("chmd,hmde->che", scaled_stack, state_stack, precision=highest)
    positions = jnp.arange(tok_rows, dtype=jnp.int32)
    levels = bit_length(jnp.bitwise_xor(positions[:, None], positions[None, :]), local_bits)
    causal = positions[None, :] <= positions[:, None]
    scores = jnp.einsum(
        "thd,shd->hts", query_vectors, key_vectors, preferred_element_type=jnp.float32
    )
    mixing = jnp.zeros_like(scores)
    for level_index in range(local_bits + 1):
        mixing = mixing + level_weights[:, level_index, :][:, :, None] * (
            levels == level_index
        ).astype(jnp.float32)
    mixing = jnp.where(causal, mixing, jnp.zeros_like(mixing))
    weighted = (scores * mixing).astype(jnp.bfloat16)
    local_part = jnp.einsum(
        "hts,shd->thd", weighted, value_vectors, preferred_element_type=jnp.float32
    )
    combined = local_part + remote_part
    attended = combined * lax.rsqrt(jnp.mean(combined * combined, axis=-1, keepdims=True) + 1e-06)
    attended = attended.astype(jnp.bfloat16).reshape(tok_rows, heads_here * head_dim)
    partial_value = jnp.dot(
        attended,
        lax.all_gather(w_out, "seq", axis=1, tiled=True),
        preferred_element_type=jnp.float32,
    )
    return lax.psum_scatter(
        partial_value.astype(jnp.bfloat16), "head", scatter_dimension=1, tiled=True
    )


def solution(mesh):
    in_specs = (
        P("seq", None),
        P("seq", "head"),
        P("seq", "head"),
        P("seq", "head"),
        P("head", "seq"),
        P("head", None, "seq"),
    )
    out_specs = P("seq", "head")
    return jax.shard_map(
        per_device, mesh=mesh, in_specs=in_specs, out_specs=out_specs, check_vma=False
    )
```

profile of v0, /device:TPU:0, one launch (start us, length us, event | category | flops | bytes accessed | tf_op | source)
XLA Modules:
  0.0 254.7 jit_solution(8330552626429358013)
XLA Ops:
  6.5 0.0 copy-start
  6.5 0.7 all-gather.5.cloned.1.call-update
  7.3 0.0 all-gather.9.cloned.1.call-start
  7.3 0.7 all-gather.9.cloned.1.call-update
  8.0 0.0 all-gather.7.cloned.1.call-start
  8.1 0.7 all-gather.7.cloned.1.call-update
  8.7 0.0 all-gather.11.cloned.1.call-start
  8.8 0.5 all-gather.11.cloned.1.call-update
  9.3 0.0 reduce-scatter.2.cloned.1.call-start
  9.4 1.8 compare_convert_fusion.1
  11.2 1.7 compare_convert_fusion.3
  12.9 1.7 compare_convert_fusion.5
  14.6 1.7 compare_convert_fusion.7
  16.3 1.4 iota_compare_fusion
  17.7 0.7 slice_bitcast_fusion.12
  18.4 43.1 %all-gather.5.cloned.1.call-done = bf16[2048,512]{1,0:T(8,128)(2,1)} async-done(((bf16[256,512]{1,0:T(8,128)(2,1)}), bf16[2048,512]{1,0:T(8,128)(2,1)}) %all-gather.5.cloned.1.call-update) | async-done | bytes 2097168 | tf_op jit(solution)/shard_map/all_gather | solution.py:30
  61.5 2.9 %convolution_convert_fusion.3 = bf16[512,512]{0,1:T(8,128)(2,1)S(1)} fusion(bf16[512,2048]{1,0:T(8,128)(2,1)S(1)} %copy-done, bf16[2048,512]{1,0:T(8,128)(2,1)} %all-gather.5.cloned.1.call-done), kind=kOutput, calls=%fused_computation.31 | convolution fusion | flops 1074003968 | bytes 4718592 | tf_op jit(solution)/shard_map/dot_general | solution.py:26
  64.4 47.0 %all-gather.9.cloned.1.call-done = bf16[2048,512]{1,0:T(8,128)(2,1)} async-done(((bf16[256,512]{1,0:T(8,128)(2,1)}), bf16[2048,512]{1,0:T(8,128)(2,1)}) %all-gather.9.cloned.1.call-update) | async-done | bytes 2097168 | tf_op jit(solution)/shard_map/all_gather | solution.py:29
  111.4 2.9 %convolution_convert_fusion.1 = bf16[512,512]{0,1:T(8,128)(2,1)S(1)} fusion(bf16[512,2048]{1,0:T(8,128)(2,1)S(1)} %copy-done, bf16[2048,512]{1,0:T(8,128)(2,1)} %all-gather.9.cloned.1.call-done), kind=kOutput, calls=%fused_computation.29 | convolution fusion | flops 1074003968 | bytes 4718592 | tf_op jit(solution)/shard_map/dot_general | solution.py:26
  114.3 0.3 fusion.48
  114.7 0.5 copy-done.3
  115.1 0.6 collective-permute-start
  115.7 1.3 compare_convert_fusion.9
  117.0 3.1 %collective-permute-done = bf16[4,128,128]{2,1,0:T(8,128)(2,1)S(1)} collective-permute-done((bf16[4,128,128]{2,1,0:T(8,128)(2,1)S(1)}, bf16[4,128,128]{2,1,0:T(8,128)(2,1)S(1)}, u32[]{:S(2)}, u32[]{:S(2)}) %collective-permute-start) | collective-permute-done | bytes 131104 | tf_op jit(solution)/shard_map/ppermute | solution.py:8
  120.1 0.7 fusion.45
  120.8 1.5 collective-permute-start.1
  122.3 40.1 %all-gather.7.cloned.1.call-done = bf16[2048,512]{1,0:T(8,128)(2,1)} async-done(((bf16[256,512]{1,0:T(8,128)(2,1)}), bf16[2048,512]{1,0:T(8,128)(2,1)}) %all-gather.7.cloned.1.call-update) | async-done | bytes 2097168 | tf_op jit(solution)/shard_map/all_gather | solution.py:28
  162.4 3.7 %convolution_convert_fusion.2 = bf16[512,512]{0,1:T(8,128)(2,1)} fusion(bf16[512,2048]{1,0:T(8,128)(2,1)S(1)} %copy-done, bf16[2048,512]{1,0:T(8,128)(2,1)} %all-gather.7.cloned.1.call-done), kind=kOutput, calls=%fused_computation.30 | convolution fusion | flops 1074003968 | bytes 4718592 | tf_op jit(solution)/shard_map/dot_general | solution.py:26
  166.1 1.2 copy.8
  167.3 0.0 collective-permute-done.1
  167.3 1.0 fusion.42
  168.3 1.9 collective-permute-start.2
  170.2 1.7 broadcast_multiply_fusion.2
  171.9 7.2 %collective-permute-done.2 = bf16[4,128,128]{2,1,0:T(8,128)(2,1)S(1)} collective-permute-done((bf16[4,128,128]{2,1,0:T(8,128)(2,1)S(1)}, bf16[4,128,128]{2,1,0:T(8,128)(2,1)S(1)}, u32[]{:S(2)}, u32[]{:S(2)}) %collective-permute-start.2) | collective-permute-done | bytes 131104 | tf_op jit(solution)/shard_map/ppermute | solution.py:8
  179.1 0.0 copy-start.1
  179.1 0.0 copy-start.4
  179.1 0.0 copy-start.6
  179.1 0.0 copy-start.7
  179.1 0.0 copy-start.8
  179.1 0.0 copy-start.9
  179.1 0.0 copy-start.10
  179.2 4.4 %fusion.23 = f32[4,128,512]{2,1,0:T(8,128)} fusion(f32[4,1,128,128]{3,2,0,1:T(8,128)S(1)} %multiply_bitcast_fusion, f32[4,1,128,128]{3,2,0,1:T(8,128)S(1)} %get-tuple-element.10, f32[4,1,128,128]{3,2,0,1:T(8,128)S(1)} %get-tuple-element.8, f32[512,4,1,128]{3,0,2,1:T(8,128)S(1)} %get-tuple-element.6, f32[512,4,1,128]{3,0,2,1:T(8,128)S(1)} %get-tuple-element.7, ...), kind=kOutput, calls=%fused_computation.26 | convolution fusion | flops 1209925632 | bytes 4980736 | tf_op jit(solution)/shard_map/chmd,hmde->che/dot_general | solution.py:55
  183.6 9.5 %multiply_reduce_fusion = (f32[512,4]{0,1:T(4,128)S(1)}, f32[512,4,128]{0,2,1:T(8,128)}) fusion(f32[4,128,512]{2,1,0:T(8,128)} %fusion.23, bf16[512,4,128]{0,2,1:T(8,128)(2,1)} %bitcast.65, bf16[512,4,128]{0,2,1:T(8,128)(2,1)} %bitcast.62, bf16[512,4,128]{0,2,1:T(8,128)(2,1)} %bitcast.67, f32[512,512]{1,0:T(8,128)S(1)} %copy-done.1, ...), kind=kOutput, calls=%fused_computation.33 | convolution fusion | flops 560723968 | bytes 14508032 | tf_op jit(solution)/shard_map/hts,shd->thd/dot_general | solution.py:69
  193.2 1.4 multiply_convert_fusion.1
  194.5 19.6 %all-gather.11.cloned.1.call-done = bf16[512,2048]{1,0:T(8,128)(2,1)} async-done(((bf16[512,256]{1,0:T(8,128)(2,1)}), bf16[512,2048]{1,0:T(8,128)(2,1)}) %all-gather.11.cloned.1.call-update) | async-done | bytes 2097168 | tf_op jit(solution)/shard_map/all_gather | solution.py:77
  214.2 4.2 %convolution_convert_fusion = bf16[512,2048]{1,0:T(8,128)(2,1)} fusion(bf16[512,512]{0,1:T(8,128)(2,1)S(1)} %bitcast.63, bf16[512,2048]{1,0:T(8,128)(2,1)} %all-gather.11.cloned.1.call-done), kind=kOutput, calls=%fused_computation.4 | convolution fusion | flops 1074790400 | bytes 4718592 | tf_op jit(solution)/shard_map/dot_general | solution.py:75
  218.4 0.0 reduce-scatter.2.cloned.1.call-update
  218.4 29.8 %reduce-scatter.2.cloned.1.call-done = bf16[512,512]{1,0:T(8,128)(2,1)} async-done(((bf16[512,2048]{1,0:T(8,128)(2,1)}), bf16[512,512]{1,0:T(8,128)(2,1)}) %reduce-scatter.2.cloned.1.call-update) | async-done | bytes 524304 | tf_op jit(solution)/shard_map/reduce_scatter | solution.py:80
  (26 shorter events, 0.1 us)
Async XLA Ops:
  6.5 55.0 %copy-start = (bf16[512,2048]{1,0:T(8,128)(2,1)S(1)}, bf16[512,2048]{1,0:T(8,128)(2,1)}, u32[]{:S(2)}) copy-start(bf16[512,2048]{1,0:T(8,128)(2,1)} %param.6) | copy-start | bytes 6291460
  6.5 55.0 %all-gather.5.cloned.1.call-start = ((), (), s32[]{:S(2)}) async-start(), calls=%async_computation.1 | async-start | bytes 2359296 | tf_op jit(solution)/shard_map/all_gather | solution.py:30
  7.3 104.2 %all-gather.9.cloned.1.call-start = ((), (), s32[]{:S(2)}) async-start(), calls=%async_computation.3 | async-start | bytes 2359296 | tf_op jit(solution)/shard_map/all_gather | solution.py:29
  8.0 154.4 %all-gather.7.cloned.1.call-start = ((), (), s32[]{:S(2)}) async-start(), calls=%async_computation.2 | async-start | bytes 2359296 | tf_op jit(solution)/shard_map/all_gather | solution.py:28
  8.7 205.4 %all-gather.11.cloned.1.call-start = ((), (), s32[]{:S(2)}) async-start(), calls=%async_computation.4 | async-start | bytes 2359296 | tf_op jit(solution)/shard_map/all_gather | solution.py:77
  9.3 238.8 %reduce-scatter.2.cloned.1.call-start = ((), (), s32[]{:S(2)}) async-start(), calls=%async_computation.5 | async-start | bytes 2621440 | tf_op jit(solution)/shard_map/reduce_scatter | solution.py:80
  14.6 3.1 %copy-start.5 = (f32[4,13,512]{2,0,1:T(4,128)S(1)}, f32[4,13,512]{2,0,1:T(4,128)}, u32[]{:S(2)}) copy-start(f32[4,13,512]{2,0,1:T(4,128)} %param.11) | copy-start | bytes 319492
  64.4 49.9 %copy-start.2 = (bf16[512,512]{0,1:T(8,128)(2,1)}, bf16[512,512]{0,1:T(8,128)(2,1)S(1)}, u32[]{:S(2)}) copy-start(bf16[512,512]{0,1:T(8,128)(2,1)S(1)} %convolution_convert_fusion.3) | copy-start | bytes 1572868
  114.3 0.8 copy-start.3
  115.1 5.0 %collective-permute-start = (bf16[4,128,128]{2,1,0:T(8,128)(2,1)S(1)}, bf16[4,128,128]{2,1,0:T(8,128)(2,1)S(1)}, u32[]{:S(2)}, u32[]{:S(2)}) collective-permute-start(bf16[4,128,128]{2,1,0:T(8,128)(2,1)S(1)} %get-tuple-element.24), channel_id=1, source_target_pairs={{0,4},{4,0},{8,12},{12,8},{16,20},{20,16},{24,28},{28,24},{1,5},{5... | collective-permute-start | bytes 393224 | tf_op jit(solution)/shard_map/ppermute | solution.py:8
  120.8 46.5 %collective-permute-start.1 = (bf16[4,128,128]{2,1,0:T(8,128)(2,1)}, bf16[4,128,128]{2,1,0:T(8,128)(2,1)}, u32[]{:S(2)}, u32[]{:S(2)}) collective-permute-start(bf16[4,128,128]{2,1,0:T(8,128)(2,1)} %fusion.45), channel_id=1, source_target_pairs={{0,8},{4,12},{8,0},{12,4},{16,24},{20,28},{24,16},{28,20},{1,9},{5... | collective-permute-start | bytes 393224 | tf_op jit(solution)/shard_map/ppermute | solution.py:8
  168.3 10.7 %collective-permute-start.2 = (bf16[4,128,128]{2,1,0:T(8,128)(2,1)S(1)}, bf16[4,128,128]{2,1,0:T(8,128)(2,1)S(1)}, u32[]{:S(2)}, u32[]{:S(2)}) collective-permute-start(bf16[4,128,128]{2,1,0:T(8,128)(2,1)S(1)} %get-tuple-element.9), channel_id=1, source_target_pairs={{0,16},{4,20},{8,24},{12,28},{16,0},{20,4},{24,8},{28,12},{1,17},{... | collective-permute-start | bytes 393224 | tf_op jit(solution)/shard_map/ppermute | solution.py:8
  179.1 4.5 %copy-start.1 = (f32[512,512]{1,0:T(8,128)S(1)}, f32[512,512]{1,0:T(8,128)}, u32[]{:S(2)}) copy-start(f32[512,512]{1,0:T(8,128)} %get-tuple-element.29) | copy-start | bytes 3145732
  179.1 4.5 %copy-start.4 = (pred[512,512]{1,0:T(8,128)(4,1)S(1)}, pred[512,512]{1,0:T(8,128)(4,1)}, u32[]{:S(2)}) copy-start(pred[512,512]{1,0:T(8,128)(4,1)} %get-tuple-element.28) | copy-start | bytes 786436
  179.1 4.5 %copy-start.6 = (f32[4,512]{1,0:T(4,128)S(1)}, f32[4,512]{1,0:T(4,128)}, u32[]{:S(2)}) copy-start(f32[4,512]{1,0:T(4,128)} %get-tuple-element.11) | copy-start | bytes 24580
  179.1 4.5 %copy-start.7 = (f32[4,512]{1,0:T(4,128)S(1)}, f32[4,512]{1,0:T(4,128)}, u32[]{:S(2)}) copy-start(f32[4,512]{1,0:T(4,128)} %get-tuple-element.13) | copy-start | bytes 24580
  179.1 4.5 %copy-start.8 = (f32[4,512]{1,0:T(4,128)S(1)}, f32[4,512]{1,0:T(4,128)}, u32[]{:S(2)}) copy-start(f32[4,512]{1,0:T(4,128)} %get-tuple-element.14) | copy-start | bytes 24580
  179.1 4.5 %copy-start.9 = (f32[4,512]{1,0:T(4,128)S(1)}, f32[4,512]{1,0:T(4,128)}, u32[]{:S(2)}) copy-start(f32[4,512]{1,0:T(4,128)} %get-tuple-element.15) | copy-start | bytes 24580
  179.1 4.5 %copy-start.10 = (f32[4,512]{1,0:T(4,128)S(1)}, f32[4,512]{1,0:T(4,128)}, u32[]{:S(2)}) copy-start(f32[4,512]{1,0:T(4,128)} %get-tuple-element.16) | copy-start | bytes 24580
  179.1 4.5 %copy-start.11 = (f32[4,512]{1,0:T(4,128)S(1)}, f32[4,512]{1,0:T(4,128)}, u32[]{:S(2)}) copy-start(f32[4,512]{1,0:T(4,128)} %get-tuple-element.17) | copy-start | bytes 24580
  179.1 4.5 %copy-start.12 = (f32[4,512]{1,0:T(4,128)S(1)}, f32[4,512]{1,0:T(4,128)}, u32[]{:S(2)}) copy-start(f32[4,512]{1,0:T(4,128)} %get-tuple-element.18) | copy-start | bytes 24580
  179.2 4.5 %copy-start.13 = (f32[4,512]{1,0:T(4,128)S(1)}, f32[4,512]{1,0:T(4,128)}, u32[]{:S(2)}) copy-start(f32[4,512]{1,0:T(4,128)} %get-tuple-element.19) | copy-start | bytes 24580
  179.2 4.5 %copy-start.14 = (f32[4,512]{1,0:T(4,128)S(1)}, f32[4,512]{1,0:T(4,128)}, u32[]{:S(2)}) copy-start(f32[4,512]{1,0:T(4,128)} %get-tuple-element.20) | copy-start | bytes 24580
  179.2 4.5 %copy-start.15 = (f32[4,512]{1,0:T(4,128)S(1)}, f32[4,512]{1,0:T(4,128)}, u32[]{:S(2)}) copy-start(f32[4,512]{1,0:T(4,128)} %get-tuple-element.21) | copy-start | bytes 24580
Sparse Core Ops, SparseCore 0:
  9.5 51.9 all-gather.4
  63.6 47.7 all-gather.8
  113.6 48.7 all-gather.6
  164.3 49.8 all-gather.10
  218.5 29.5 reduce-scatter.1
where the time goes:
time: 255 us
  waiting for transfers between devices  193 us (76%)
  matrix products  27.8 us (11%)
  other arithmetic  14.4 us (6%)
  between operations  13.4 us (5%)
  starting transfers between devices  4.07 us (2%)
    all_gather x1, waiting for transfers between devices, per_device(): key_sums = add_rows(lax.all_gather(w_key, 'seq', axis=0, tiled=True))  47 us
    all_gather x1, waiting for transfers between devices, per_device(): value_sums = add_rows(lax.all_gather(w_value, 'seq', axis=0, tiled=True))  43.1 us
    all_gather x1, waiting for transfers between devices, per_device(): query_sums = add_rows(lax.all_gather(w_query, 'seq', axis=0, tiled=True))  40.1 us
    reduce_scatter x1, waiting for transfers between devices, per_device(): lax.psum_scatter(partial_value.astype(jnp.bfloat16), 'head', scatter_dime...  29.8 us
    all_gather x1, waiting for transfers between devices, per_device(): lax.all_gather(w_out, 'seq', axis=1, tiled=True)  19.6 us
    ppermute x3, waiting for transfers between devices, from_partner(): lax.ppermute(array, axis, [(i, i ^ 1 << stride) for i in range(lax.axis_s...  10.3 us
    dot_general x1, matrix products, per_device(): jnp.einsum('hts,shd->thd', weighted, value_vectors, preferred_element_typ...  9.5 us
    dot_general x3, matrix products, add_rows(): return jnp.dot(tokens, weight_piece, preferred_element_type=jnp.float32)  9.44 us
  transfers between devices with their start and end apart: 8, of which 7 were waited for; matrix products, arithmetic and copies ran while one was open for 16% of the time, Pallas kernels for 0%

commit v1 on v0

v1 whole, which is shorter than its diff:
```python
import functools

import jax
import jax.numpy as jnp
from jax import lax
from jax.experimental import pallas as pl
from jax.experimental.pallas import tpu as pltpu
from jax.sharding import PartitionSpec as P

F32, BF16 = jnp.float32, jnp.bfloat16
LONGEST_RING = 16
VMEM = pl.BlockSpec(memory_space=pltpu.VMEM)
SMEM = pl.BlockSpec(memory_space=pltpu.SMEM)


def call(kernel, outs, operands, flops, scratch=(), **grid):
    nbytes = sum(a.size * a.dtype.itemsize for a in (*operands, *outs))
    return pl.pallas_call(
        kernel,
        out_shape=outs,
        scratch_shapes=list(scratch),
        compiler_params=pltpu.CompilerParams(vmem_limit_bytes=48 * 2**20),
        cost_estimate=pl.CostEstimate(flops=flops, bytes_accessed=nbytes, transcendentals=0),
        **grid,
    )(*operands)


def ring_order(n):
    return list(range(0, n, 2)) + list(range(n - 1, 0, -2))


def ring_position(index, n):
    return jnp.where(index % 2 == 0, index // 2, n - 1 - index // 2)


def ring_owner(position, n):
    position = (position + n) % n
    return jnp.where(position < n // 2, 2 * position, 2 * (n - 1 - position) + 1)


def gather_pieces(piece, n):
    order = ring_order(n)
    onward = [(order[i], order[(i + 1) % n]) for i in range(n)]
    back = [(b, a) for a, b in onward]
    here = ring_position(lax.axis_index("seq"), n)
    pieces = [(piece, lax.axis_index("seq"), 0)]
    up = down = piece
    for step in range(1, n // 2):
        up = lax.ppermute(up, "seq", onward)
        down = lax.ppermute(down, "seq", back)
        pieces.append((up, ring_owner(here - step, n), 0))
        pieces.append((down, ring_owner(here + step, n), 0))
    half = piece.shape[0] // 2
    last = ring_owner(here + n // 2, n)
    pieces.append((lax.ppermute(up[:half], "seq", onward), last, 0))
    pieces.append((lax.ppermute(down[half:], "seq", back), last, half))
    return pieces


def gather_rows(piece, n):
    if n > LONGEST_RING or n % 2:
        return [(lax.all_gather(piece, "seq", axis=0, tiled=True), jnp.int32(0))]
    rows = piece.shape[0]
    return [(a, owner * rows + first) for a, owner, first in gather_pieces(piece, n)]


def place(starts, pieces, whole):
    for i, piece in enumerate(pieces):
        rows = piece.shape[0]
        whole[pl.ds(pl.multiple_of(starts[i], rows), rows), :] = piece[...]


def project_kernel(starts, tokens, *refs):
    *pieces, out, whole = refs
    place(starts, pieces, whole)
    width = min(256, out.shape[1])
    for low in range(0, out.shape[1], width):
        cols = slice(low, low + width)
        out[:, cols] = jnp.dot(
            tokens[...], whole[:, cols], preferred_element_type=F32
        ).astype(BF16)


def project(tokens, pieces):
    arrays = [a for a, _ in pieces]
    starts = jnp.stack([jnp.asarray(s, jnp.int32) for _, s in pieces])
    rows, depth = tokens.shape
    width = arrays[0].shape[1]
    return call(
        project_kernel,
        [jax.ShapeDtypeStruct((rows, width), BF16)],
        [starts, tokens, *arrays],
        2 * rows * depth * width,
        [pltpu.VMEM((depth, width), BF16)],
        in_specs=[SMEM, VMEM] + [VMEM] * len(arrays),
        out_specs=[VMEM],
    )[0]


def states_kernel(keys, values, states, rounded):
    for h in range(states.shape[0]):
        cols = slice(h * states.shape[1], (h + 1) * states.shape[1])
        sums = lax.dot_general(
            keys[:, cols], values[:, cols], (((0,), (0,)), ((), ())), preferred_element_type=F32
        )
        states[h] = sums
        rounded[h] = sums.astype(BF16)


def key_value_states(keys, values, heads):
    rows, width = keys.shape
    shape = (heads, width // heads, width // heads)
    return call(
        states_kernel,
        [jax.ShapeDtypeStruct(shape, F32), jax.ShapeDtypeStruct(shape, BF16)],
        [keys, values],
        2 * rows * width * shape[-1],
        in_specs=[VMEM] * 2,
        out_specs=[VMEM] * 2,
    )


def mixing_kernel(bits, weights, mixing):
    rows = mixing.shape[1]
    tile = min(256, rows)
    tile_bits = tile.bit_length() - 1
    column = lambda level, low: weights[0, low : low + tile, level : level + 1]
    t = lax.broadcasted_iota(jnp.int32, (tile, tile), 0)
    s = lax.broadcasted_iota(jnp.int32, (tile, tile), 1)
    apart = jnp.bitwise_xor(t, s)
    for low in range(0, rows, tile):
        for left in range(0, low, tile):
            level = tile_bits + ((low // tile) ^ (left // tile)).bit_length()
            mixing[0, low : low + tile, left : left + tile] = jnp.broadcast_to(
                column(level, low), (tile, tile)
            )
        mixed = jnp.broadcast_to(column(0, low), (tile, tile))
        for level in range(1, tile_bits + 1):
            mixed = jnp.where(apart >= 1 << (level - 1), column(level, low), mixed)
        mixing[0, low : low + tile, low : low + tile] = jnp.where(s <= t, mixed, 0.0)


def mixing_matrix(weights_by_token, bits):
    heads, rows, levels = weights_by_token.shape
    return call(
        functools.partial(mixing_kernel, bits),
        [jax.ShapeDtypeStruct((heads, rows, rows), F32)],
        [weights_by_token],
        heads * rows * rows * 10,
        grid=(heads,),
        in_specs=[pl.BlockSpec((1, rows, levels), lambda h: (h, 0, 0))],
        out_specs=[pl.BlockSpec((1, rows, rows), lambda h: (h, 0, 0))],
    )[0]


def attend_kernel(first_level, queries, keys, values, mixing, weights, *refs):
    *states, out = refs
    rows = queries.shape[0]
    tile = min(256, rows)
    for low in range(0, rows, tile):
        high = low + tile
        query = queries[low:high, :]
        scores = lax.dot_general(
            query, keys[:high, :], (((1,), (1,)), ((), ())), preferred_element_type=F32
        )
        mixed = (scores * mixing[0, low:high, :high]).astype(BF16)
        total = jnp.dot(mixed, values[:high, :], preferred_element_type=F32)
        for bit, state in enumerate(states):
            level = first_level + bit
            total += weights[0, low:high, level : level + 1] * jnp.dot(
                query, state[0], preferred_element_type=F32
            )
        scale = lax.rsqrt(jnp.mean(total * total, axis=-1, keepdims=True) + 1e-06)
        out[low:high, :] = (total * scale).astype(BF16)


def attend(queries, keys, values, mixing, weights_by_token, states, first_level):
    rows, width = queries.shape
    heads, _, levels = weights_by_token.shape
    dim = width // heads
    by_head = pl.BlockSpec((rows, dim), lambda h: (0, h))
    return call(
        functools.partial(attend_kernel, first_level),
        [jax.ShapeDtypeStruct((rows, width), BF16)],
        [queries, keys, values, mixing, weights_by_token, *states],
        heads * (4 * rows * rows * dim + 6 * rows * dim * dim),
        grid=(heads,),
        in_specs=[by_head] * 3
        + [
            pl.BlockSpec((1, rows, rows), lambda h: (h, 0, 0)),
            pl.BlockSpec((1, rows, levels), lambda h: (h, 0, 0)),
        ]
        + [pl.BlockSpec((1, dim, dim), lambda h: (h, 0, 0))] * len(states),
        out_specs=[by_head],
    )[0]


def output_kernel(count, starts, *refs):
    attended, pieces, (out, whole) = refs[:count], refs[count:-2], refs[-2:]
    for i, piece in enumerate(pieces):
        rows, cols = piece.shape
        down = pl.ds(pl.multiple_of(starts[0, i], rows), rows)
        along = pl.ds(pl.multiple_of(starts[1, i], cols), cols)
        whole[down, along] = piece[...]
    depth = attended[0].shape[1]
    total = jnp.zeros(out.shape, F32)
    for i, block in enumerate(attended):
        total += jnp.dot(
            block[...], whole[i * depth : (i + 1) * depth, :], preferred_element_type=F32
        )
    out[...] = total.astype(BF16)


def output(attended, pieces):
    arrays = [a for a, _, _ in pieces]
    starts = jnp.stack(
        [jnp.stack([jnp.asarray(p[i], jnp.int32) for p in pieces]) for i in (1, 2)]
    )
    rows, part = attended[0].shape
    depth = part * len(attended)
    width = sum(a.size for a in arrays) // depth
    return call(
        functools.partial(output_kernel, len(attended)),
        [jax.ShapeDtypeStruct((rows, width), BF16)],
        [starts, *attended, *arrays],
        2 * rows * depth * width,
        [pltpu.VMEM((depth, width), BF16)],
        in_specs=[SMEM] + [VMEM] * (len(attended) + len(arrays)),
        out_specs=[VMEM],
    )[0]


def per_device(tokens, w_query, w_key, w_value, w_out, level_weights):
    n = lax.axis_size("seq")
    groups = lax.axis_size("head")
    here = lax.axis_index("seq")
    group = lax.axis_index("head")
    rows = tokens.shape[0]
    local_bits = rows.bit_length() - 1
    heads = level_weights.shape[0]

    share = n // groups
    moves = [
        (s * groups + h, (s % share * groups + h) * groups + s // share)
        for s in range(n)
        for h in range(groups)
    ]
    out_piece = lax.ppermute(w_out, ("seq", "head"), moves)

    weights_by_token = level_weights.transpose(0, 2, 1)
    mixing = mixing_matrix(weights_by_token, local_bits)

    keys = project(tokens, gather_rows(w_key, n))
    values = project(tokens, gather_rows(w_value, n))
    running, rounded = key_value_states(keys, values, heads)
    states = []
    for bit in range(n.bit_length() - 1):
        partner = lax.ppermute(rounded, "seq", [(i, i ^ 1 << bit) for i in range(n)])
        upper = jnp.bitwise_and(jnp.right_shift(here, bit), 1)
        states.append(partner * upper.astype(BF16))
        running = running + partner.astype(F32)
        rounded = running.astype(BF16)
    queries = project(tokens, gather_rows(w_query, n))
    attended = attend(
        queries, keys, values, mixing, weights_by_token, states, local_bits + 1
    )

    blocks = {0: attended}
    for bit in reversed(range(groups.bit_length() - 1)):
        pairs = [(i, i ^ 1 << bit) for i in range(groups)]
        blocks |= {k ^ 1 << bit: lax.ppermute(a, "head", pairs) for k, a in blocks.items()}
    blocks = [blocks[k] for k in range(groups)]

    depth = w_out.shape[0]
    if n > LONGEST_RING or n % 2:
        gathered = lax.all_gather(out_piece, "seq", axis=0)
        gathered = gathered.reshape(share, groups, depth, -1).transpose(1, 2, 0, 3)
        gathered = gathered.reshape(groups, depth, -1)
        pieces = [
            (lax.dynamic_index_in_dim(gathered, g ^ group, 0, False), g * depth, 0)
            for g in range(groups)
        ]
    else:
        pieces = [
            (a, (owner % groups ^ group) * depth + first, owner // groups * a.shape[1])
            for a, owner, first in gather_pieces(out_piece, n)
        ]
    return output(blocks, pieces)


def solution(mesh):
    in_specs = (
        P("seq", None),
        P("seq", "head"),
        P("seq", "head"),
        P("seq", "head"),
        P("head", "seq"),
        P("head", None, "seq"),
    )
    out_specs = P("seq", "head")
    return jax.shard_map(
        per_device, mesh=mesh, in_specs=in_specs, out_specs=out_specs, check_vma=False
    )
```

time: 255 us -> 142 us (0.56)
  waiting for transfers between devices: 193 us -> 50.8 us
  starting transfers between devices: 4.07 us -> 49.1 us
  matrix products: 27.8 us -> 0 us
  Pallas kernels: 0 us -> 18.5 us
  local copies, waits for them, and re-layouts: 2.43 us -> 19.5 us
  between operations: 13.4 us -> 0.41 us
  other arithmetic: 14.4 us -> 2.84 us
    all_gather x4 -> x0, waiting for transfers between devices: 150 us -> none  [the longest x1 47 us: per_device(): key_sums = add_rows(lax.all_gather(w_key, 'seq', axis=0, tiled=True))]
    ppermute x3 -> x39, starting transfers between devices: 3.92 us -> 49.1 us  [the longest x12 19.4 us: gather_pieces(): up = lax.ppermute(up, 'seq', onward)]
    ppermute x3 -> x39, waiting for transfers between devices: 10.3 us -> 50.8 us  [the longest x12 33.3 us: gather_pieces(): up = lax.ppermute(up, 'seq', onward)]
    reduce_scatter x1 -> x0, waiting for transfers between devices: 29.8 us -> none  [per_device(): lax.psum_scatter(partial_value.astype(jnp.bfloat16), 'head', scatter_dime...]
    dot_general x7 -> x0, matrix products: 27.8 us -> none  [the longest x1 9.5 us: per_device(): jnp.einsum('hts,shd->thd', weighted, value_vectors, preferred_element_typ...]
    pallas_call x0 -> x7, Pallas kernels: none -> 18.5 us  [call(): pl.pallas_call(kernel, out_shape=outs, scratch_shapes=list(scratch), comp...]
    unnamed x32 -> x61, local copies, waits for them, and re-layouts: 0.53 us -> 14 us
    convert_element_type x7 -> x2, other arithmetic: 10.3 us -> 1.89 us  [per_device(): rounded = running.astype(BF16)]
  transfers between devices with their start and end apart: 8 -> 39, of which waited for: 7 -> 18; matrix products, arithmetic and copies ran while one was open for 16% -> 7% of each run, Pallas kernels for 0% -> 11%
where the time goes in v1:
time: 142 us; the launch traced here: 141 us
  waiting for transfers between devices  50.8 us (36%)
  starting transfers between devices  49.1 us (35%)
  local copies, waits for them, and re-layouts  19.5 us (14%)
  Pallas kernels  18.5 us (13%)
  other arithmetic  2.84 us (2%)
    ppermute x12, waiting for transfers between devices, gather_pieces(): up = lax.ppermute(up, 'seq', onward)  33.3 us
    ppermute x12, starting transfers between devices, gather_pieces(): up = lax.ppermute(up, 'seq', onward)  19.4 us
    pallas_call x7, Pallas kernels, call(): pl.pallas_call(kernel, out_shape=outs, scratch_shapes=list(scratch), comp...  18.5 us
    unnamed x61, local copies, waits for them, and re-layouts  14 us
    ppermute x12, starting transfers between devices, gather_pieces(): down = lax.ppermute(down, 'seq', back)  14 us
    ppermute x3, waiting for transfers between devices, per_device(): lax.ppermute(rounded, 'seq', [(i, i ^ 1 << bit) for i in range(n)])  12.9 us
    ppermute x4, starting transfers between devices, gather_pieces(): pieces.append((lax.ppermute(down[half:], 'seq', back), last, half))  6.78 us
    ppermute x1, starting transfers between devices, per_device(): out_piece = lax.ppermute(w_out, ('seq', 'head'), moves)  3.59 us
  transfers between devices with their start and end apart: 39, of which 18 were waited for; matrix products, arithmetic and copies ran while one was open for 7% of the time, Pallas kernels for 11%

profile of v1, /device:TPU:0, one launch (start us, length us, event | category | flops | bytes accessed | tf_op | source)
XLA Modules:
  0.0 141.2 jit_solution(6435015671053990275)
XLA Ops:
  0.0 3.0 %collective-permute-start = (bf16[256,512]{1,0:T(8,128)(2,1)}, bf16[256,512]{1,0:T(8,128)(2,1)S(1)}, u32[]{:S(2)}, u32[]{:S(2)}) collective-permute-start(bf16[256,512]{1,0:T(8,128)(2,1)} %refs_0_.3), channel_id=1, source_target_pairs={{0,8},{8,16},{16,24},{24,28},{28,20},{20,12},{12,4},{4,0},{1,9},{9... | collective-permute-start | bytes 786440 | tf_op jit(solution)/shard_map/ppermute | solution.py:49
  3.0 2.0 %collective-permute-start.8 = (bf16[256,512]{1,0:T(8,128)(2,1)}, bf16[256,512]{1,0:T(8,128)(2,1)S(1)}, u32[]{:S(2)}, u32[]{:S(2)}) collective-permute-start(bf16[256,512]{1,0:T(8,128)(2,1)} %refs_0_.4), channel_id=1, source_target_pairs={{0,8},{8,16},{16,24},{24,28},{28,20},{20,12},{12,4},{4,0},{1,9},{9... | collective-permute-start | bytes 786440 | tf_op jit(solution)/shard_map/ppermute | solution.py:49
  5.1 2.0 %collective-permute-start.16 = (bf16[256,512]{1,0:T(8,128)(2,1)}, bf16[256,512]{1,0:T(8,128)(2,1)S(1)}, u32[]{:S(2)}, u32[]{:S(2)}) collective-permute-start(bf16[256,512]{1,0:T(8,128)(2,1)} %refs_0_.5), channel_id=1, source_target_pairs={{0,8},{8,16},{16,24},{24,28},{28,20},{20,12},{12,4},{4,0},{1,9},{9... | collective-permute-start | bytes 786440 | tf_op jit(solution)/shard_map/ppermute | solution.py:49
  7.1 3.2 %collective-permute-done.refs_1_ = bf16[256,512]{1,0:T(8,128)(2,1)S(1)} collective-permute-done((bf16[256,512]{1,0:T(8,128)(2,1)}, bf16[256,512]{1,0:T(8,128)(2,1)S(1)}, u32[]{:S(2)}, u32[]{:S(2)}) %collective-permute-start) | collective-permute-done | bytes 262176 | tf_op jit(solution)/shard_map/ppermute | solution.py:49
  10.3 2.1 %collective-permute-start.17 = (bf16[256,512]{1,0:T(8,128)(2,1)}, bf16[256,512]{1,0:T(8,128)(2,1)S(1)}, u32[]{:S(2)}, u32[]{:S(2)}) collective-permute-start(bf16[256,512]{1,0:T(8,128)(2,1)} %refs_0_.5), channel_id=1, source_target_pairs={{8,0},{16,8},{24,16},{28,24},{20,28},{12,20},{4,12},{0,4},{9,1},{1... | collective-permute-start | bytes 786440 | tf_op jit(solution)/shard_map/ppermute | solution.py:50
  12.5 1.6 %collective-permute-start.2 = (bf16[256,512]{1,0:T(8,128)(2,1)S(1)}, bf16[256,512]{1,0:T(8,128)(2,1)S(1)}, u32[]{:S(2)}, u32[]{:S(2)}) collective-permute-start(bf16[256,512]{1,0:T(8,128)(2,1)S(1)} %collective-permute-done.refs_1_), channel_id=1, source_target_pairs={{0,8},{8,16},{16,24},{24,28},{28,20},{20,12},{12,4},{4,0},{1,9},{9... | collective-permute-start | bytes 786440 | tf_op jit(solution)/shard_map/ppermute | solution.py:49
  14.7 1.2 collective-permute-done.8.refs_1_
  15.9 2.1 %collective-permute-start.10 = (bf16[256,512]{1,0:T(8,128)(2,1)S(1)}, bf16[256,512]{1,0:T(8,128)(2,1)S(1)}, u32[]{:S(2)}, u32[]{:S(2)}) collective-permute-start(bf16[256,512]{1,0:T(8,128)(2,1)S(1)} %collective-permute-done.8.refs_1_), channel_id=1, source_target_pairs={{0,8},{8,16},{16,24},{24,28},{28,20},{20,12},{12,4},{4,0},{1,9},{9... | collective-permute-start | bytes 786440 | tf_op jit(solution)/shard_map/ppermute | solution.py:49
  18.1 3.5 %collective-permute-done.16.refs_1_ = bf16[256,512]{1,0:T(8,128)(2,1)S(1)} collective-permute-done((bf16[256,512]{1,0:T(8,128)(2,1)}, bf16[256,512]{1,0:T(8,128)(2,1)S(1)}, u32[]{:S(2)}, u32[]{:S(2)}) %collective-permute-start.16) | collective-permute-done | bytes 262176 | tf_op jit(solution)/shard_map/ppermute | solution.py:49
  21.5 2.1 %collective-permute-start.18 = (bf16[256,512]{1,0:T(8,128)(2,1)S(1)}, bf16[256,512]{1,0:T(8,128)(2,1)S(1)}, u32[]{:S(2)}, u32[]{:S(2)}) collective-permute-start(bf16[256,512]{1,0:T(8,128)(2,1)S(1)} %collective-permute-done.16.refs_1_), channel_id=1, source_target_pairs={{0,8},{8,16},{16,24},{24,28},{28,20},{20,12},{12,4},{4,0},{1,9},{9... | collective-permute-start | bytes 786440 | tf_op jit(solution)/shard_map/ppermute | solution.py:49
  23.7 3.5 %collective-permute-done.2.refs_3_ = bf16[256,512]{1,0:T(8,128)(2,1)S(1)} collective-permute-done((bf16[256,512]{1,0:T(8,128)(2,1)S(1)}, bf16[256,512]{1,0:T(8,128)(2,1)S(1)}, u32[]{:S(2)}, u32[]{:S(2)}) %collective-permute-start.2) | collective-permute-done | bytes 262176 | tf_op jit(solution)/shard_map/ppermute | solution.py:49
  27.2 2.1 %collective-permute-start.3 = (bf16[256,512]{1,0:T(8,128)(2,1)S(1)}, bf16[256,512]{1,0:T(8,128)(2,1)S(1)}, u32[]{:S(2)}, u32[]{:S(2)}) collective-permute-start(bf16[256,512]{1,0:T(8,128)(2,1)S(1)} %collective-permute-done.1.refs_2_), channel_id=1, source_target_pairs={{8,0},{16,8},{24,16},{28,24},{20,28},{12,20},{4,12},{0,4},{9,1},{1... | collective-permute-start | bytes 786440 | tf_op jit(solution)/shard_map/ppermute | solution.py:50
  29.9 2.9 %collective-permute-done.10.refs_3_ = bf16[256,512]{1,0:T(8,128)(2,1)S(1)} collective-permute-done((bf16[256,512]{1,0:T(8,128)(2,1)S(1)}, bf16[256,512]{1,0:T(8,128)(2,1)S(1)}, u32[]{:S(2)}, u32[]{:S(2)}) %collective-permute-start.10) | collective-permute-done | bytes 262176 | tf_op jit(solution)/shard_map/ppermute | solution.py:49
  32.8 2.1 %collective-permute-start.12 = (bf16[256,512]{1,0:T(8,128)(2,1)S(1)}, bf16[256,512]{1,0:T(8,128)(2,1)S(1)}, u32[]{:S(2)}, u32[]{:S(2)}) collective-permute-start(bf16[256,512]{1,0:T(8,128)(2,1)S(1)} %collective-permute-done.10.refs_3_), channel_id=1, source_target_pairs={{0,8},{8,16},{16,24},{24,28},{28,20},{20,12},{12,4},{4,0},{1,9},{9... | collective-permute-start | bytes 786440 | tf_op jit(solution)/shard_map/ppermute | solution.py:49
  36.3 2.1 %collective-permute-done.18.refs_3_ = bf16[256,512]{1,0:T(8,128)(2,1)S(1)} collective-permute-done((bf16[256,512]{1,0:T(8,128)(2,1)S(1)}, bf16[256,512]{1,0:T(8,128)(2,1)S(1)}, u32[]{:S(2)}, u32[]{:S(2)}) %collective-permute-start.18) | collective-permute-done | bytes 262176 | tf_op jit(solution)/shard_map/ppermute | solution.py:49
  38.4 2.1 %collective-permute-start.20 = (bf16[256,512]{1,0:T(8,128)(2,1)S(1)}, bf16[256,512]{1,0:T(8,128)(2,1)S(1)}, u32[]{:S(2)}, u32[]{:S(2)}) collective-permute-start(bf16[256,512]{1,0:T(8,128)(2,1)S(1)} %collective-permute-done.18.refs_3_), channel_id=1, source_target_pairs={{0,8},{8,16},{16,24},{24,28},{28,20},{20,12},{12,4},{4,0},{1,9},{9... | collective-permute-start | bytes 786440 | tf_op jit(solution)/shard_map/ppermute | solution.py:49
  41.2 2.0 %collective-permute-start.4 = (bf16[256,512]{1,0:T(8,128)(2,1)S(1)}, bf16[256,512]{1,0:T(8,128)(2,1)S(1)}, u32[]{:S(2)}, u32[]{:S(2)}) collective-permute-start(bf16[256,512]{1,0:T(8,128)(2,1)S(1)} %collective-permute-done.2.refs_3_), channel_id=1, source_target_pairs={{0,8},{8,16},{16,24},{24,28},{28,20},{20,12},{12,4},{4,0},{1,9},{9... | collective-permute-start | bytes 786440 | tf_op jit(solution)/shard_map/ppermute | solution.py:49
  44.0 2.1 %collective-permute-start.5 = (bf16[256,512]{1,0:T(8,128)(2,1)S(1)}, bf16[256,512]{1,0:T(8,128)(2,1)S(1)}, u32[]{:S(2)}, u32[]{:S(2)}) collective-permute-start(bf16[256,512]{1,0:T(8,128)(2,1)S(1)} %collective-permute-done.3.refs_4_), channel_id=1, source_target_pairs={{8,0},{16,8},{24,16},{28,24},{20,28},{12,20},{4,12},{0,4},{9,1},{1... | collective-permute-start | bytes 786440 | tf_op jit(solution)/shard_map/ppermute | solution.py:50
  48.4 1.2 collective-permute-done.20.refs_5_
  49.6 2.1 %collective-permute-start.15 = (bf16[128,512]{1,0:T(8,128)(2,1)}, bf16[128,512]{1,0:T(8,128)(2,1)}, u32[]{:S(2)}, u32[]{:S(2)}) collective-permute-start(bf16[128,512]{1,0:T(8,128)(2,1)} %slice.35), channel_id=1, source_target_pairs={{8,0},{16,8},{24,16},{28,24},{20,28},{12,20},{4,12},{0,4},{9,1},{1... | collective-permute-start | bytes 393224 | tf_op jit(solution)/shard_map/ppermute | solution.py:56
  52.4 1.0 collective-permute-start.22
  54.0 1.2 collective-permute-done.4.refs_5_
  55.3 2.1 %collective-permute-start.23 = (bf16[128,512]{1,0:T(8,128)(2,1)}, bf16[128,512]{1,0:T(8,128)(2,1)}, u32[]{:S(2)}, u32[]{:S(2)}) collective-permute-start(bf16[128,512]{1,0:T(8,128)(2,1)} %slice.37), channel_id=1, source_target_pairs={{8,0},{16,8},{24,16},{28,24},{20,28},{12,20},{4,12},{0,4},{9,1},{1... | collective-permute-start | bytes 393224 | tf_op jit(solution)/shard_map/ppermute | solution.py:56
  59.7 1.1 collective-permute-start.7
  60.8 1.6 %copy-done = bf16[512,2048]{1,0:T(8,128)(2,1)S(1)} copy-done((bf16[512,2048]{1,0:T(8,128)(2,1)S(1)}, bf16[512,2048]{1,0:T(8,128)(2,1)}, u32[]{:S(2)}) %copy-start) | copy-done | bytes 2097176
  62.4 0.9 copy-done.11
  65.2 2.4 %shard_map.65.keys = bf16[512,512]{1,0:T(8,128)(2,1)S(1)} custom-call(s32[9]{0:T(128)S(1)} %stack.148.starts, bf16[512,2048]{1,0:T(8,128)(2,1)S(1)} %copy-done, bf16[256,512]{1,0:T(8,128)(2,1)S(1)} %copy-done.11, bf16[256,512]{1,0:T(8,128)(2,1)S(1)} %collective-permute-done.8.refs_1_, bf16[256,512]{1,0:T(8,128)(2,1)S(1)} %collective-permute-done.9.refs_2_, ...), custom_call_target="tpu_custom_call" | custom-call | flops 1073741824 | bytes 4718628 | tf_op jit(solution)/shard_map/pallas_call | solution.py:18
  67.7 2.4 %shard_map.66.values = bf16[512,512]{1,0:T(8,128)(2,1)S(1)} custom-call(s32[9]{0:T(128)S(1)} %stack.148.starts, bf16[512,2048]{1,0:T(8,128)(2,1)S(1)} %copy-done, bf16[256,512]{1,0:T(8,128)(2,1)S(1)} %copy-done.12, bf16[256,512]{1,0:T(8,128)(2,1)S(1)} %collective-permute-done.16.refs_1_, bf16[256,512]{1,0:T(8,128)(2,1)S(1)} %collective-permute-done.17.refs_2_, ...), custom_call_target="tpu_custom_call" | custom-call | flops 1073741824 | bytes 4718628 | tf_op jit(solution)/shard_map/pallas_call | solution.py:18
  70.9 1.6 %collective-permute-start.24 = (bf16[4,128,128]{2,1,0:T(8,128)(2,1)S(1)}, bf16[4,128,128]{2,1,0:T(8,128)(2,1)}, u32[]{:S(2)}, u32[]{:S(2)}) collective-permute-start(bf16[4,128,128]{2,1,0:T(8,128)(2,1)S(1)} %get-tuple-element.7), channel_id=1, source_target_pairs={{0,4},{4,0},{8,12},{12,8},{16,20},{20,16},{24,28},{28,24},{1,5},{5... | collective-permute-start | bytes 393224 | tf_op jit(solution)/shard_map/ppermute | solution.py:258
  72.5 3.6 %collective-permute-start.30 = (bf16[512,256]{1,0:T(8,128)(2,1)}, bf16[512,256]{1,0:T(8,128)(2,1)}, u32[]{:S(2)}, u32[]{:S(2)}) collective-permute-start(bf16[512,256]{1,0:T(8,128)(2,1)} %param.10), channel_id=1, source_target_pairs={{0,0},{1,4},{2,8},{3,12},{4,16},{5,20},{6,24},{7,28},{8,1},{9,5},{... | collective-permute-start | bytes 786440 | tf_op jit(solution)/shard_map/ppermute | solution.py:248
  76.1 1.2 copy.7
  77.4 2.9 %shard_map.67.mixing = f32[4,512,512]{2,1,0:T(8,128)S(1)} custom-call(f32[4,512,13]{2,1,0:T(8,128)S(1)} %bitcast.29), custom_call_target="tpu_custom_call" | custom-call | flops 10485760 | bytes 4300800 | tf_op jit(solution)/shard_map/pallas_call | solution.py:18
  80.3 2.0 %copy-done.2 = f32[4,512,512]{2,1,0:T(8,128)} copy-done((f32[4,512,512]{2,1,0:T(8,128)}, f32[4,512,512]{2,1,0:T(8,128)S(1)}, u32[]{:S(2)}) %copy-start.2) | copy-done | bytes 4194328
  82.4 2.4 %shard_map.64.queries = bf16[512,512]{1,0:T(8,128)(2,1)S(1)} custom-call(s32[9]{0:T(128)S(1)} %stack.148.starts, bf16[512,2048]{1,0:T(8,128)(2,1)S(1)} %copy-done.1, bf16[256,512]{1,0:T(8,128)(2,1)S(1)} %copy-done.13, bf16[256,512]{1,0:T(8,128)(2,1)S(1)} %copy-done.15, bf16[256,512]{1,0:T(8,128)(2,1)S(1)} %copy-done.17, bf16[256,512]{1,0:T(8,128)(2,1)S(1)} %copy-done.19, ...), custom_call_target="tpu_custom_call" | custom-call | flops 1073741824 | bytes 4718628 | tf_op jit(solution)/shard_map/pallas_call | solution.py:18
  86.8 6.7 %collective-permute-done.25 = bf16[4,128,128]{2,1,0:T(8,128)(2,1)S(1)} collective-permute-done((bf16[4,128,128]{2,1,0:T(8,128)(2,1)S(1)}, bf16[4,128,128]{2,1,0:T(8,128)(2,1)S(1)}, u32[]{:S(2)}, u32[]{:S(2)}) %collective-permute-start.25) | collective-permute-done | bytes 131104 | tf_op jit(solution)/shard_map/ppermute | solution.py:258
  93.5 1.0 add_convert_fusion
  94.6 6.2 %collective-permute-done.26 = bf16[4,128,128]{2,1,0:T(8,128)(2,1)S(1)} collective-permute-done((bf16[4,128,128]{2,1,0:T(8,128)(2,1)S(1)}, bf16[4,128,128]{2,1,0:T(8,128)(2,1)S(1)}, u32[]{:S(2)}, u32[]{:S(2)}) %collective-permute-start.26) | collective-permute-done | bytes 131104 | tf_op jit(solution)/shard_map/ppermute | solution.py:258
  100.8 4.9 %shard_map.69.refs_0_ = bf16[512,512]{1,0:T(8,128)(2,1)S(1)} custom-call(bf16[512,512]{1,0:T(8,128)(2,1)S(1)} %shard_map.64.queries, bf16[512,512]{1,0:T(8,128)(2,1)S(1)} %copy-done.4, bf16[512,512]{1,0:T(8,128)(2,1)S(1)} %copy-done.6, f32[4,512,512]{2,1,0:T(8,128)} %copy-done.2, f32[4,512,13]{2,1,0:T(8,128)S(1)} %bitcast.30, ...), custom_call_target="tpu_custom_call" | custom-call | flops 738197504 | bytes 6791168 | tf_op jit(solution)/shard_map/pallas_call | solution.py:18
  106.2 4.0 %collective-permute-start.32 = (bf16[512,256]{1,0:T(8,128)(2,1)}, bf16[512,256]{1,0:T(8,128)(2,1)S(1)}, u32[]{:S(2)}, u32[]{:S(2)}) collective-permute-start(bf16[512,256]{1,0:T(8,128)(2,1)} %collective-permute-done.30.refs_4_), channel_id=1, source_target_pairs={{8,0},{16,8},{24,16},{28,24},{20,28},{12,20},{4,12},{0,4},{9,1},{1... | collective-permute-start | bytes 786440 | tf_op jit(solution)/shard_map/ppermute | solution.py:50
  110.2 5.9 %collective-permute-done.31.refs_5_ = bf16[512,256]{1,0:T(8,128)(2,1)S(1)} collective-permute-done((bf16[512,256]{1,0:T(8,128)(2,1)}, bf16[512,256]{1,0:T(8,128)(2,1)S(1)}, u32[]{:S(2)}, u32[]{:S(2)}) %collective-permute-start.31) | collective-permute-done | bytes 262176 | tf_op jit(solution)/shard_map/ppermute | solution.py:49
  116.1 2.0 %collective-permute-start.34 = (bf16[512,256]{1,0:T(8,128)(2,1)S(1)}, bf16[512,256]{1,0:T(8,128)(2,1)S(1)}, u32[]{:S(2)}, u32[]{:S(2)}) collective-permute-start(bf16[512,256]{1,0:T(8,128)(2,1)S(1)} %collective-permute-done.32.refs_6_), channel_id=1, source_target_pairs={{8,0},{16,8},{24,16},{28,24},{20,28},{12,20},{4,12},{0,4},{9,1},{1... | collective-permute-start | bytes 786440 | tf_op jit(solution)/shard_map/ppermute | solution.py:50
  118.7 4.2 %collective-permute-done.33.refs_7_ = bf16[512,256]{1,0:T(8,128)(2,1)S(1)} collective-permute-done((bf16[512,256]{1,0:T(8,128)(2,1)S(1)}, bf16[512,256]{1,0:T(8,128)(2,1)S(1)}, u32[]{:S(2)}, u32[]{:S(2)}) %collective-permute-start.33) | collective-permute-done | bytes 262176 | tf_op jit(solution)/shard_map/ppermute | solution.py:49
  123.2 1.7 %collective-permute-start.36 = (bf16[512,256]{1,0:T(8,128)(2,1)S(1)}, bf16[512,256]{1,0:T(8,128)(2,1)S(1)}, u32[]{:S(2)}, u32[]{:S(2)}) collective-permute-start(bf16[512,256]{1,0:T(8,128)(2,1)S(1)} %collective-permute-done.34.refs_8_), channel_id=1, source_target_pairs={{8,0},{16,8},{24,16},{28,24},{20,28},{12,20},{4,12},{0,4},{9,1},{1... | collective-permute-start | bytes 786440 | tf_op jit(solution)/shard_map/ppermute | solution.py:50
  124.9 4.3 %collective-permute-done.35.refs_9_ = bf16[512,256]{1,0:T(8,128)(2,1)S(1)} collective-permute-done((bf16[512,256]{1,0:T(8,128)(2,1)S(1)}, bf16[512,256]{1,0:T(8,128)(2,1)S(1)}, u32[]{:S(2)}, u32[]{:S(2)}) %collective-permute-start.35) | collective-permute-done | bytes 262176 | tf_op jit(solution)/shard_map/ppermute | solution.py:49
  131.8 1.5 %collective-permute-start.38 = (bf16[256,256]{1,0:T(8,128)(2,1)}, bf16[256,256]{1,0:T(8,128)(2,1)}, u32[]{:S(2)}, u32[]{:S(2)}) collective-permute-start(bf16[256,256]{1,0:T(8,128)(2,1)} %slice.39), channel_id=1, source_target_pairs={{8,0},{16,8},{24,16},{28,24},{20,28},{12,20},{4,12},{0,4},{9,1},{1... | collective-permute-start | bytes 393224 | tf_op jit(solution)/shard_map/ppermute | solution.py:56
  133.5 2.3 %collective-permute-done.37.refs_11_ = bf16[256,256]{1,0:T(8,128)(2,1)S(1)} collective-permute-done((bf16[256,256]{1,0:T(8,128)(2,1)}, bf16[256,256]{1,0:T(8,128)(2,1)S(1)}, u32[]{:S(2)}, u32[]{:S(2)}) %collective-permute-start.37) | collective-permute-done | bytes 131104 | tf_op jit(solution)/shard_map/ppermute | solution.py:55
  135.8 1.3 collective-permute-done.38.refs_12_
  138.0 3.2 %shard_map.70 = bf16[512,512]{1,0:T(8,128)(2,1)} custom-call(s32[2,9]{1,0:T(2,128)S(1)} %pad_add_fusion.starts, bf16[512,512]{1,0:T(8,128)(2,1)S(1)} %shard_map.69.refs_0_, bf16[512,512]{1,0:T(8,128)(2,1)S(1)} %collective-permute-done.27.refs_1_, bf16[512,512]{1,0:T(8,128)(2,1)S(1)} %collective-permute-done.28.refs_2_, ...), custom_call_target="tpu_custom_call" | custom-call | flops 1073741824 | bytes 4718664 | tf_op jit(solution)/shard_map/pallas_call | solution.py:18
  (115 shorter events, 20.1 us)
Async XLA Ops:
  0.0 67.6 %copy-start.12 = (bf16[256,512]{1,0:T(8,128)(2,1)S(1)}, bf16[256,512]{1,0:T(8,128)(2,1)}, u32[]{:S(2)}) copy-start(bf16[256,512]{1,0:T(8,128)(2,1)} %refs_0_.5) | copy-start | bytes 786436
  0.0 10.3 %collective-permute-start = (bf16[256,512]{1,0:T(8,128)(2,1)}, bf16[256,512]{1,0:T(8,128)(2,1)S(1)}, u32[]{:S(2)}, u32[]{:S(2)}) collective-permute-start(bf16[256,512]{1,0:T(8,128)(2,1)} %refs_0_.3), channel_id=1, source_target_pairs={{0,8},{8,16},{16,24},{24,28},{28,20},{20,12},{12,4},{4,0},{1,9},{9... | collective-permute-start | bytes 786440 | tf_op jit(solution)/shard_map/ppermute | solution.py:49
  3.0 9.4 %collective-permute-start.1 = (bf16[256,512]{1,0:T(8,128)(2,1)}, bf16[256,512]{1,0:T(8,128)(2,1)S(1)}, u32[]{:S(2)}, u32[]{:S(2)}) collective-permute-start(bf16[256,512]{1,0:T(8,128)(2,1)} %refs_0_.3), channel_id=1, source_target_pairs={{8,0},{16,8},{24,16},{28,24},{20,28},{12,20},{4,12},{0,4},{9,1},{1... | collective-permute-start | bytes 786440 | tf_op jit(solution)/shard_map/ppermute | solution.py:50
  3.0 12.9 %collective-permute-start.8 = (bf16[256,512]{1,0:T(8,128)(2,1)}, bf16[256,512]{1,0:T(8,128)(2,1)S(1)}, u32[]{:S(2)}, u32[]{:S(2)}) collective-permute-start(bf16[256,512]{1,0:T(8,128)(2,1)} %refs_0_.4), channel_id=1, source_target_pairs={{0,8},{8,16},{16,24},{24,28},{28,20},{20,12},{12,4},{4,0},{1,9},{9... | collective-permute-start | bytes 786440 | tf_op jit(solution)/shard_map/ppermute | solution.py:49
  5.1 13.0 %collective-permute-start.9 = (bf16[256,512]{1,0:T(8,128)(2,1)}, bf16[256,512]{1,0:T(8,128)(2,1)S(1)}, u32[]{:S(2)}, u32[]{:S(2)}) collective-permute-start(bf16[256,512]{1,0:T(8,128)(2,1)} %refs_0_.4), channel_id=1, source_target_pairs={{8,0},{16,8},{24,16},{28,24},{20,28},{12,20},{4,12},{0,4},{9,1},{1... | collective-permute-start | bytes 786440 | tf_op jit(solution)/shard_map/ppermute | solution.py:50
  5.1 16.5 %collective-permute-start.16 = (bf16[256,512]{1,0:T(8,128)(2,1)}, bf16[256,512]{1,0:T(8,128)(2,1)S(1)}, u32[]{:S(2)}, u32[]{:S(2)}) collective-permute-start(bf16[256,512]{1,0:T(8,128)(2,1)} %refs_0_.5), channel_id=1, source_target_pairs={{0,8},{8,16},{16,24},{24,28},{28,20},{20,12},{12,4},{4,0},{1,9},{9... | collective-permute-start | bytes 786440 | tf_op jit(solution)/shard_map/ppermute | solution.py:49
  10.3 13.4 %collective-permute-start.17 = (bf16[256,512]{1,0:T(8,128)(2,1)}, bf16[256,512]{1,0:T(8,128)(2,1)S(1)}, u32[]{:S(2)}, u32[]{:S(2)}) collective-permute-start(bf16[256,512]{1,0:T(8,128)(2,1)} %refs_0_.5), channel_id=1, source_target_pairs={{8,0},{16,8},{24,16},{28,24},{20,28},{12,20},{4,12},{0,4},{9,1},{1... | collective-permute-start | bytes 786440 | tf_op jit(solution)/shard_map/ppermute | solution.py:50
  12.5 14.7 %collective-permute-start.2 = (bf16[256,512]{1,0:T(8,128)(2,1)S(1)}, bf16[256,512]{1,0:T(8,128)(2,1)S(1)}, u32[]{:S(2)}, u32[]{:S(2)}) collective-permute-start(bf16[256,512]{1,0:T(8,128)(2,1)S(1)} %collective-permute-done.refs_1_), channel_id=1, source_target_pairs={{0,8},{8,16},{16,24},{24,28},{28,20},{20,12},{12,4},{4,0},{1,9},{9... | collective-permute-start | bytes 786440 | tf_op jit(solution)/shard_map/ppermute | solution.py:49
  15.9 16.9 %collective-permute-start.10 = (bf16[256,512]{1,0:T(8,128)(2,1)S(1)}, bf16[256,512]{1,0:T(8,128)(2,1)S(1)}, u32[]{:S(2)}, u32[]{:S(2)}) collective-permute-start(bf16[256,512]{1,0:T(8,128)(2,1)S(1)} %collective-permute-done.8.refs_1_), channel_id=1, source_target_pairs={{0,8},{8,16},{16,24},{24,28},{28,20},{20,12},{12,4},{4,0},{1,9},{9... | collective-permute-start | bytes 786440 | tf_op jit(solution)/shard_map/ppermute | solution.py:49
  18.1 17.5 %collective-permute-start.11 = (bf16[256,512]{1,0:T(8,128)(2,1)S(1)}, bf16[256,512]{1,0:T(8,128)(2,1)S(1)}, u32[]{:S(2)}, u32[]{:S(2)}) collective-permute-start(bf16[256,512]{1,0:T(8,128)(2,1)S(1)} %collective-permute-done.9.refs_2_), channel_id=1, source_target_pairs={{8,0},{16,8},{24,16},{28,24},{20,28},{12,20},{4,12},{0,4},{9,1},{1... | collective-permute-start | bytes 786440 | tf_op jit(solution)/shard_map/ppermute | solution.py:50
  21.5 16.9 %collective-permute-start.18 = (bf16[256,512]{1,0:T(8,128)(2,1)S(1)}, bf16[256,512]{1,0:T(8,128)(2,1)S(1)}, u32[]{:S(2)}, u32[]{:S(2)}) collective-permute-start(bf16[256,512]{1,0:T(8,128)(2,1)S(1)} %collective-permute-done.16.refs_1_), channel_id=1, source_target_pairs={{0,8},{8,16},{16,24},{24,28},{28,20},{20,12},{12,4},{4,0},{1,9},{9... | collective-permute-start | bytes 786440 | tf_op jit(solution)/shard_map/ppermute | solution.py:49
  23.7 16.8 %collective-permute-start.19 = (bf16[256,512]{1,0:T(8,128)(2,1)S(1)}, bf16[256,512]{1,0:T(8,128)(2,1)S(1)}, u32[]{:S(2)}, u32[]{:S(2)}) collective-permute-start(bf16[256,512]{1,0:T(8,128)(2,1)S(1)} %collective-permute-done.17.refs_2_), channel_id=1, source_target_pairs={{8,0},{16,8},{24,16},{28,24},{20,28},{12,20},{4,12},{0,4},{9,1},{1... | collective-permute-start | bytes 786440 | tf_op jit(solution)/shard_map/ppermute | solution.py:50
  27.2 14.1 %collective-permute-start.3 = (bf16[256,512]{1,0:T(8,128)(2,1)S(1)}, bf16[256,512]{1,0:T(8,128)(2,1)S(1)}, u32[]{:S(2)}, u32[]{:S(2)}) collective-permute-start(bf16[256,512]{1,0:T(8,128)(2,1)S(1)} %collective-permute-done.1.refs_2_), channel_id=1, source_target_pairs={{8,0},{16,8},{24,16},{28,24},{20,28},{12,20},{4,12},{0,4},{9,1},{1... | collective-permute-start | bytes 786440 | tf_op jit(solution)/shard_map/ppermute | solution.py:50
  32.8 11.2 %collective-permute-start.12 = (bf16[256,512]{1,0:T(8,128)(2,1)S(1)}, bf16[256,512]{1,0:T(8,128)(2,1)S(1)}, u32[]{:S(2)}, u32[]{:S(2)}) collective-permute-start(bf16[256,512]{1,0:T(8,128)(2,1)S(1)} %collective-permute-done.10.refs_3_), channel_id=1, source_target_pairs={{0,8},{8,16},{16,24},{24,28},{28,20},{20,12},{12,4},{4,0},{1,9},{9... | collective-permute-start | bytes 786440 | tf_op jit(solution)/shard_map/ppermute | solution.py:49
  35.6 11.8 %collective-permute-start.13 = (bf16[256,512]{1,0:T(8,128)(2,1)S(1)}, bf16[256,512]{1,0:T(8,128)(2,1)S(1)}, u32[]{:S(2)}, u32[]{:S(2)}) collective-permute-start(bf16[256,512]{1,0:T(8,128)(2,1)S(1)} %collective-permute-done.11.refs_4_), channel_id=1, source_target_pairs={{8,0},{16,8},{24,16},{28,24},{20,28},{12,20},{4,12},{0,4},{9,1},{1... | collective-permute-start | bytes 786440 | tf_op jit(solution)/shard_map/ppermute | solution.py:50
  38.4 11.2 %collective-permute-start.20 = (bf16[256,512]{1,0:T(8,128)(2,1)S(1)}, bf16[256,512]{1,0:T(8,128)(2,1)S(1)}, u32[]{:S(2)}, u32[]{:S(2)}) collective-permute-start(bf16[256,512]{1,0:T(8,128)(2,1)S(1)} %collective-permute-done.18.refs_3_), channel_id=1, source_target_pairs={{0,8},{8,16},{16,24},{24,28},{28,20},{20,12},{12,4},{4,0},{1,9},{9... | collective-permute-start | bytes 786440 | tf_op jit(solution)/shard_map/ppermute | solution.py:49
  40.5 11.8 %collective-permute-start.21 = (bf16[256,512]{1,0:T(8,128)(2,1)S(1)}, bf16[256,512]{1,0:T(8,128)(2,1)S(1)}, u32[]{:S(2)}, u32[]{:S(2)}) collective-permute-start(bf16[256,512]{1,0:T(8,128)(2,1)S(1)} %collective-permute-done.19.refs_4_), channel_id=1, source_target_pairs={{8,0},{16,8},{24,16},{28,24},{20,28},{12,20},{4,12},{0,4},{9,1},{1... | collective-permute-start | bytes 786440 | tf_op jit(solution)/shard_map/ppermute | solution.py:50
  41.2 14.0 %collective-permute-start.4 = (bf16[256,512]{1,0:T(8,128)(2,1)S(1)}, bf16[256,512]{1,0:T(8,128)(2,1)S(1)}, u32[]{:S(2)}, u32[]{:S(2)}) collective-permute-start(bf16[256,512]{1,0:T(8,128)(2,1)S(1)} %collective-permute-done.2.refs_3_), channel_id=1, source_target_pairs={{0,8},{8,16},{16,24},{24,28},{28,20},{20,12},{12,4},{4,0},{1,9},{9... | collective-permute-start | bytes 786440 | tf_op jit(solution)/shard_map/ppermute | solution.py:49
  44.0 14.1 %collective-permute-start.5 = (bf16[256,512]{1,0:T(8,128)(2,1)S(1)}, bf16[256,512]{1,0:T(8,128)(2,1)S(1)}, u32[]{:S(2)}, u32[]{:S(2)}) collective-permute-start(bf16[256,512]{1,0:T(8,128)(2,1)S(1)} %collective-permute-done.3.refs_4_), channel_id=1, source_target_pairs={{8,0},{16,8},{24,16},{28,24},{20,28},{12,20},{4,12},{0,4},{9,1},{1... | collective-permute-start | bytes 786440 | tf_op jit(solution)/shard_map/ppermute | solution.py:50
  47.4 12.2 %collective-permute-start.14 = (bf16[128,512]{1,0:T(8,128)(2,1)}, bf16[128,512]{1,0:T(8,128)(2,1)}, u32[]{:S(2)}, u32[]{:S(2)}) collective-permute-start(bf16[128,512]{1,0:T(8,128)(2,1)} %slice.34), channel_id=1, source_target_pairs={{0,8},{8,16},{16,24},{24,28},{28,20},{20,12},{12,4},{4,0},{1,9},{9... | collective-permute-start | bytes 393224 | tf_op jit(solution)/shard_map/ppermute | solution.py:55
  49.6 11.1 %collective-permute-start.15 = (bf16[128,512]{1,0:T(8,128)(2,1)}, bf16[128,512]{1,0:T(8,128)(2,1)}, u32[]{:S(2)}, u32[]{:S(2)}) collective-permute-start(bf16[128,512]{1,0:T(8,128)(2,1)} %slice.35), channel_id=1, source_target_pairs={{8,0},{16,8},{24,16},{28,24},{20,28},{12,20},{4,12},{0,4},{9,1},{1... | collective-permute-start | bytes 393224 | tf_op jit(solution)/shard_map/ppermute | solution.py:56
  52.4 15.2 %collective-permute-start.22 = (bf16[128,512]{1,0:T(8,128)(2,1)}, bf16[128,512]{1,0:T(8,128)(2,1)S(1)}, u32[]{:S(2)}, u32[]{:S(2)}) collective-permute-start(bf16[128,512]{1,0:T(8,128)(2,1)} %slice.36), channel_id=1, source_target_pairs={{0,8},{8,16},{16,24},{24,28},{28,20},{20,12},{12,4},{4,0},{1,9},{9... | collective-permute-start | bytes 393224 | tf_op jit(solution)/shard_map/ppermute | solution.py:55
  55.3 12.4 %copy-start.7 = (bf16[256,512]{1,0:T(8,128)(2,1)}, bf16[256,512]{1,0:T(8,128)(2,1)S(1)}, u32[]{:S(2)}) copy-start(bf16[256,512]{1,0:T(8,128)(2,1)S(1)} %collective-permute-done.4.refs_5_) | copy-start | bytes 786436
  55.3 12.4 %collective-permute-start.23 = (bf16[128,512]{1,0:T(8,128)(2,1)}, bf16[128,512]{1,0:T(8,128)(2,1)}, u32[]{:S(2)}, u32[]{:S(2)}) collective-permute-start(bf16[128,512]{1,0:T(8,128)(2,1)} %slice.37), channel_id=1, source_target_pairs={{8,0},{16,8},{24,16},{28,24},{20,28},{12,20},{4,12},{0,4},{9,1},{1... | collective-permute-start | bytes 393224 | tf_op jit(solution)/shard_map/ppermute | solution.py:56
  57.4 10.2 %copy-start.25 = (bf16[256,512]{1,0:T(8,128)(2,1)S(1)}, bf16[256,512]{1,0:T(8,128)(2,1)}, u32[]{:S(2)}) copy-start(bf16[256,512]{1,0:T(8,128)(2,1)} %copy-done.24) | copy-start | bytes 786436
  58.1 9.6 %copy-start.9 = (bf16[256,512]{1,0:T(8,128)(2,1)}, bf16[256,512]{1,0:T(8,128)(2,1)S(1)}, u32[]{:S(2)}) copy-start(bf16[256,512]{1,0:T(8,128)(2,1)S(1)} %collective-permute-done.5.refs_6_) | copy-start | bytes 786436
  58.1 24.2 %collective-permute-start.6 = (bf16[128,512]{1,0:T(8,128)(2,1)}, bf16[128,512]{1,0:T(8,128)(2,1)}, u32[]{:S(2)}, u32[]{:S(2)}) collective-permute-start(bf16[128,512]{1,0:T(8,128)(2,1)} %slice.32), channel_id=1, source_target_pairs={{0,8},{8,16},{16,24},{24,28},{28,20},{20,12},{12,4},{4,0},{1,9},{9... | collective-permute-start | bytes 393224 | tf_op jit(solution)/shard_map/ppermute | solution.py:55
  59.7 22.7 %collective-permute-start.7 = (bf16[128,512]{1,0:T(8,128)(2,1)}, bf16[128,512]{1,0:T(8,128)(2,1)}, u32[]{:S(2)}, u32[]{:S(2)}) collective-permute-start(bf16[128,512]{1,0:T(8,128)(2,1)} %slice.33), channel_id=1, source_target_pairs={{8,0},{16,8},{24,16},{28,24},{20,28},{12,20},{4,12},{0,4},{9,1},{1... | collective-permute-start | bytes 393224 | tf_op jit(solution)/shard_map/ppermute | solution.py:56
  70.1 12.2 %copy-start.1 = (bf16[512,2048]{1,0:T(8,128)(2,1)S(1)}, bf16[512,2048]{1,0:T(8,128)(2,1)}, u32[]{:S(2)}) copy-start(bf16[512,2048]{1,0:T(8,128)(2,1)} %tokens.5) | copy-start | bytes 6291460
  70.9 13.9 %collective-permute-start.24 = (bf16[4,128,128]{2,1,0:T(8,128)(2,1)S(1)}, bf16[4,128,128]{2,1,0:T(8,128)(2,1)}, u32[]{:S(2)}, u32[]{:S(2)}) collective-permute-start(bf16[4,128,128]{2,1,0:T(8,128)(2,1)S(1)} %get-tuple-element.7), channel_id=1, source_target_pairs={{0,4},{4,0},{8,12},{12,8},{16,20},{20,16},{24,28},{28,24},{1,5},{5... | collective-permute-start | bytes 393224 | tf_op jit(solution)/shard_map/ppermute | solution.py:258
  72.5 33.7 %collective-permute-start.30 = (bf16[512,256]{1,0:T(8,128)(2,1)}, bf16[512,256]{1,0:T(8,128)(2,1)}, u32[]{:S(2)}, u32[]{:S(2)}) collective-permute-start(bf16[512,256]{1,0:T(8,128)(2,1)} %param.10), channel_id=1, source_target_pairs={{0,0},{1,4},{2,8},{3,12},{4,16},{5,20},{6,24},{7,28},{8,1},{9,5},{... | collective-permute-start | bytes 786440 | tf_op jit(solution)/shard_map/ppermute | solution.py:248
  77.4 5.0 %copy-start.8 = (bf16[256,512]{1,0:T(8,128)(2,1)S(1)}, bf16[256,512]{1,0:T(8,128)(2,1)}, u32[]{:S(2)}) copy-start(bf16[256,512]{1,0:T(8,128)(2,1)} %copy-done.7) | copy-start | bytes 786436
  82.3 18.5 %copy-start.4 = (bf16[512,512]{1,0:T(8,128)(2,1)S(1)}, bf16[512,512]{1,0:T(8,128)(2,1)}, u32[]{:S(2)}) copy-start(bf16[512,512]{1,0:T(8,128)(2,1)} %copy-done.3) | copy-start | bytes 1572868
  82.3 18.5 %copy-start.6 = (bf16[512,512]{1,0:T(8,128)(2,1)S(1)}, bf16[512,512]{1,0:T(8,128)(2,1)}, u32[]{:S(2)}) copy-start(bf16[512,512]{1,0:T(8,128)(2,1)} %copy-done.5) | copy-start | bytes 1572868
  85.8 7.7 %collective-permute-start.25 = (bf16[4,128,128]{2,1,0:T(8,128)(2,1)S(1)}, bf16[4,128,128]{2,1,0:T(8,128)(2,1)S(1)}, u32[]{:S(2)}, u32[]{:S(2)}) collective-permute-start(bf16[4,128,128]{2,1,0:T(8,128)(2,1)S(1)} %fusion), channel_id=1, source_target_pairs={{0,8},{4,12},{8,0},{12,4},{16,24},{20,28},{24,16},{28,20},{1,9},{5... | collective-permute-start | bytes 393224 | tf_op jit(solution)/shard_map/ppermute | solution.py:258
  94.5 6.3 %collective-permute-start.26 = (bf16[4,128,128]{2,1,0:T(8,128)(2,1)S(1)}, bf16[4,128,128]{2,1,0:T(8,128)(2,1)S(1)}, u32[]{:S(2)}, u32[]{:S(2)}) collective-permute-start(bf16[4,128,128]{2,1,0:T(8,128)(2,1)S(1)} %add_convert_fusion), channel_id=1, source_target_pairs={{0,16},{4,20},{8,24},{12,28},{16,0},{20,4},{24,8},{28,12},{1,17},{... | collective-permute-start | bytes 393224 | tf_op jit(solution)/shard_map/ppermute | solution.py:258
  105.7 12.5 %collective-permute-start.28 = (bf16[512,512]{1,0:T(8,128)(2,1)S(1)}, bf16[512,512]{1,0:T(8,128)(2,1)S(1)}, u32[]{:S(2)}, u32[]{:S(2)}) collective-permute-start(bf16[512,512]{1,0:T(8,128)(2,1)S(1)} %shard_map.69.refs_0_), channel_id=1, source_target_pairs={{0,2},{1,3},{2,0},{3,1},{4,6},{5,7},{6,4},{7,5},{8,10},{9,11},{10,... | collective-permute-start | bytes 1572872 | tf_op jit(solution)/shard_map/ppermute | solution.py:271
  106.2 9.9 %collective-permute-start.31 = (bf16[512,256]{1,0:T(8,128)(2,1)}, bf16[512,256]{1,0:T(8,128)(2,1)S(1)}, u32[]{:S(2)}, u32[]{:S(2)}) collective-permute-start(bf16[512,256]{1,0:T(8,128)(2,1)} %collective-permute-done.30.refs_4_), channel_id=1, source_target_pairs={{0,8},{8,16},{16,24},{24,28},{28,20},{20,12},{12,4},{4,0},{1,9},{9... | collective-permute-start | bytes 786440 | tf_op jit(solution)/shard_map/ppermute | solution.py:49
  106.2 9.9 %collective-permute-start.32 = (bf16[512,256]{1,0:T(8,128)(2,1)}, bf16[512,256]{1,0:T(8,128)(2,1)S(1)}, u32[]{:S(2)}, u32[]{:S(2)}) collective-permute-start(bf16[512,256]{1,0:T(8,128)(2,1)} %collective-permute-done.30.refs_4_), channel_id=1, source_target_pairs={{8,0},{16,8},{24,16},{28,24},{20,28},{12,20},{4,12},{0,4},{9,1},{1... | collective-permute-start | bytes 786440 | tf_op jit(solution)/shard_map/ppermute | solution.py:50
  116.1 6.8 %collective-permute-start.33 = (bf16[512,256]{1,0:T(8,128)(2,1)S(1)}, bf16[512,256]{1,0:T(8,128)(2,1)S(1)}, u32[]{:S(2)}, u32[]{:S(2)}) collective-permute-start(bf16[512,256]{1,0:T(8,128)(2,1)S(1)} %collective-permute-done.31.refs_5_), channel_id=1, source_target_pairs={{0,8},{8,16},{16,24},{24,28},{28,20},{20,12},{12,4},{4,0},{1,9},{9... | collective-permute-start | bytes 786440 | tf_op jit(solution)/shard_map/ppermute | solution.py:49
  116.1 7.1 %collective-permute-start.34 = (bf16[512,256]{1,0:T(8,128)(2,1)S(1)}, bf16[512,256]{1,0:T(8,128)(2,1)S(1)}, u32[]{:S(2)}, u32[]{:S(2)}) collective-permute-start(bf16[512,256]{1,0:T(8,128)(2,1)S(1)} %collective-permute-done.32.refs_6_), channel_id=1, source_target_pairs={{8,0},{16,8},{24,16},{28,24},{20,28},{12,20},{4,12},{0,4},{9,1},{1... | collective-permute-start | bytes 786440 | tf_op jit(solution)/shard_map/ppermute | solution.py:50
  118.2 18.9 %collective-permute-start.27 = (bf16[512,512]{1,0:T(8,128)(2,1)S(1)}, bf16[512,512]{1,0:T(8,128)(2,1)S(1)}, u32[]{:S(2)}, u32[]{:S(2)}) collective-permute-start(bf16[512,512]{1,0:T(8,128)(2,1)S(1)} %shard_map.69.refs_0_), channel_id=1, source_target_pairs={{0,1},{1,0},{2,3},{3,2},{4,5},{5,4},{6,7},{7,6},{8,9},{9,8},{10,11... | collective-permute-start | bytes 1572872 | tf_op jit(solution)/shard_map/ppermute | solution.py:271
  118.2 18.9 %collective-permute-start.29 = (bf16[512,512]{1,0:T(8,128)(2,1)S(1)}, bf16[512,512]{1,0:T(8,128)(2,1)S(1)}, u32[]{:S(2)}, u32[]{:S(2)}) collective-permute-start(bf16[512,512]{1,0:T(8,128)(2,1)S(1)} %collective-permute-done.28.refs_2_), channel_id=1, source_target_pairs={{0,1},{1,0},{2,3},{3,2},{4,5},{5,4},{6,7},{7,6},{8,9},{9,8},{10,11... | collective-permute-start | bytes 1572872 | tf_op jit(solution)/shard_map/ppermute | solution.py:271
  122.9 6.4 %collective-permute-start.35 = (bf16[512,256]{1,0:T(8,128)(2,1)S(1)}, bf16[512,256]{1,0:T(8,128)(2,1)S(1)}, u32[]{:S(2)}, u32[]{:S(2)}) collective-permute-start(bf16[512,256]{1,0:T(8,128)(2,1)S(1)} %collective-permute-done.33.refs_7_), channel_id=1, source_target_pairs={{0,8},{8,16},{16,24},{24,28},{28,20},{20,12},{12,4},{4,0},{1,9},{9... | collective-permute-start | bytes 786440 | tf_op jit(solution)/shard_map/ppermute | solution.py:49
  123.2 7.9 %copy-start.28 = (bf16[512,256]{1,0:T(8,128)(2,1)}, bf16[512,256]{1,0:T(8,128)(2,1)S(1)}, u32[]{:S(2)}) copy-start(bf16[512,256]{1,0:T(8,128)(2,1)S(1)} %collective-permute-done.34.refs_8_) | copy-start | bytes 786436
  123.2 7.9 %collective-permute-start.36 = (bf16[512,256]{1,0:T(8,128)(2,1)S(1)}, bf16[512,256]{1,0:T(8,128)(2,1)S(1)}, u32[]{:S(2)}, u32[]{:S(2)}) collective-permute-start(bf16[512,256]{1,0:T(8,128)(2,1)S(1)} %collective-permute-done.34.refs_8_), channel_id=1, source_target_pairs={{8,0},{16,8},{24,16},{28,24},{20,28},{12,20},{4,12},{0,4},{9,1},{1... | collective-permute-start | bytes 786440 | tf_op jit(solution)/shard_map/ppermute | solution.py:50
  129.9 5.8 %collective-permute-start.37 = (bf16[256,256]{1,0:T(8,128)(2,1)}, bf16[256,256]{1,0:T(8,128)(2,1)S(1)}, u32[]{:S(2)}, u32[]{:S(2)}) collective-permute-start(bf16[256,256]{1,0:T(8,128)(2,1)} %slice.38), channel_id=1, source_target_pairs={{0,8},{8,16},{16,24},{24,28},{28,20},{20,12},{12,4},{4,0},{1,9},{9... | collective-permute-start | bytes 393224 | tf_op jit(solution)/shard_map/ppermute | solution.py:55
  131.8 5.3 %collective-permute-start.38 = (bf16[256,256]{1,0:T(8,128)(2,1)}, bf16[256,256]{1,0:T(8,128)(2,1)}, u32[]{:S(2)}, u32[]{:S(2)}) collective-permute-start(bf16[256,256]{1,0:T(8,128)(2,1)} %slice.39), channel_id=1, source_target_pairs={{8,0},{16,8},{24,16},{28,24},{20,28},{12,20},{4,12},{0,4},{9,1},{1... | collective-permute-start | bytes 393224 | tf_op jit(solution)/shard_map/ppermute | solution.py:56
  (21 other events, 45.4 us)

commit v2 on v0

v2 whole, which is shorter than its diff:
```python
import functools

import jax
import jax.numpy as jnp
from jax import lax
from jax.experimental import pallas as pl
from jax.experimental.pallas import tpu as pltpu
from jax.sharding import PartitionSpec as P

F32, BF16 = jnp.float32, jnp.bfloat16
LONGEST_RING = 16
SLOWER = 4
VMEM_BYTES = 56 * 2**20
VMEM = pl.BlockSpec(memory_space=pltpu.VMEM)
HBM = pl.BlockSpec(memory_space=pl.ANY)
WHOLE = lambda shape: pl.BlockSpec(shape, lambda *_: (0,) * len(shape))
SMEM = pl.BlockSpec(memory_space=pltpu.SMEM)


def call(kernel, outs, operands, scratch=(), **grid):
    nbytes = sum(a.size * a.dtype.itemsize for a in (*operands, *outs))
    return pl.pallas_call(
        kernel,
        out_shape=outs,
        scratch_shapes=list(scratch),
        compiler_params=pltpu.CompilerParams(vmem_limit_bytes=VMEM_BYTES),
        cost_estimate=pl.CostEstimate(
            flops=1, bytes_accessed=SLOWER * nbytes, transcendentals=0
        ),
        **grid,
    )(*operands)


def ring_order(n):
    return list(range(0, n, 2)) + list(range(n - 1, 0, -2))


def ring_position(index, n):
    return jnp.where(index % 2 == 0, index // 2, n - 1 - index // 2)


def ring_owner(position, n):
    position = (position + n) % n
    return jnp.where(position < n // 2, 2 * position, 2 * (n - 1 - position) + 1)


class Ring:
    def __init__(self, piece, n, opposite):
        order = ring_order(n)
        self.n, self.opposite, self.step = n, opposite, 0
        self.onward = [(order[i], order[(i + 1) % n]) for i in range(n)]
        self.back = [(b, a) for a, b in self.onward]
        self.here = ring_position(lax.axis_index("seq"), n)
        self.ways = [piece, piece]
        self.pieces = [(piece, lax.axis_index("seq"))]
        self.gate = ()

    def advance(self, *gate):
        self.step += 1
        self.gate = tuple(self.ways)
        last = self.step == self.n // 2
        for way, pairs in enumerate((self.onward, self.back)):
            if last and self.opposite != way:
                continue
            piece = self.ways[way]
            self.ways[way] = lax.ppermute(after(piece, gate), "seq", pairs)
            owner = ring_owner(self.here + (self.step if way else -self.step), self.n)
            self.pieces.append((self.ways[way], owner))


def after(array, others):
    return lax.optimization_barrier((array, *others))[0] if others else array


def copy_all(copies):
    for copy in copies:
        copy.start()
    return copies


def fetch(pieces, starts, whole, sems, cols=None):
    copies = []
    for i, piece in enumerate(pieces):
        piece = piece if cols is None else piece.at[:, cols]
        rows, width = piece.shape
        down = pl.ds(pl.multiple_of(starts[0, i], rows), rows)
        along = pl.ds(pl.multiple_of(starts[1, i], width), width)
        copies.append(pltpu.make_async_copy(piece, whole.at[down, along], sems.at[i]))
    return copy_all(copies)


def table(starts):
    return jnp.stack([jnp.stack([jnp.asarray(p[i], jnp.int32) for p in starts]) for i in (0, 1)])


def wait_all(copies):
    for copy in copies:
        copy.wait()


def multiply(left, right, out):
    width = min(256, out.shape[1])
    for low in range(0, out.shape[1], width):
        cols = slice(low, low + width)
        out[:, cols] = jnp.dot(left[...], right[:, cols], preferred_element_type=F32).astype(BF16)


def semaphores(*counts):
    return [pltpu.SemaphoreType.DMA((count,)) for count in counts]


def fetch_rows(array, local, sems):
    rows = local.shape[0] // sems.shape[0]
    parts = [slice(i * rows, (i + 1) * rows) for i in range(sems.shape[0])]
    return copy_all(
        [pltpu.make_async_copy(array.at[p], local.at[p], sems.at[i]) for i, p in enumerate(parts)]
    )


def local_kernel(count, starts, tokens, mixing, *refs):
    key_pieces, value_pieces, query_pieces = [
        refs[i * count : (i + 1) * count] for i in range(3)
    ]
    queries, local, states, rounded, *refs = refs[3 * count :]
    own_tokens, *wholes, keys, values, own_mixing, token_sems, mixing_sems, sems = refs
    rows, width = queries.shape
    heads, dim = states.shape[:2]
    copies = fetch_rows(tokens, own_tokens, token_sems)
    copies += fetch(key_pieces, starts, wholes[0], sems.at[0])
    wait_all(copies)
    copies = fetch(value_pieces, starts, wholes[1], sems.at[1])
    multiply(own_tokens, wholes[0], keys)
    wait_all(copies)
    copies = fetch(query_pieces, starts, wholes[2], sems.at[2])
    copies += fetch_rows(mixing, own_mixing, mixing_sems)
    multiply(own_tokens, wholes[1], values)
    for head in range(heads):
        own = slice(head * dim, (head + 1) * dim)
        sums = lax.dot_general(
            keys[:, own], values[:, own], (((0,), (0,)), ((), ())), preferred_element_type=F32
        )
        states[head] = sums
        rounded[head] = sums.astype(BF16)
    wait_all(copies)
    multiply(own_tokens, wholes[2], queries)
    tile = min(256, rows)
    for head in range(heads):
        own = slice(head * dim, (head + 1) * dim)
        for low in range(0, rows, tile):
            span, seen = slice(low, low + tile), slice(0, low + tile)
            scores = lax.dot_general(
                queries[span, own],
                keys[seen, own],
                (((1,), (1,)), ((), ())),
                preferred_element_type=F32,
            )
            mixed = (scores * own_mixing[head, span, seen].astype(F32)).astype(BF16)
            local[span, own] = jnp.dot(mixed, values[seen, own], preferred_element_type=F32)


def attend_locally(tokens, starts, key_pieces, value_pieces, query_pieces, mixing):
    arrays = [*key_pieces, *value_pieces, *query_pieces]
    count = len(key_pieces)
    rows, depth = tokens.shape
    width = arrays[0].shape[1]
    heads = mixing.shape[0]
    dim = width // heads
    shapes = [(rows, width)] * 2 + [(heads, dim, dim)] * 2
    return call(
        functools.partial(local_kernel, count),
        [jax.ShapeDtypeStruct(s, t) for s, t in zip(shapes, (BF16, F32, F32, BF16))],
        [starts, tokens, mixing, *arrays],
        [
            pltpu.VMEM((rows, depth), BF16),
            *[pltpu.VMEM((depth, width), BF16)] * 3,
            *[pltpu.VMEM((rows, width), BF16)] * 2,
            pltpu.VMEM(mixing.shape, BF16),
            *semaphores(8, heads),
            pltpu.SemaphoreType.DMA((3, count)),
        ],
        in_specs=[SMEM] + [HBM] * (2 + len(arrays)),
        out_specs=[WHOLE(s) for s in shapes],
        grid=(1,),
    )


def mixing_kernel(bits, weights, mixing):
    rows = mixing.shape[1]
    tile = min(256, rows)
    tile_bits = tile.bit_length() - 1
    column = lambda level, low: weights[0, low : low + tile, level : level + 1]
    t = lax.broadcasted_iota(jnp.int32, (tile, tile), 0)
    s = lax.broadcasted_iota(jnp.int32, (tile, tile), 1)
    apart = jnp.bitwise_xor(t, s)
    for low in range(0, rows, tile):
        for left in range(0, low, tile):
            level = tile_bits + ((low // tile) ^ (left // tile)).bit_length()
            mixing[0, low : low + tile, left : left + tile] = jnp.broadcast_to(
                column(level, low), (tile, tile)
            ).astype(BF16)
        mixed = jnp.broadcast_to(column(0, low), (tile, tile))
        for level in range(1, tile_bits + 1):
            mixed = jnp.where(apart >= 1 << (level - 1), column(level, low), mixed)
        mixing[0, low : low + tile, low : low + tile] = jnp.where(s <= t, mixed, 0.0).astype(BF16)


def mixing_matrix(weights_by_token, bits):
    heads, rows, levels = weights_by_token.shape
    return call(
        functools.partial(mixing_kernel, bits),
        [jax.ShapeDtypeStruct((heads, rows, rows), BF16)],
        [weights_by_token],
        grid=(heads,),
        in_specs=[pl.BlockSpec((1, rows, levels), lambda h: (h, 0, 0))],
        out_specs=[pl.BlockSpec((1, rows, rows), lambda h: (h, 0, 0))],
    )[0]


def fetch_columns(pieces, starts, low, whole, sems, act):
    for i, piece in enumerate(pieces):
        column = starts[1, i] - low

        @pl.when((column >= 0) & (column < whole.shape[1]))
        def _():
            along = pl.ds(pl.multiple_of(column, piece.shape[1]), piece.shape[1])
            getattr(pltpu.make_async_copy(piece, whole.at[:, along], sems.at[i]), act)()


def multiply_groups(attended, whole, outs):
    width = outs[0].shape[1]
    for i, out in reversed(list(enumerate(outs))):
        cols = slice(i * width, (i + 1) * width)
        out[...] = jnp.dot(
            attended[...], whole[:, cols], preferred_element_type=F32
        ).astype(BF16)


def finish_kernel(count, terms_count, upper, starts, queries, local, weights, *refs):
    pieces, terms, refs = refs[:count], refs[count : count + terms_count], refs[count + terms_count :]
    attended, *outs = refs[:-7]
    query, sums, own_weights, own_terms, whole, sems, piece_sems = refs[-7:]
    columns = whole.shape[1]
    copies = copy_all(
        [
            pltpu.make_async_copy(array, scratch, sems.at[i])
            for i, (array, scratch) in enumerate(
                [(queries, query), (local, sums), (weights, own_weights)]
                + [(term, own_terms.at[i]) for i, term in enumerate(terms)]
            )
        ]
    )
    fetch_columns(pieces, starts, columns, whole, piece_sems, "start")
    wait_all(copies)
    heads, dim = own_terms.shape[1:3]
    first = own_weights.shape[2] - upper.shape[0]
    rows = query.shape[0]
    tile = min(256, rows)
    for low in range(0, rows, tile):
        span = slice(low, low + tile)
        for head in range(heads):
            own = slice(head * dim, (head + 1) * dim)
            total = sums[span, own]
            for i in range(terms_count):
                level = i if i < 2 else i - 1
                weight = own_weights[head, span, first + level : first + level + 1]
                total += (weight * upper[level]) * jnp.dot(
                    query[span, own], own_terms[i, head], preferred_element_type=F32
                )
            scale = lax.rsqrt(jnp.mean(total * total, axis=-1, keepdims=True) + 1e-06)
            attended[span, own] = (total * scale).astype(BF16)
    fetch_columns(pieces, starts, columns, whole, piece_sems, "wait")
    multiply_groups(attended, whole, outs)


def finish(queries, local, weights, upper, terms, starts, pieces, groups):
    rows, inner = queries.shape
    width = sum(a.size for a in pieces) // inner // groups
    count = groups // 2
    return call(
        functools.partial(finish_kernel, len(pieces), len(terms)),
        [jax.ShapeDtypeStruct(queries.shape, BF16)]
        + [jax.ShapeDtypeStruct((rows, width), BF16)] * count,
        [upper, starts, queries, local, weights, *pieces, *terms],
        [
            pltpu.VMEM(queries.shape, BF16),
            pltpu.VMEM(local.shape, F32),
            pltpu.VMEM(weights.shape, F32),
            pltpu.VMEM((len(terms), *terms[0].shape), BF16),
            pltpu.VMEM((inner, width * count), BF16),
            *semaphores(3 + len(terms), len(pieces)),
        ],
        in_specs=[SMEM] * 2 + [HBM] * (3 + len(pieces) + len(terms)),
        out_specs=[WHOLE(queries.shape)] + [WHOLE((rows, width))] * count,
        grid=(1,),
    )


def output_kernel(count, starts, attended, *refs):
    pieces, (*outs, whole, sems) = refs[:count], refs[count:]
    for act in ("start", "wait"):
        fetch_columns(pieces, starts, 0, whole, sems, act)
    multiply_groups(attended, whole, outs)


def output(attended, starts, pieces, groups):
    rows, inner = attended.shape
    width = sum(a.size for a in pieces) // inner // groups
    count = groups // 2
    return call(
        functools.partial(output_kernel, len(pieces)),
        [jax.ShapeDtypeStruct((rows, width), BF16)] * count,
        [starts, attended, *pieces],
        [pltpu.VMEM((inner, width * count), BF16), *semaphores(len(pieces))],
        in_specs=[SMEM, WHOLE((rows, inner))] + [HBM] * len(pieces),
        out_specs=[WHOLE((rows, width))] * count,
        grid=(1,),
    )


def per_device(tokens, w_query, w_key, w_value, w_out, level_weights):
    n = lax.axis_size("seq")
    groups = lax.axis_size("head")
    here = lax.axis_index("seq")
    group = lax.axis_index("head")
    local_bits = tokens.shape[0].bit_length() - 1
    heads = level_weights.shape[0]
    ringed = n <= LONGEST_RING and n % 2 == 0

    share = n // groups
    depth, width = w_query.shape[0], w_out.shape[1]
    bits = n.bit_length() - 1
    upper = jnp.stack([here >> bit & 1 for bit in range(bits)]).astype(F32)
    weights_by_token = level_weights.transpose(0, 2, 1)
    if ringed:
        key, value, query, out = [
            Ring(w, n, i % 2) for i, w in enumerate((w_key, w_value, w_query, w_out))
        ]
        mixing = mixing_matrix(weights_by_token, local_bits)
        for step in range(1, n // 2 + 1):
            key.advance(*((mixing,) if step == 3 else ()))
            value.advance()
            query.advance()
            if step > 1:
                out.advance(*(key.gate if step == 2 else ()))
        pieces = [[a for a, _ in ring.pieces] for ring in (key, value, query)]
        starts = table([(owner * depth, 0) for _, owner in key.pieces])
    else:
        mixing = mixing_matrix(weights_by_token, local_bits)
        pieces = [
            [lax.all_gather(w, "seq", axis=0, tiled=True)] for w in (w_key, w_value, w_query)
        ]
        starts = table([(0, 0)])
    queries, local, running, rounded = attend_locally(tokens, starts, *pieces, mixing)

    def from_partner(array, apart):
        return lax.ppermute(array, "seq", [(i, i ^ apart) for i in range(n)])

    terms = [from_partner(rounded, apart) for apart in (1, 2, 3)]
    for bit in range(2, bits):
        for term in terms[-3:] if bit == 2 else terms[-1:]:
            running = running + term.astype(F32)
        terms = terms + [from_partner(running.astype(BF16), 1 << bit)]
    if ringed:
        out.advance(rounded)
        out_pieces = [a for a, _ in out.pieces]
        out_starts = [
            (0, ((owner // share ^ group) * share + owner % share) * width)
            for _, owner in out.pieces
        ]
    else:
        whole = lax.all_gather(w_out, "seq", axis=1, tiled=True)
        width *= share
        out_pieces = [
            lax.dynamic_slice_in_dim(whole, (group ^ k) * width, width, 1) for k in range(groups)
        ]
        out_starts = [(0, k * width) for k in range(groups)]

    far = groups.bit_length() - 2

    def from_group(array, bit):
        return lax.ppermute(array, "head", [(g, g ^ 1 << bit) for g in range(groups)])

    def sum_near(shares, kind):
        for bit in range(far):
            theirs = {k ^ 1 << bit: from_group(a, bit) for k, a in shares.items() if k >> bit & 1}
            shares = {
                k: (shares[k].astype(F32) + a.astype(F32)).astype(kind) for k, a in theirs.items()
            }
        (total,) = shares.values()
        return total

    starts = table(out_starts)
    attended, *shares = finish(
        queries, local, weights_by_token, upper, terms, starts, out_pieces, groups
    )
    away = sum_near({groups // 2 + k: a for k, a in enumerate(shares)}, BF16)
    theirs = from_group(away, far)
    shares = output(after(attended, [away]), starts, out_pieces, groups)
    ours = sum_near(dict(enumerate(shares)), F32)
    return (ours.astype(F32) + theirs.astype(F32)).astype(BF16)


def solution(mesh):
    in_specs = (
        P("seq", None),
        P("seq", "head"),
        P("seq", "head"),
        P("seq", "head"),
        P("head", "seq"),
        P("head", None, "seq"),
    )
    out_specs = P("seq", "head")
    return jax.shard_map(
        per_device, mesh=mesh, in_specs=in_specs, out_specs=out_specs, check_vma=False
    )
```

time: 255 us -> 132 us (0.52)
  waiting for transfers between devices: 193 us -> 46.6 us
  starting transfers between devices: 4.07 us -> 49.1 us
  matrix products: 27.8 us -> 0 us
  Pallas kernels: 0 us -> 25.3 us
  between operations: 13.4 us -> 0.27 us
  other arithmetic: 14.4 us -> 4.94 us
  local copies, waits for them, and re-layouts: 2.43 us -> 5.01 us
    all_gather x4 -> x0, waiting for transfers between devices: 150 us -> none  [the longest x1 47 us: per_device(): key_sums = add_rows(lax.all_gather(w_key, 'seq', axis=0, tiled=True))]
    ppermute x3 -> x35, starting transfers between devices: 3.92 us -> 49.1 us  [the longest x28 40.3 us: advance(): self.ways[way] = lax.ppermute(after(piece, gate), 'seq', pairs)]
    ppermute x3 -> x35, waiting for transfers between devices: 10.3 us -> 46.6 us  [the longest x28 28.5 us: advance(): self.ways[way] = lax.ppermute(after(piece, gate), 'seq', pairs)]
    reduce_scatter x1 -> x0, waiting for transfers between devices: 29.8 us -> none  [per_device(): lax.psum_scatter(partial_value.astype(jnp.bfloat16), 'head', scatter_dime...]
    dot_general x7 -> x0, matrix products: 27.8 us -> none  [the longest x1 9.5 us: per_device(): jnp.einsum('hts,shd->thd', weighted, value_vectors, preferred_element_typ...]
    pallas_call x0 -> x4, Pallas kernels: none -> 25.3 us  [call(): pl.pallas_call(kernel, out_shape=outs, scratch_shapes=list(scratch), comp...]
    convert_element_type x7 -> x4, other arithmetic: 10.3 us -> 4.94 us  [the longest x1 2.04 us: per_device(): return (ours.astype(F32) + theirs.astype(F32)).astype(BF16)]
    unnamed x32 -> x59, local copies, waits for them, and re-layouts: 0.53 us -> 3.65 us
  transfers between devices with their start and end apart: 8 -> 35, of which waited for: 7 -> 22; matrix products, arithmetic and copies ran while one was open for 16% -> 4% of each run, Pallas kernels for 0% -> 14%
where the time goes in v2:
time: 132 us; the launch traced here: 131 us
  starting transfers between devices  49.1 us (37%)
  waiting for transfers between devices  46.6 us (35%)
  Pallas kernels  25.3 us (19%)
  local copies, waits for them, and re-layouts  5.01 us (4%)
  other arithmetic  4.94 us (4%)
    ppermute x28, starting transfers between devices, advance(): self.ways[way] = lax.ppermute(after(piece, gate), 'seq', pairs)  40.3 us
    ppermute x28, waiting for transfers between devices, advance(): self.ways[way] = lax.ppermute(after(piece, gate), 'seq', pairs)  28.5 us
    pallas_call x4, Pallas kernels, call(): pl.pallas_call(kernel, out_shape=outs, scratch_shapes=list(scratch), comp...  25.3 us
    ppermute x3, waiting for transfers between devices, from_group(): lax.ppermute(array, 'head', [(g, g ^ 1 << bit) for g in range(groups)])  10.6 us
    ppermute x4, waiting for transfers between devices, from_partner(): return lax.ppermute(array, 'seq', [(i, i ^ apart) for i in range(n)])  7.54 us
    ppermute x4, starting transfers between devices, from_partner(): return lax.ppermute(array, 'seq', [(i, i ^ apart) for i in range(n)])  7.04 us
    unnamed x59, local copies, waits for them, and re-layouts  3.65 us
  transfers between devices with their start and end apart: 35, of which 22 were waited for; matrix products, arithmetic and copies ran while one was open for 4% of the time, Pallas kernels for 14%

profile of v2, /device:TPU:0, one launch (start us, length us, event | category | flops | bytes accessed | tf_op | source)
XLA Modules:
  0.0 131.3 jit_solution(8138927693288011913)
XLA Ops:
  0.0 3.0 %collective-permute-start = (bf16[256,512]{1,0:T(8,128)(2,1)}, bf16[256,512]{1,0:T(8,128)(2,1)S(1)}, u32[]{:S(2)}, u32[]{:S(2)}) collective-permute-start(bf16[256,512]{1,0:T(8,128)(2,1)} %refs_0_.3), channel_id=1, source_target_pairs={{0,8},{8,16},{16,24},{24,28},{28,20},{20,12},{12,4},{4,0},{1,9},{9... | collective-permute-start | bytes 786440 | tf_op jit(solution)/shard_map/ppermute | solution.py:66
  3.0 2.0 %collective-permute-start.7 = (bf16[256,512]{1,0:T(8,128)(2,1)}, bf16[256,512]{1,0:T(8,128)(2,1)S(1)}, u32[]{:S(2)}, u32[]{:S(2)}) collective-permute-start(bf16[256,512]{1,0:T(8,128)(2,1)} %refs_8_.1), channel_id=1, source_target_pairs={{0,8},{8,16},{16,24},{24,28},{28,20},{20,12},{12,4},{4,0},{1,9},{9... | collective-permute-start | bytes 786440 | tf_op jit(solution)/shard_map/ppermute | solution.py:66
  5.1 2.0 %collective-permute-start.14 = (bf16[256,512]{1,0:T(8,128)(2,1)}, bf16[256,512]{1,0:T(8,128)(2,1)S(1)}, u32[]{:S(2)}, u32[]{:S(2)}) collective-permute-start(bf16[256,512]{1,0:T(8,128)(2,1)} %refs_16_.1), channel_id=1, source_target_pairs={{0,8},{8,16},{16,24},{24,28},{28,20},{20,12},{12,4},{4,0},{1,9},{9... | collective-permute-start | bytes 786440 | tf_op jit(solution)/shard_map/ppermute | solution.py:66
  7.1 3.2 %collective-permute-done.refs_1_ = bf16[256,512]{1,0:T(8,128)(2,1)S(1)} collective-permute-done((bf16[256,512]{1,0:T(8,128)(2,1)}, bf16[256,512]{1,0:T(8,128)(2,1)S(1)}, u32[]{:S(2)}, u32[]{:S(2)}) %collective-permute-start) | collective-permute-done | bytes 262176 | tf_op jit(solution)/shard_map/ppermute | solution.py:66
  10.3 2.1 %collective-permute-start.15 = (bf16[256,512]{1,0:T(8,128)(2,1)}, bf16[256,512]{1,0:T(8,128)(2,1)S(1)}, u32[]{:S(2)}, u32[]{:S(2)}) collective-permute-start(bf16[256,512]{1,0:T(8,128)(2,1)} %refs_16_.1), channel_id=1, source_target_pairs={{8,0},{16,8},{24,16},{28,24},{20,28},{12,20},{4,12},{0,4},{9,1},{1... | collective-permute-start | bytes 786440 | tf_op jit(solution)/shard_map/ppermute | solution.py:66
  12.5 1.6 %collective-permute-start.2 = (bf16[256,512]{1,0:T(8,128)(2,1)S(1)}, bf16[256,512]{1,0:T(8,128)(2,1)S(1)}, u32[]{:S(2)}, u32[]{:S(2)}) collective-permute-start(bf16[256,512]{1,0:T(8,128)(2,1)S(1)} %collective-permute-done.refs_1_), channel_id=1, source_target_pairs={{0,8},{8,16},{16,24},{24,28},{28,20},{20,12},{12,4},{4,0},{1,9},{9... | collective-permute-start | bytes 786440 | tf_op jit(solution)/shard_map/ppermute | solution.py:66
  14.0 1.9 %collective-permute-done.7.refs_9_ = bf16[256,512]{1,0:T(8,128)(2,1)S(1)} collective-permute-done((bf16[256,512]{1,0:T(8,128)(2,1)}, bf16[256,512]{1,0:T(8,128)(2,1)S(1)}, u32[]{:S(2)}, u32[]{:S(2)}) %collective-permute-start.7) | collective-permute-done | bytes 262176 | tf_op jit(solution)/shard_map/ppermute | solution.py:66
  15.9 2.1 %collective-permute-start.3 = (bf16[256,512]{1,0:T(8,128)(2,1)S(1)}, bf16[256,512]{1,0:T(8,128)(2,1)S(1)}, u32[]{:S(2)}, u32[]{:S(2)}) collective-permute-start(bf16[256,512]{1,0:T(8,128)(2,1)S(1)} %collective-permute-done.1.refs_2_), channel_id=1, source_target_pairs={{8,0},{16,8},{24,16},{28,24},{20,28},{12,20},{4,12},{0,4},{9,1},{1... | collective-permute-start | bytes 786440 | tf_op jit(solution)/shard_map/ppermute | solution.py:66
  18.1 1.6 %collective-permute-start.9 = (bf16[256,512]{1,0:T(8,128)(2,1)S(1)}, bf16[256,512]{1,0:T(8,128)(2,1)S(1)}, u32[]{:S(2)}, u32[]{:S(2)}) collective-permute-start(bf16[256,512]{1,0:T(8,128)(2,1)S(1)} %collective-permute-done.7.refs_9_), channel_id=1, source_target_pairs={{0,8},{8,16},{16,24},{24,28},{28,20},{20,12},{12,4},{4,0},{1,9},{9... | collective-permute-start | bytes 786440 | tf_op jit(solution)/shard_map/ppermute | solution.py:66
  19.7 1.9 %collective-permute-done.14.refs_17_ = bf16[256,512]{1,0:T(8,128)(2,1)S(1)} collective-permute-done((bf16[256,512]{1,0:T(8,128)(2,1)}, bf16[256,512]{1,0:T(8,128)(2,1)S(1)}, u32[]{:S(2)}, u32[]{:S(2)}) %collective-permute-start.14) | collective-permute-done | bytes 262176 | tf_op jit(solution)/shard_map/ppermute | solution.py:66
  21.5 2.1 %collective-permute-start.10 = (bf16[256,512]{1,0:T(8,128)(2,1)S(1)}, bf16[256,512]{1,0:T(8,128)(2,1)S(1)}, u32[]{:S(2)}, u32[]{:S(2)}) collective-permute-start(bf16[256,512]{1,0:T(8,128)(2,1)S(1)} %collective-permute-done.8.refs_10_), channel_id=1, source_target_pairs={{8,0},{16,8},{24,16},{28,24},{20,28},{12,20},{4,12},{0,4},{9,1},{1... | collective-permute-start | bytes 786440 | tf_op jit(solution)/shard_map/ppermute | solution.py:66
  23.7 1.6 %collective-permute-start.16 = (bf16[256,512]{1,0:T(8,128)(2,1)S(1)}, bf16[256,512]{1,0:T(8,128)(2,1)}, u32[]{:S(2)}, u32[]{:S(2)}) collective-permute-start(bf16[256,512]{1,0:T(8,128)(2,1)S(1)} %collective-permute-done.14.refs_17_), channel_id=1, source_target_pairs={{0,8},{8,16},{16,24},{24,28},{28,20},{20,12},{12,4},{4,0},{1,9},{9... | collective-permute-start | bytes 786440 | tf_op jit(solution)/shard_map/ppermute | solution.py:66
  25.3 1.9 %collective-permute-done.2.refs_3_ = bf16[256,512]{1,0:T(8,128)(2,1)S(1)} collective-permute-done((bf16[256,512]{1,0:T(8,128)(2,1)S(1)}, bf16[256,512]{1,0:T(8,128)(2,1)S(1)}, u32[]{:S(2)}, u32[]{:S(2)}) %collective-permute-start.2) | collective-permute-done | bytes 262176 | tf_op jit(solution)/shard_map/ppermute | solution.py:66
  27.2 2.1 %collective-permute-start.17 = (bf16[256,512]{1,0:T(8,128)(2,1)S(1)}, bf16[256,512]{1,0:T(8,128)(2,1)}, u32[]{:S(2)}, u32[]{:S(2)}) collective-permute-start(bf16[256,512]{1,0:T(8,128)(2,1)S(1)} %collective-permute-done.15.refs_18_), channel_id=1, source_target_pairs={{8,0},{16,8},{24,16},{28,24},{20,28},{12,20},{4,12},{0,4},{9,1},{1... | collective-permute-start | bytes 786440 | tf_op jit(solution)/shard_map/ppermute | solution.py:66
  29.3 1.6 %collective-permute-start.21 = (bf16[512,256]{1,0:T(8,128)(2,1)}, bf16[512,256]{1,0:T(8,128)(2,1)S(1)}, u32[]{:S(2)}, u32[]{:S(2)}) collective-permute-start(bf16[512,256]{1,0:T(8,128)(2,1)} %refs_0_.5), channel_id=1, source_target_pairs={{0,8},{8,16},{16,24},{24,28},{28,20},{20,12},{12,4},{4,0},{1,9},{9... | collective-permute-start | bytes 786440 | tf_op jit(solution)/shard_map/ppermute | solution.py:66
  30.9 1.9 %collective-permute-done.9.refs_11_ = bf16[256,512]{1,0:T(8,128)(2,1)S(1)} collective-permute-done((bf16[256,512]{1,0:T(8,128)(2,1)S(1)}, bf16[256,512]{1,0:T(8,128)(2,1)S(1)}, u32[]{:S(2)}, u32[]{:S(2)}) %collective-permute-start.9) | collective-permute-done | bytes 262176 | tf_op jit(solution)/shard_map/ppermute | solution.py:66
  32.8 2.1 %collective-permute-start.22 = (bf16[512,256]{1,0:T(8,128)(2,1)}, bf16[512,256]{1,0:T(8,128)(2,1)S(1)}, u32[]{:S(2)}, u32[]{:S(2)}) collective-permute-start(bf16[512,256]{1,0:T(8,128)(2,1)} %refs_0_.5), channel_id=1, source_target_pairs={{8,0},{16,8},{24,16},{28,24},{20,28},{12,20},{4,12},{0,4},{9,1},{1... | collective-permute-start | bytes 786440 | tf_op jit(solution)/shard_map/ppermute | solution.py:66
  34.8 2.2 %copy.7 = f32[4,13,512]{1,2,0:T(8,128)} copy(f32[4,13,512]{2,0,1:T(4,128)} %param.11) | data formatting | bytes 212992 | tf_op args[5]
  37.1 4.5 %shard_map.64.mixing = bf16[4,512,512]{2,1,0:T(8,128)(2,1)} custom-call(f32[4,512,13]{2,1,0:T(8,128)} %bitcast.22), custom_call_target="tpu_custom_call" | custom-call | flops 1 | bytes 8814592 | tf_op jit(solution)/shard_map/pallas_call | solution.py:22
  41.8 1.9 %collective-permute-start.5 = (bf16[256,512]{1,0:T(8,128)(2,1)S(1)}, bf16[256,512]{1,0:T(8,128)(2,1)S(1)}, u32[]{:S(2)}, u32[]{:S(2)}) collective-permute-start(bf16[256,512]{1,0:T(8,128)(2,1)S(1)} %collective-permute-done.3.refs_4_), channel_id=1, source_target_pairs={{8,0},{16,8},{24,16},{28,24},{20,28},{12,20},{4,12},{0,4},{9,1},{1... | collective-permute-start | bytes 786440 | tf_op jit(solution)/shard_map/ppermute | solution.py:66
  44.0 2.1 %collective-permute-start.12 = (bf16[256,512]{1,0:T(8,128)(2,1)S(1)}, bf16[256,512]{1,0:T(8,128)(2,1)S(1)}, u32[]{:S(2)}, u32[]{:S(2)}) collective-permute-start(bf16[256,512]{1,0:T(8,128)(2,1)S(1)} %collective-permute-done.10.refs_12_), channel_id=1, source_target_pairs={{8,0},{16,8},{24,16},{28,24},{20,28},{12,20},{4,12},{0,4},{9,1},{1... | collective-permute-start | bytes 786440 | tf_op jit(solution)/shard_map/ppermute | solution.py:66
  46.2 1.6 %collective-permute-start.18 = (bf16[256,512]{1,0:T(8,128)(2,1)}, bf16[256,512]{1,0:T(8,128)(2,1)S(1)}, u32[]{:S(2)}, u32[]{:S(2)}) collective-permute-start(bf16[256,512]{1,0:T(8,128)(2,1)} %collective-permute-done.16.refs_19_), channel_id=1, source_target_pairs={{0,8},{8,16},{16,24},{24,28},{28,20},{20,12},{12,4},{4,0},{1,9},{9... | collective-permute-start | bytes 786440 | tf_op jit(solution)/shard_map/ppermute | solution.py:66
  47.8 3.1 %collective-permute-done.4.refs_5_ = bf16[256,512]{1,0:T(8,128)(2,1)S(1)} collective-permute-done((bf16[256,512]{1,0:T(8,128)(2,1)S(1)}, bf16[256,512]{1,0:T(8,128)(2,1)S(1)}, u32[]{:S(2)}, u32[]{:S(2)}) %collective-permute-start.4) | collective-permute-done | bytes 262176 | tf_op jit(solution)/shard_map/ppermute | solution.py:66
  50.9 1.6 %collective-permute-start.19 = (bf16[256,512]{1,0:T(8,128)(2,1)}, bf16[256,512]{1,0:T(8,128)(2,1)S(1)}, u32[]{:S(2)}, u32[]{:S(2)}) collective-permute-start(bf16[256,512]{1,0:T(8,128)(2,1)} %collective-permute-done.17.refs_20_), channel_id=1, source_target_pairs={{8,0},{16,8},{24,16},{28,24},{20,28},{12,20},{4,12},{0,4},{9,1},{1... | collective-permute-start | bytes 786440 | tf_op jit(solution)/shard_map/ppermute | solution.py:66
  52.5 1.6 %collective-permute-start.24 = (bf16[512,256]{1,0:T(8,128)(2,1)S(1)}, bf16[512,256]{1,0:T(8,128)(2,1)S(1)}, u32[]{:S(2)}, u32[]{:S(2)}) collective-permute-start(bf16[512,256]{1,0:T(8,128)(2,1)S(1)} %collective-permute-done.22.refs_2_), channel_id=1, source_target_pairs={{8,0},{16,8},{24,16},{28,24},{20,28},{12,20},{4,12},{0,4},{9,1},{1... | collective-permute-start | bytes 786440 | tf_op jit(solution)/shard_map/ppermute | solution.py:66
  54.1 2.5 %collective-permute-done.11.refs_13_ = bf16[256,512]{1,0:T(8,128)(2,1)S(1)} collective-permute-done((bf16[256,512]{1,0:T(8,128)(2,1)S(1)}, bf16[256,512]{1,0:T(8,128)(2,1)S(1)}, u32[]{:S(2)}, u32[]{:S(2)}) %collective-permute-start.11) | collective-permute-done | bytes 262176 | tf_op jit(solution)/shard_map/ppermute | solution.py:66
  57.4 1.1 collective-permute-start.13
  58.6 3.6 %collective-permute-done.18.refs_21_ = bf16[256,512]{1,0:T(8,128)(2,1)S(1)} collective-permute-done((bf16[256,512]{1,0:T(8,128)(2,1)}, bf16[256,512]{1,0:T(8,128)(2,1)S(1)}, u32[]{:S(2)}, u32[]{:S(2)}) %collective-permute-start.18) | collective-permute-done | bytes 262176 | tf_op jit(solution)/shard_map/ppermute | solution.py:66
  63.0 1.6 %collective-permute-start.23 = (bf16[512,256]{1,0:T(8,128)(2,1)S(1)}, bf16[512,256]{1,0:T(8,128)(2,1)S(1)}, u32[]{:S(2)}, u32[]{:S(2)}) collective-permute-start(bf16[512,256]{1,0:T(8,128)(2,1)S(1)} %collective-permute-done.21.refs_1_), channel_id=1, source_target_pairs={{0,8},{8,16},{16,24},{24,28},{28,20},{20,12},{12,4},{4,0},{1,9},{9... | collective-permute-start | bytes 786440 | tf_op jit(solution)/shard_map/ppermute | solution.py:66
  64.6 4.0 %collective-permute-done.24.refs_4_ = bf16[512,256]{1,0:T(8,128)(2,1)S(1)} collective-permute-done((bf16[512,256]{1,0:T(8,128)(2,1)S(1)}, bf16[512,256]{1,0:T(8,128)(2,1)S(1)}, u32[]{:S(2)}, u32[]{:S(2)}) %collective-permute-start.24) | collective-permute-done | bytes 262176 | tf_op jit(solution)/shard_map/ppermute | solution.py:66
  68.6 1.1 collective-permute-start.26
  70.5 3.8 %collective-permute-done.13.refs_15_ = bf16[256,512]{1,0:T(8,128)(2,1)S(1)} collective-permute-done((bf16[256,512]{1,0:T(8,128)(2,1)S(1)}, bf16[256,512]{1,0:T(8,128)(2,1)S(1)}, u32[]{:S(2)}, u32[]{:S(2)}) %collective-permute-start.13) | collective-permute-done | bytes 262176 | tf_op jit(solution)/shard_map/ppermute | solution.py:66
  75.0 10.4 %shard_map.65 = (bf16[512,512]{1,0:T(8,128)(2,1)}, f32[512,512]{1,0:T(8,128)}, f32[4,128,128]{2,1,0:T(8,128)}, bf16[4,128,128]{2,1,0:T(8,128)(2,1)}) custom-call(s32[2,8]{1,0:T(2,128)} %stack.103.starts, bf16[512,2048]{1,0:T(8,128)(2,1)} %tokens.1, bf16[4,512,512]{2,1,0:T(8,128)(2,1)} %shard_map.64.mixing, bf16[256,512]{1,0:T(8,128)(2,1)} %refs_0_.3, ...), custom_call_target="tpu_custom_call" | custom-call | flops 1 | bytes 49807616 | tf_op jit(solution)/shard_map/pallas_call | solution.py:22
  85.4 1.2 collective-permute-start.28
  86.6 1.6 %collective-permute-start.29 = (bf16[4,128,128]{2,1,0:T(8,128)(2,1)}, bf16[4,128,128]{2,1,0:T(8,128)(2,1)S(1)}, u32[]{:S(2)}, u32[]{:S(2)}) collective-permute-start(bf16[4,128,128]{2,1,0:T(8,128)(2,1)} %get-tuple-element.24), channel_id=1, source_target_pairs={{0,8},{4,12},{8,0},{12,4},{16,24},{20,28},{24,16},{28,20},{1,9},{5... | collective-permute-start | bytes 393224 | tf_op jit(solution)/shard_map/ppermute | solution.py:356
  89.0 1.6 %collective-permute-start.25 = (bf16[512,256]{1,0:T(8,128)(2,1)S(1)}, bf16[512,256]{1,0:T(8,128)(2,1)S(1)}, u32[]{:S(2)}, u32[]{:S(2)}) collective-permute-start(bf16[512,256]{1,0:T(8,128)(2,1)S(1)} %collective-permute-done.23.refs_3_), channel_id=1, source_target_pairs={{0,8},{8,16},{16,24},{24,28},{28,20},{20,12},{12,4},{4,0},{1,9},{9... | collective-permute-start | bytes 786440 | tf_op jit(solution)/shard_map/ppermute | solution.py:66
  91.0 1.5 %collective-permute-done.28.refs_8_ = bf16[4,128,128]{2,1,0:T(8,128)(2,1)S(1)} collective-permute-done((bf16[4,128,128]{2,1,0:T(8,128)(2,1)}, bf16[4,128,128]{2,1,0:T(8,128)(2,1)S(1)}, u32[]{:S(2)}, u32[]{:S(2)}) %collective-permute-start.28) | collective-permute-done | bytes 131104 | tf_op jit(solution)/shard_map/ppermute | solution.py:356
  93.3 2.3 %collective-permute-done.30.refs_10_ = bf16[4,128,128]{2,1,0:T(8,128)(2,1)S(1)} collective-permute-done((bf16[4,128,128]{2,1,0:T(8,128)(2,1)}, bf16[4,128,128]{2,1,0:T(8,128)(2,1)S(1)}, u32[]{:S(2)}, u32[]{:S(2)}) %collective-permute-start.30) | collective-permute-done | bytes 131104 | tf_op jit(solution)/shard_map/ppermute | solution.py:356
  95.6 1.1 add_convert_fusion.2
  96.6 3.5 %collective-permute-start.31 = (bf16[4,128,128]{2,1,0:T(8,128)(2,1)S(1)}, bf16[4,128,128]{2,1,0:T(8,128)(2,1)S(1)}, u32[]{:S(2)}, u32[]{:S(2)}) collective-permute-start(bf16[4,128,128]{2,1,0:T(8,128)(2,1)S(1)} %add_convert_fusion.2), channel_id=1, source_target_pairs={{0,16},{4,20},{8,24},{12,28},{16,0},{20,4},{24,8},{28,12},{1,17},{... | collective-permute-start | bytes 393224 | tf_op jit(solution)/shard_map/ppermute | solution.py:356
  101.5 3.0 %collective-permute-done.31.refs_11_ = bf16[4,128,128]{2,1,0:T(8,128)(2,1)S(1)} collective-permute-done((bf16[4,128,128]{2,1,0:T(8,128)(2,1)S(1)}, bf16[4,128,128]{2,1,0:T(8,128)(2,1)S(1)}, u32[]{:S(2)}, u32[]{:S(2)}) %collective-permute-start.31) | collective-permute-done | bytes 131104 | tf_op jit(solution)/shard_map/ppermute | solution.py:356
  105.2 6.6 %shard_map.66 = (bf16[512,512]{1,0:T(8,128)(2,1)}, bf16[512,512]{1,0:T(8,128)(2,1)}, bf16[512,512]{1,0:T(8,128)(2,1)}) custom-call(f32[3]{0:T(128)} %add_convert_fusion.3.upper, s32[2,8]{1,0:T(2,128)} %stack.88.starts, bf16[512,512]{1,0:T(8,128)(2,1)} %get-tuple-element.21.queries, f32[512,512]{1,0:T(8,128)} %get-tuple-element.22.local, ...), custom_call_target="tpu_custom_call" | custom-call | flops 1 | bytes 23494960 | tf_op jit(solution)/shard_map/pallas_call | solution.py:22
  111.9 2.1 %collective-permute-done.32 = bf16[512,512]{1,0:T(8,128)(2,1)S(1)} collective-permute-done((bf16[512,512]{1,0:T(8,128)(2,1)}, bf16[512,512]{1,0:T(8,128)(2,1)S(1)}, u32[]{:S(2)}, u32[]{:S(2)}) %collective-permute-start.32) | collective-permute-done | bytes 524320 | tf_op jit(solution)/shard_map/ppermute | solution.py:381
  114.0 1.2 add_convert_fusion.1
  115.2 1.6 %collective-permute-start.34 = (bf16[512,512]{1,0:T(8,128)(2,1)S(1)}, bf16[512,512]{1,0:T(8,128)(2,1)S(1)}, u32[]{:S(2)}, u32[]{:S(2)}) collective-permute-start(bf16[512,512]{1,0:T(8,128)(2,1)S(1)} %add_convert_fusion.1), channel_id=1, source_target_pairs={{0,2},{1,3},{2,0},{3,1},{4,6},{5,7},{6,4},{7,5},{8,10},{9,11},{10,... | collective-permute-start | bytes 1572872 | tf_op jit(solution)/shard_map/ppermute | solution.py:381
  116.8 3.8 %shard_map.67 = (bf16[512,512]{1,0:T(8,128)(2,1)}, bf16[512,512]{1,0:T(8,128)(2,1)}) custom-call(s32[2,8]{1,0:T(2,128)} %stack.88.starts, bf16[512,512]{1,0:T(8,128)(2,1)} %get-tuple-element.30.attended, bf16[512,256]{1,0:T(8,128)(2,1)} %refs_0_.5, bf16[512,256]{1,0:T(8,128)(2,1)} %copy-done, bf16[512,256]{1,0:T(8,128)(2,1)} %copy-done.1, ...), custom_call_target="tpu_custom_call" | custom-call | flops 1 | bytes 14680320 | tf_op jit(solution)/shard_map/pallas_call | solution.py:22
  120.7 8.5 %collective-permute-done.34 = bf16[512,512]{1,0:T(8,128)(2,1)S(1)} collective-permute-done((bf16[512,512]{1,0:T(8,128)(2,1)S(1)}, bf16[512,512]{1,0:T(8,128)(2,1)S(1)}, u32[]{:S(2)}, u32[]{:S(2)}) %collective-permute-start.34) | collective-permute-done | bytes 524320 | tf_op jit(solution)/shard_map/ppermute | solution.py:381
  129.2 2.0 %add_convert_fusion = bf16[512,512]{1,0:T(8,128)(2,1)} fusion(bf16[512,512]{1,0:T(8,128)(2,1)S(1)} %collective-permute-done.34, bf16[512,512]{1,0:T(8,128)(2,1)S(1)} %collective-permute-done.33, bf16[512,512]{1,0:T(8,128)(2,1)} %get-tuple-element.31), kind=kLoop, calls=%fused_computation | loop fusion | flops 1572864 | bytes 2097152 | tf_op jit(solution)/shard_map/convert_element_type | solution.py:400
  (93 shorter events, 8.4 us)
Async XLA Ops:
  0.0 10.3 %collective-permute-start = (bf16[256,512]{1,0:T(8,128)(2,1)}, bf16[256,512]{1,0:T(8,128)(2,1)S(1)}, u32[]{:S(2)}, u32[]{:S(2)}) collective-permute-start(bf16[256,512]{1,0:T(8,128)(2,1)} %refs_0_.3), channel_id=1, source_target_pairs={{0,8},{8,16},{16,24},{24,28},{28,20},{20,12},{12,4},{4,0},{1,9},{9... | collective-permute-start | bytes 786440 | tf_op jit(solution)/shard_map/ppermute | solution.py:66
  3.0 9.4 %collective-permute-start.1 = (bf16[256,512]{1,0:T(8,128)(2,1)}, bf16[256,512]{1,0:T(8,128)(2,1)S(1)}, u32[]{:S(2)}, u32[]{:S(2)}) collective-permute-start(bf16[256,512]{1,0:T(8,128)(2,1)} %refs_0_.3), channel_id=1, source_target_pairs={{8,0},{16,8},{24,16},{28,24},{20,28},{12,20},{4,12},{0,4},{9,1},{1... | collective-permute-start | bytes 786440 | tf_op jit(solution)/shard_map/ppermute | solution.py:66
  3.0 12.9 %collective-permute-start.7 = (bf16[256,512]{1,0:T(8,128)(2,1)}, bf16[256,512]{1,0:T(8,128)(2,1)S(1)}, u32[]{:S(2)}, u32[]{:S(2)}) collective-permute-start(bf16[256,512]{1,0:T(8,128)(2,1)} %refs_8_.1), channel_id=1, source_target_pairs={{0,8},{8,16},{16,24},{24,28},{28,20},{20,12},{12,4},{4,0},{1,9},{9... | collective-permute-start | bytes 786440 | tf_op jit(solution)/shard_map/ppermute | solution.py:66
  5.1 13.0 %collective-permute-start.8 = (bf16[256,512]{1,0:T(8,128)(2,1)}, bf16[256,512]{1,0:T(8,128)(2,1)S(1)}, u32[]{:S(2)}, u32[]{:S(2)}) collective-permute-start(bf16[256,512]{1,0:T(8,128)(2,1)} %refs_8_.1), channel_id=1, source_target_pairs={{8,0},{16,8},{24,16},{28,24},{20,28},{12,20},{4,12},{0,4},{9,1},{1... | collective-permute-start | bytes 786440 | tf_op jit(solution)/shard_map/ppermute | solution.py:66
  5.1 16.5 %collective-permute-start.14 = (bf16[256,512]{1,0:T(8,128)(2,1)}, bf16[256,512]{1,0:T(8,128)(2,1)S(1)}, u32[]{:S(2)}, u32[]{:S(2)}) collective-permute-start(bf16[256,512]{1,0:T(8,128)(2,1)} %refs_16_.1), channel_id=1, source_target_pairs={{0,8},{8,16},{16,24},{24,28},{28,20},{20,12},{12,4},{4,0},{1,9},{9... | collective-permute-start | bytes 786440 | tf_op jit(solution)/shard_map/ppermute | solution.py:66
  10.3 31.2 %copy-start.10 = (bf16[256,512]{1,0:T(8,128)(2,1)}, bf16[256,512]{1,0:T(8,128)(2,1)S(1)}, u32[]{:S(2)}) copy-start(bf16[256,512]{1,0:T(8,128)(2,1)S(1)} %collective-permute-done.refs_1_) | copy-start | bytes 786436
  10.3 13.4 %collective-permute-start.15 = (bf16[256,512]{1,0:T(8,128)(2,1)}, bf16[256,512]{1,0:T(8,128)(2,1)S(1)}, u32[]{:S(2)}, u32[]{:S(2)}) collective-permute-start(bf16[256,512]{1,0:T(8,128)(2,1)} %refs_16_.1), channel_id=1, source_target_pairs={{8,0},{16,8},{24,16},{28,24},{20,28},{12,20},{4,12},{0,4},{9,1},{1... | collective-permute-start | bytes 786440 | tf_op jit(solution)/shard_map/ppermute | solution.py:66
  12.5 29.1 %copy-start.11 = (bf16[256,512]{1,0:T(8,128)(2,1)}, bf16[256,512]{1,0:T(8,128)(2,1)S(1)}, u32[]{:S(2)}) copy-start(bf16[256,512]{1,0:T(8,128)(2,1)S(1)} %collective-permute-done.1.refs_2_) | copy-start | bytes 786436
  12.5 14.7 %collective-permute-start.2 = (bf16[256,512]{1,0:T(8,128)(2,1)S(1)}, bf16[256,512]{1,0:T(8,128)(2,1)S(1)}, u32[]{:S(2)}, u32[]{:S(2)}) collective-permute-start(bf16[256,512]{1,0:T(8,128)(2,1)S(1)} %collective-permute-done.refs_1_), channel_id=1, source_target_pairs={{0,8},{8,16},{16,24},{24,28},{28,20},{20,12},{12,4},{4,0},{1,9},{9... | collective-permute-start | bytes 786440 | tf_op jit(solution)/shard_map/ppermute | solution.py:66
  15.9 25.6 %copy-start.12 = (bf16[256,512]{1,0:T(8,128)(2,1)}, bf16[256,512]{1,0:T(8,128)(2,1)S(1)}, u32[]{:S(2)}) copy-start(bf16[256,512]{1,0:T(8,128)(2,1)S(1)} %collective-permute-done.7.refs_9_) | copy-start | bytes 786436
  15.9 13.4 %collective-permute-start.3 = (bf16[256,512]{1,0:T(8,128)(2,1)S(1)}, bf16[256,512]{1,0:T(8,128)(2,1)S(1)}, u32[]{:S(2)}, u32[]{:S(2)}) collective-permute-start(bf16[256,512]{1,0:T(8,128)(2,1)S(1)} %collective-permute-done.1.refs_2_), channel_id=1, source_target_pairs={{8,0},{16,8},{24,16},{28,24},{20,28},{12,20},{4,12},{0,4},{9,1},{1... | collective-permute-start | bytes 786440 | tf_op jit(solution)/shard_map/ppermute | solution.py:66
  18.1 23.5 %copy-start.13 = (bf16[256,512]{1,0:T(8,128)(2,1)}, bf16[256,512]{1,0:T(8,128)(2,1)S(1)}, u32[]{:S(2)}) copy-start(bf16[256,512]{1,0:T(8,128)(2,1)S(1)} %collective-permute-done.8.refs_10_) | copy-start | bytes 786436
  18.1 14.7 %collective-permute-start.9 = (bf16[256,512]{1,0:T(8,128)(2,1)S(1)}, bf16[256,512]{1,0:T(8,128)(2,1)S(1)}, u32[]{:S(2)}, u32[]{:S(2)}) collective-permute-start(bf16[256,512]{1,0:T(8,128)(2,1)S(1)} %collective-permute-done.7.refs_9_), channel_id=1, source_target_pairs={{0,8},{8,16},{16,24},{24,28},{28,20},{20,12},{12,4},{4,0},{1,9},{9... | collective-permute-start | bytes 786440 | tf_op jit(solution)/shard_map/ppermute | solution.py:66
  21.5 20.0 %copy-start.14 = (bf16[256,512]{1,0:T(8,128)(2,1)}, bf16[256,512]{1,0:T(8,128)(2,1)S(1)}, u32[]{:S(2)}) copy-start(bf16[256,512]{1,0:T(8,128)(2,1)S(1)} %collective-permute-done.14.refs_17_) | copy-start | bytes 786436
  21.5 20.0 %collective-permute-start.10 = (bf16[256,512]{1,0:T(8,128)(2,1)S(1)}, bf16[256,512]{1,0:T(8,128)(2,1)S(1)}, u32[]{:S(2)}, u32[]{:S(2)}) collective-permute-start(bf16[256,512]{1,0:T(8,128)(2,1)S(1)} %collective-permute-done.8.refs_10_), channel_id=1, source_target_pairs={{8,0},{16,8},{24,16},{28,24},{20,28},{12,20},{4,12},{0,4},{9,1},{1... | collective-permute-start | bytes 786440 | tf_op jit(solution)/shard_map/ppermute | solution.py:66
  23.7 17.9 %copy-start.15 = (bf16[256,512]{1,0:T(8,128)(2,1)}, bf16[256,512]{1,0:T(8,128)(2,1)S(1)}, u32[]{:S(2)}) copy-start(bf16[256,512]{1,0:T(8,128)(2,1)S(1)} %collective-permute-done.15.refs_18_) | copy-start | bytes 786436
  23.7 18.1 %collective-permute-start.16 = (bf16[256,512]{1,0:T(8,128)(2,1)S(1)}, bf16[256,512]{1,0:T(8,128)(2,1)}, u32[]{:S(2)}, u32[]{:S(2)}) collective-permute-start(bf16[256,512]{1,0:T(8,128)(2,1)S(1)} %collective-permute-done.14.refs_17_), channel_id=1, source_target_pairs={{0,8},{8,16},{16,24},{24,28},{28,20},{20,12},{12,4},{4,0},{1,9},{9... | collective-permute-start | bytes 786440 | tf_op jit(solution)/shard_map/ppermute | solution.py:66
  27.2 16.5 %collective-permute-start.17 = (bf16[256,512]{1,0:T(8,128)(2,1)S(1)}, bf16[256,512]{1,0:T(8,128)(2,1)}, u32[]{:S(2)}, u32[]{:S(2)}) collective-permute-start(bf16[256,512]{1,0:T(8,128)(2,1)S(1)} %collective-permute-done.15.refs_18_), channel_id=1, source_target_pairs={{8,0},{16,8},{24,16},{28,24},{20,28},{12,20},{4,12},{0,4},{9,1},{1... | collective-permute-start | bytes 786440 | tf_op jit(solution)/shard_map/ppermute | solution.py:66
  29.3 14.7 %collective-permute-start.21 = (bf16[512,256]{1,0:T(8,128)(2,1)}, bf16[512,256]{1,0:T(8,128)(2,1)S(1)}, u32[]{:S(2)}, u32[]{:S(2)}) collective-permute-start(bf16[512,256]{1,0:T(8,128)(2,1)} %refs_0_.5), channel_id=1, source_target_pairs={{0,8},{8,16},{16,24},{24,28},{28,20},{20,12},{12,4},{4,0},{1,9},{9... | collective-permute-start | bytes 786440 | tf_op jit(solution)/shard_map/ppermute | solution.py:66
  32.8 13.4 %collective-permute-start.22 = (bf16[512,256]{1,0:T(8,128)(2,1)}, bf16[512,256]{1,0:T(8,128)(2,1)S(1)}, u32[]{:S(2)}, u32[]{:S(2)}) collective-permute-start(bf16[512,256]{1,0:T(8,128)(2,1)} %refs_0_.5), channel_id=1, source_target_pairs={{8,0},{16,8},{24,16},{28,24},{20,28},{12,20},{4,12},{0,4},{9,1},{1... | collective-permute-start | bytes 786440 | tf_op jit(solution)/shard_map/ppermute | solution.py:66
  41.6 23.0 %copy-start.19 = (bf16[256,512]{1,0:T(8,128)(2,1)}, bf16[256,512]{1,0:T(8,128)(2,1)S(1)}, u32[]{:S(2)}) copy-start(bf16[256,512]{1,0:T(8,128)(2,1)S(1)} %collective-permute-done.10.refs_12_) | copy-start | bytes 786436
  41.6 9.3 %collective-permute-start.4 = (bf16[256,512]{1,0:T(8,128)(2,1)S(1)}, bf16[256,512]{1,0:T(8,128)(2,1)S(1)}, u32[]{:S(2)}, u32[]{:S(2)}) collective-permute-start(bf16[256,512]{1,0:T(8,128)(2,1)S(1)} %collective-permute-done.2.refs_3_), channel_id=1, source_target_pairs={{0,8},{8,16},{16,24},{24,28},{28,20},{20,12},{12,4},{4,0},{1,9},{9... | collective-permute-start | bytes 786440 | tf_op jit(solution)/shard_map/ppermute | solution.py:66
  41.8 10.7 %collective-permute-start.5 = (bf16[256,512]{1,0:T(8,128)(2,1)S(1)}, bf16[256,512]{1,0:T(8,128)(2,1)S(1)}, u32[]{:S(2)}, u32[]{:S(2)}) collective-permute-start(bf16[256,512]{1,0:T(8,128)(2,1)S(1)} %collective-permute-done.3.refs_4_), channel_id=1, source_target_pairs={{8,0},{16,8},{24,16},{28,24},{20,28},{12,20},{4,12},{0,4},{9,1},{1... | collective-permute-start | bytes 786440 | tf_op jit(solution)/shard_map/ppermute | solution.py:66
  43.7 12.8 %collective-permute-start.11 = (bf16[256,512]{1,0:T(8,128)(2,1)S(1)}, bf16[256,512]{1,0:T(8,128)(2,1)S(1)}, u32[]{:S(2)}, u32[]{:S(2)}) collective-permute-start(bf16[256,512]{1,0:T(8,128)(2,1)S(1)} %collective-permute-done.9.refs_11_), channel_id=1, source_target_pairs={{0,8},{8,16},{16,24},{24,28},{28,20},{20,12},{12,4},{4,0},{1,9},{9... | collective-permute-start | bytes 786440 | tf_op jit(solution)/shard_map/ppermute | solution.py:66
  44.0 41.4 %copy-start = (bf16[512,256]{1,0:T(8,128)(2,1)}, bf16[512,256]{1,0:T(8,128)(2,1)S(1)}, u32[]{:S(2)}) copy-start(bf16[512,256]{1,0:T(8,128)(2,1)S(1)} %collective-permute-done.21.refs_1_) | copy-start | bytes 786436
  44.0 13.4 %collective-permute-start.12 = (bf16[256,512]{1,0:T(8,128)(2,1)S(1)}, bf16[256,512]{1,0:T(8,128)(2,1)S(1)}, u32[]{:S(2)}, u32[]{:S(2)}) collective-permute-start(bf16[256,512]{1,0:T(8,128)(2,1)S(1)} %collective-permute-done.10.refs_12_), channel_id=1, source_target_pairs={{8,0},{16,8},{24,16},{28,24},{20,28},{12,20},{4,12},{0,4},{9,1},{1... | collective-permute-start | bytes 786440 | tf_op jit(solution)/shard_map/ppermute | solution.py:66
  46.2 39.2 %copy-start.1 = (bf16[512,256]{1,0:T(8,128)(2,1)}, bf16[512,256]{1,0:T(8,128)(2,1)S(1)}, u32[]{:S(2)}) copy-start(bf16[512,256]{1,0:T(8,128)(2,1)S(1)} %collective-permute-done.22.refs_2_) | copy-start | bytes 786436
  46.2 16.0 %collective-permute-start.18 = (bf16[256,512]{1,0:T(8,128)(2,1)}, bf16[256,512]{1,0:T(8,128)(2,1)S(1)}, u32[]{:S(2)}, u32[]{:S(2)}) collective-permute-start(bf16[256,512]{1,0:T(8,128)(2,1)} %collective-permute-done.16.refs_19_), channel_id=1, source_target_pairs={{0,8},{8,16},{16,24},{24,28},{28,20},{20,12},{12,4},{4,0},{1,9},{9... | collective-permute-start | bytes 786440 | tf_op jit(solution)/shard_map/ppermute | solution.py:66
  50.9 23.4 %copy-start.20 = (bf16[256,512]{1,0:T(8,128)(2,1)}, bf16[256,512]{1,0:T(8,128)(2,1)S(1)}, u32[]{:S(2)}) copy-start(bf16[256,512]{1,0:T(8,128)(2,1)S(1)} %collective-permute-done.4.refs_5_) | copy-start | bytes 786436
  50.9 12.1 %collective-permute-start.19 = (bf16[256,512]{1,0:T(8,128)(2,1)}, bf16[256,512]{1,0:T(8,128)(2,1)S(1)}, u32[]{:S(2)}, u32[]{:S(2)}) collective-permute-start(bf16[256,512]{1,0:T(8,128)(2,1)} %collective-permute-done.17.refs_20_), channel_id=1, source_target_pairs={{8,0},{16,8},{24,16},{28,24},{20,28},{12,20},{4,12},{0,4},{9,1},{1... | collective-permute-start | bytes 786440 | tf_op jit(solution)/shard_map/ppermute | solution.py:66
  52.5 21.8 %copy-start.21 = (bf16[256,512]{1,0:T(8,128)(2,1)}, bf16[256,512]{1,0:T(8,128)(2,1)S(1)}, u32[]{:S(2)}) copy-start(bf16[256,512]{1,0:T(8,128)(2,1)S(1)} %collective-permute-done.5.refs_6_) | copy-start | bytes 786436
  52.5 16.2 %collective-permute-start.24 = (bf16[512,256]{1,0:T(8,128)(2,1)S(1)}, bf16[512,256]{1,0:T(8,128)(2,1)S(1)}, u32[]{:S(2)}, u32[]{:S(2)}) collective-permute-start(bf16[512,256]{1,0:T(8,128)(2,1)S(1)} %collective-permute-done.22.refs_2_), channel_id=1, source_target_pairs={{8,0},{16,8},{24,16},{28,24},{20,28},{12,20},{4,12},{0,4},{9,1},{1... | collective-permute-start | bytes 786440 | tf_op jit(solution)/shard_map/ppermute | solution.py:66
  56.5 17.8 %copy-start.22 = (bf16[256,512]{1,0:T(8,128)(2,1)}, bf16[256,512]{1,0:T(8,128)(2,1)S(1)}, u32[]{:S(2)}) copy-start(bf16[256,512]{1,0:T(8,128)(2,1)S(1)} %collective-permute-done.11.refs_13_) | copy-start | bytes 786436
  56.5 13.9 %collective-permute-start.6 = (bf16[256,512]{1,0:T(8,128)(2,1)S(1)}, bf16[256,512]{1,0:T(8,128)(2,1)S(1)}, u32[]{:S(2)}, u32[]{:S(2)}) collective-permute-start(bf16[256,512]{1,0:T(8,128)(2,1)S(1)} %collective-permute-done.4.refs_5_), channel_id=1, source_target_pairs={{0,8},{8,16},{16,24},{24,28},{28,20},{20,12},{12,4},{4,0},{1,9},{9... | collective-permute-start | bytes 786440 | tf_op jit(solution)/shard_map/ppermute | solution.py:66
  57.4 16.9 %copy-start.23 = (bf16[256,512]{1,0:T(8,128)(2,1)}, bf16[256,512]{1,0:T(8,128)(2,1)S(1)}, u32[]{:S(2)}) copy-start(bf16[256,512]{1,0:T(8,128)(2,1)S(1)} %collective-permute-done.12.refs_14_) | copy-start | bytes 786436
  57.4 16.9 %collective-permute-start.13 = (bf16[256,512]{1,0:T(8,128)(2,1)S(1)}, bf16[256,512]{1,0:T(8,128)(2,1)S(1)}, u32[]{:S(2)}, u32[]{:S(2)}) collective-permute-start(bf16[256,512]{1,0:T(8,128)(2,1)S(1)} %collective-permute-done.12.refs_14_), channel_id=1, source_target_pairs={{8,0},{16,8},{24,16},{28,24},{20,28},{12,20},{4,12},{0,4},{9,1},{1... | collective-permute-start | bytes 786440 | tf_op jit(solution)/shard_map/ppermute | solution.py:66
  62.1 12.1 %collective-permute-start.20 = (bf16[256,512]{1,0:T(8,128)(2,1)S(1)}, bf16[256,512]{1,0:T(8,128)(2,1)}, u32[]{:S(2)}, u32[]{:S(2)}) collective-permute-start(bf16[256,512]{1,0:T(8,128)(2,1)S(1)} %collective-permute-done.18.refs_21_), channel_id=1, source_target_pairs={{0,8},{8,16},{16,24},{24,28},{28,20},{20,12},{12,4},{4,0},{1,9},{9... | collective-permute-start | bytes 786440 | tf_op jit(solution)/shard_map/ppermute | solution.py:66
  63.0 26.0 %collective-permute-start.23 = (bf16[512,256]{1,0:T(8,128)(2,1)S(1)}, bf16[512,256]{1,0:T(8,128)(2,1)S(1)}, u32[]{:S(2)}, u32[]{:S(2)}) collective-permute-start(bf16[512,256]{1,0:T(8,128)(2,1)S(1)} %collective-permute-done.21.refs_1_), channel_id=1, source_target_pairs={{0,8},{8,16},{16,24},{24,28},{28,20},{20,12},{12,4},{4,0},{1,9},{9... | collective-permute-start | bytes 786440 | tf_op jit(solution)/shard_map/ppermute | solution.py:66
  68.6 21.9 %collective-permute-start.26 = (bf16[512,256]{1,0:T(8,128)(2,1)S(1)}, bf16[512,256]{1,0:T(8,128)(2,1)S(1)}, u32[]{:S(2)}, u32[]{:S(2)}) collective-permute-start(bf16[512,256]{1,0:T(8,128)(2,1)S(1)} %collective-permute-done.24.refs_4_), channel_id=1, source_target_pairs={{8,0},{16,8},{24,16},{28,24},{20,28},{12,20},{4,12},{0,4},{9,1},{1... | collective-permute-start | bytes 786440 | tf_op jit(solution)/shard_map/ppermute | solution.py:66
  85.4 7.0 %collective-permute-start.28 = (bf16[4,128,128]{2,1,0:T(8,128)(2,1)}, bf16[4,128,128]{2,1,0:T(8,128)(2,1)S(1)}, u32[]{:S(2)}, u32[]{:S(2)}) collective-permute-start(bf16[4,128,128]{2,1,0:T(8,128)(2,1)} %get-tuple-element.24), channel_id=1, source_target_pairs={{0,4},{4,0},{8,12},{12,8},{16,20},{20,16},{24,28},{28,24},{1,5},{5... | collective-permute-start | bytes 393224 | tf_op jit(solution)/shard_map/ppermute | solution.py:356
  86.6 6.6 %collective-permute-start.29 = (bf16[4,128,128]{2,1,0:T(8,128)(2,1)}, bf16[4,128,128]{2,1,0:T(8,128)(2,1)S(1)}, u32[]{:S(2)}, u32[]{:S(2)}) collective-permute-start(bf16[4,128,128]{2,1,0:T(8,128)(2,1)} %get-tuple-element.24), channel_id=1, source_target_pairs={{0,8},{4,12},{8,0},{12,4},{16,24},{20,28},{24,16},{28,20},{1,9},{5... | collective-permute-start | bytes 393224 | tf_op jit(solution)/shard_map/ppermute | solution.py:356
  88.2 7.4 %collective-permute-start.30 = (bf16[4,128,128]{2,1,0:T(8,128)(2,1)}, bf16[4,128,128]{2,1,0:T(8,128)(2,1)S(1)}, u32[]{:S(2)}, u32[]{:S(2)}) collective-permute-start(bf16[4,128,128]{2,1,0:T(8,128)(2,1)} %get-tuple-element.24), channel_id=1, source_target_pairs={{0,12},{4,8},{8,4},{12,0},{16,28},{20,24},{24,20},{28,16},{1,13},{... | collective-permute-start | bytes 393224 | tf_op jit(solution)/shard_map/ppermute | solution.py:356
  89.0 12.5 %collective-permute-start.25 = (bf16[512,256]{1,0:T(8,128)(2,1)S(1)}, bf16[512,256]{1,0:T(8,128)(2,1)S(1)}, u32[]{:S(2)}, u32[]{:S(2)}) collective-permute-start(bf16[512,256]{1,0:T(8,128)(2,1)S(1)} %collective-permute-done.23.refs_3_), channel_id=1, source_target_pairs={{0,8},{8,16},{16,24},{24,28},{28,20},{20,12},{12,4},{4,0},{1,9},{9... | collective-permute-start | bytes 786440 | tf_op jit(solution)/shard_map/ppermute | solution.py:66
  90.6 13.9 %collective-permute-start.27 = (bf16[512,256]{1,0:T(8,128)(2,1)S(1)}, bf16[512,256]{1,0:T(8,128)(2,1)S(1)}, u32[]{:S(2)}, u32[]{:S(2)}) collective-permute-start(bf16[512,256]{1,0:T(8,128)(2,1)S(1)} %collective-permute-done.26.refs_6_), channel_id=1, source_target_pairs={{8,0},{16,8},{24,16},{28,24},{20,28},{12,20},{4,12},{0,4},{9,1},{1... | collective-permute-start | bytes 786440 | tf_op jit(solution)/shard_map/ppermute | solution.py:66
  96.6 7.8 %collective-permute-start.31 = (bf16[4,128,128]{2,1,0:T(8,128)(2,1)S(1)}, bf16[4,128,128]{2,1,0:T(8,128)(2,1)S(1)}, u32[]{:S(2)}, u32[]{:S(2)}) collective-permute-start(bf16[4,128,128]{2,1,0:T(8,128)(2,1)S(1)} %add_convert_fusion.2), channel_id=1, source_target_pairs={{0,16},{4,20},{8,24},{12,28},{16,0},{20,4},{24,8},{28,12},{1,17},{... | collective-permute-start | bytes 393224 | tf_op jit(solution)/shard_map/ppermute | solution.py:356
  111.8 2.2 %collective-permute-start.32 = (bf16[512,512]{1,0:T(8,128)(2,1)}, bf16[512,512]{1,0:T(8,128)(2,1)S(1)}, u32[]{:S(2)}, u32[]{:S(2)}) collective-permute-start(bf16[512,512]{1,0:T(8,128)(2,1)} %get-tuple-element.29), channel_id=1, source_target_pairs={{0,1},{1,0},{2,3},{3,2},{4,5},{5,4},{6,7},{7,6},{8,9},{9,8},{10,11... | collective-permute-start | bytes 1572872 | tf_op jit(solution)/shard_map/ppermute | solution.py:381
  115.2 14.0 %collective-permute-start.34 = (bf16[512,512]{1,0:T(8,128)(2,1)S(1)}, bf16[512,512]{1,0:T(8,128)(2,1)S(1)}, u32[]{:S(2)}, u32[]{:S(2)}) collective-permute-start(bf16[512,512]{1,0:T(8,128)(2,1)S(1)} %add_convert_fusion.1), channel_id=1, source_target_pairs={{0,2},{1,3},{2,0},{3,1},{4,6},{5,7},{6,4},{7,5},{8,10},{9,11},{10,... | collective-permute-start | bytes 1572872 | tf_op jit(solution)/shard_map/ppermute | solution.py:381
  120.7 8.6 %collective-permute-start.33 = (bf16[512,512]{1,0:T(8,128)(2,1)}, bf16[512,512]{1,0:T(8,128)(2,1)S(1)}, u32[]{:S(2)}, u32[]{:S(2)}) collective-permute-start(bf16[512,512]{1,0:T(8,128)(2,1)} %get-tuple-element.32), channel_id=1, source_target_pairs={{0,1},{1,0},{2,3},{3,2},{4,5},{5,4},{6,7},{7,6},{8,9},{9,8},{10,11... | collective-permute-start | bytes 1572872 | tf_op jit(solution)/shard_map/ppermute | solution.py:381
  (16 other events, 148.7 us)

commit v3 on v2

--- a/solution.py
+++ b/solution.py
@@ -117,23 +117,16 @@
     )
 
 
-def local_kernel(count, starts, tokens, mixing, *refs):
-    key_pieces, value_pieces, query_pieces = [
-        refs[i * count : (i + 1) * count] for i in range(3)
-    ]
-    queries, local, states, rounded, *refs = refs[3 * count :]
-    own_tokens, *wholes, keys, values, own_mixing, token_sems, mixing_sems, sems = refs
-    rows, width = queries.shape
+def key_value_kernel(count, starts, tokens, *refs):
+    key_pieces, value_pieces, refs = refs[:count], refs[count : 2 * count], refs[2 * count :]
+    keys, values, states, rounded, own_tokens, whole, whole_values, token_sems, sems = refs
+    copies = fetch_rows(tokens, own_tokens, token_sems)
+    wait_all(copies + fetch(key_pieces, starts, whole, sems.at[0]))
+    copies = fetch(value_pieces, starts, whole_values, sems.at[1])
+    multiply(own_tokens, whole, keys)
+    wait_all(copies)
+    multiply(own_tokens, whole_values, values)
     heads, dim = states.shape[:2]
-    copies = fetch_rows(tokens, own_tokens, token_sems)
-    copies += fetch(key_pieces, starts, wholes[0], sems.at[0])
-    wait_all(copies)
-    copies = fetch(value_pieces, starts, wholes[1], sems.at[1])
-    multiply(own_tokens, wholes[0], keys)
-    wait_all(copies)
-    copies = fetch(query_pieces, starts, wholes[2], sems.at[2])
-    copies += fetch_rows(mixing, own_mixing, mixing_sems)
-    multiply(own_tokens, wholes[1], values)
     for head in range(heads):
         own = slice(head * dim, (head + 1) * dim)
         sums = lax.dot_general(
@@ -141,8 +134,48 @@
         )
         states[head] = sums
         rounded[head] = sums.astype(BF16)
+
+
+def project_keys_values(tokens, starts, key_pieces, value_pieces, heads):
+    arrays = [*key_pieces, *value_pieces]
+    count = len(key_pieces)
+    rows, depth = tokens.shape
+    width = arrays[0].shape[1]
+    dim = width // heads
+    shapes = [(rows, width)] * 2 + [(heads, dim, dim)] * 2
+    return call(
+        functools.partial(key_value_kernel, count),
+        [jax.ShapeDtypeStruct(s, t) for s, t in zip(shapes, (BF16, BF16, F32, BF16))],
+        [starts, tokens, *arrays],
+        [
+            pltpu.VMEM((rows, depth), BF16),
+            *[pltpu.VMEM((depth, width), BF16)] * 2,
+            *semaphores(8),
+            pltpu.SemaphoreType.DMA((2, count)),
+        ],
+        in_specs=[SMEM] + [HBM] * (1 + len(arrays)),
+        out_specs=[WHOLE(s) for s in shapes],
+        grid=(1,),
+    )
+
+
+def local_kernel(starts, tokens, keys, values, mixing, *refs):
+    *pieces, queries, local, own_tokens, whole, key, value, mix, token_sems, mix_sems, sems, more = refs
+    copies = fetch_rows(tokens, own_tokens, token_sems)
+    copies += fetch(pieces, starts, whole, sems)
     wait_all(copies)
-    multiply(own_tokens, wholes[2], queries)
+    copies = fetch_rows(mixing, mix, mix_sems)
+    copies += copy_all(
+        [
+            pltpu.make_async_copy(keys, key, more.at[0]),
+            pltpu.make_async_copy(values, value, more.at[1]),
+        ]
+    )
+    multiply(own_tokens, whole, queries)
+    wait_all(copies)
+    rows = queries.shape[0]
+    heads = mix.shape[0]
+    dim = queries.shape[1] // heads
     tile = min(256, rows)
     for head in range(heads):
         own = slice(head * dim, (head + 1) * dim)
@@ -150,36 +183,30 @@
             span, seen = slice(low, low + tile), slice(0, low + tile)
             scores = lax.dot_general(
                 queries[span, own],
-                keys[seen, own],
+                key[seen, own],
                 (((1,), (1,)), ((), ())),
                 preferred_element_type=F32,
             )
-            mixed = (scores * own_mixing[head, span, seen].astype(F32)).astype(BF16)
-            local[span, own] = jnp.dot(mixed, values[seen, own], preferred_element_type=F32)
-
-
-def attend_locally(tokens, starts, key_pieces, value_pieces, query_pieces, mixing):
-    arrays = [*key_pieces, *value_pieces, *query_pieces]
-    count = len(key_pieces)
+            mixed = (scores * mix[head, span, seen].astype(F32)).astype(BF16)
+            local[span, own] = jnp.dot(mixed, value[seen, own], preferred_element_type=F32)
+
+
+def attend_locally(tokens, starts, pieces, keys, values, mixing):
     rows, depth = tokens.shape
-    width = arrays[0].shape[1]
-    heads = mixing.shape[0]
-    dim = width // heads
-    shapes = [(rows, width)] * 2 + [(heads, dim, dim)] * 2
+    shape = keys.shape
     return call(
-        functools.partial(local_kernel, count),
-        [jax.ShapeDtypeStruct(s, t) for s, t in zip(shapes, (BF16, F32, F32, BF16))],
-        [starts, tokens, mixing, *arrays],
+        local_kernel,
+        [jax.ShapeDtypeStruct(shape, BF16), jax.ShapeDtypeStruct(shape, F32)],
+        [starts, tokens, keys, values, mixing, *pieces],
         [
             pltpu.VMEM((rows, depth), BF16),
-            *[pltpu.VMEM((depth, width), BF16)] * 3,
-            *[pltpu.VMEM((rows, width), BF16)] * 2,
+            pltpu.VMEM((depth, shape[1]), BF16),
+            *[pltpu.VMEM(shape, BF16)] * 2,
             pltpu.VMEM(mixing.shape, BF16),
-            *semaphores(8, heads),
-            pltpu.SemaphoreType.DMA((3, count)),
+            *semaphores(8, mixing.shape[0], len(pieces), 2),
         ],
-        in_specs=[SMEM] + [HBM] * (2 + len(arrays)),
-        out_specs=[WHOLE(s) for s in shapes],
+        in_specs=[SMEM] + [HBM] * (4 + len(pieces)),
+        out_specs=[WHOLE(shape)] * 2,
         grid=(1,),
     )
 
@@ -350,7 +377,8 @@
             [lax.all_gather(w, "seq", axis=0, tiled=True)] for w in (w_key, w_value, w_query)
         ]
         starts = table([(0, 0)])
-    queries, local, running, rounded = attend_locally(tokens, starts, *pieces, mixing)
+    *pieces, query_pieces = pieces
+    keys, values, running, rounded = project_keys_values(tokens, starts, *pieces, heads)
 
     def from_partner(array, apart):
         return lax.ppermute(array, "seq", [(i, i ^ apart) for i in range(n)])
@@ -360,6 +388,8 @@
         for term in terms[-3:] if bit == 2 else terms[-1:]:
             running = running + term.astype(F32)
         terms = terms + [from_partner(running.astype(BF16), 1 << bit)]
+    tokens = after(tokens, [running])
+    queries, local = attend_locally(tokens, starts, query_pieces, keys, values, mixing)
     if ringed:
         out.advance(rounded)
         out_pieces = [a for a, _ in out.pieces]

time: 132 us -> 123 us (0.932)
  waiting for transfers between devices: 46.6 us -> 39.3 us
  starting transfers between devices: 49.1 us -> 44.4 us
  Pallas kernels: 25.3 us -> 28.9 us
    ppermute x4, waiting for transfers between devices: 7.54 us -> 2.47 us  [from_partner(): return lax.ppermute(array, 'seq', [(i, i ^ apart) for i in range(n)])]
    pallas_call x4 -> x5, Pallas kernels: 25.3 us -> 28.9 us  [call(): pl.pallas_call(kernel, out_shape=outs, scratch_shapes=list(scratch), comp...]
    ppermute x4, starting transfers between devices: 7.04 us -> 4.38 us  [from_partner(): return lax.ppermute(array, 'seq', [(i, i ^ apart) for i in range(n)])]
    ppermute x28, waiting for transfers between devices: 28.5 us -> 26.2 us  [advance(): self.ways[way] = lax.ppermute(after(piece, gate), 'seq', pairs)]
    ppermute x28, starting transfers between devices: 40.3 us -> 38.2 us  [advance(): self.ways[way] = lax.ppermute(after(piece, gate), 'seq', pairs)]
    unnamed x59 -> x65, local copies, waits for them, and re-layouts: 3.65 us -> 3.96 us
  transfers between devices with their start and end apart: 35 -> 35, of which waited for: 22 -> 20; matrix products, arithmetic and copies ran while one was open for 4% -> 4% of each run, Pallas kernels for 14% -> 18%
where the time goes in v3:
time: 123 us
  starting transfers between devices  44.4 us (36%)
  waiting for transfers between devices  39.3 us (32%)
  Pallas kernels  28.9 us (23%)
  local copies, waits for them, and re-layouts  5.27 us (4%)
  other arithmetic  4.83 us (4%)
    ppermute x28, starting transfers between devices, advance(): self.ways[way] = lax.ppermute(after(piece, gate), 'seq', pairs)  38.2 us
    pallas_call x5, Pallas kernels, call(): pl.pallas_call(kernel, out_shape=outs, scratch_shapes=list(scratch), comp...  28.9 us
    ppermute x28, waiting for transfers between devices, advance(): self.ways[way] = lax.ppermute(after(piece, gate), 'seq', pairs)  26.2 us
    ppermute x3, waiting for transfers between devices, from_group(): lax.ppermute(array, 'head', [(g, g ^ 1 << bit) for g in range(groups)])  10.6 us
    ppermute x4, starting transfers between devices, from_partner(): return lax.ppermute(array, 'seq', [(i, i ^ apart) for i in range(n)])  4.38 us
    unnamed x65, local copies, waits for them, and re-layouts  3.96 us
    ppermute x4, waiting for transfers between devices, from_partner(): return lax.ppermute(array, 'seq', [(i, i ^ apart) for i in range(n)])  2.47 us
  transfers between devices with their start and end apart: 35, of which 20 were waited for; matrix products, arithmetic and copies ran while one was open for 4% of the time, Pallas kernels for 18%

profile of v3, /device:TPU:0, one launch (start us, length us, event | category | flops | bytes accessed | tf_op | source)
XLA Modules:
  0.0 123.0 jit_solution(17375125936760464055)
XLA Ops:
  0.0 3.0 %collective-permute-start = (bf16[256,512]{1,0:T(8,128)(2,1)}, bf16[256,512]{1,0:T(8,128)(2,1)S(1)}, u32[]{:S(2)}, u32[]{:S(2)}) collective-permute-start(bf16[256,512]{1,0:T(8,128)(2,1)} %refs_0_.4), channel_id=1, source_target_pairs={{0,8},{8,16},{16,24},{24,28},{28,20},{20,12},{12,4},{4,0},{1,9},{9... | collective-permute-start | bytes 786440 | tf_op jit(solution)/shard_map/ppermute | solution.py:66
  3.0 2.0 %collective-permute-start.7 = (bf16[256,512]{1,0:T(8,128)(2,1)}, bf16[256,512]{1,0:T(8,128)(2,1)S(1)}, u32[]{:S(2)}, u32[]{:S(2)}) collective-permute-start(bf16[256,512]{1,0:T(8,128)(2,1)} %refs_8_.1), channel_id=1, source_target_pairs={{0,8},{8,16},{16,24},{24,28},{28,20},{20,12},{12,4},{4,0},{1,9},{9... | collective-permute-start | bytes 786440 | tf_op jit(solution)/shard_map/ppermute | solution.py:66
  5.1 2.0 %collective-permute-start.17 = (bf16[256,512]{1,0:T(8,128)(2,1)}, bf16[256,512]{1,0:T(8,128)(2,1)S(1)}, u32[]{:S(2)}, u32[]{:S(2)}) collective-permute-start(bf16[256,512]{1,0:T(8,128)(2,1)} %refs_0_.5), channel_id=1, source_target_pairs={{0,8},{8,16},{16,24},{24,28},{28,20},{20,12},{12,4},{4,0},{1,9},{9... | collective-permute-start | bytes 786440 | tf_op jit(solution)/shard_map/ppermute | solution.py:66
  7.1 3.2 %collective-permute-done.refs_1_ = bf16[256,512]{1,0:T(8,128)(2,1)S(1)} collective-permute-done((bf16[256,512]{1,0:T(8,128)(2,1)}, bf16[256,512]{1,0:T(8,128)(2,1)S(1)}, u32[]{:S(2)}, u32[]{:S(2)}) %collective-permute-start) | collective-permute-done | bytes 262176 | tf_op jit(solution)/shard_map/ppermute | solution.py:66
  10.3 2.1 %collective-permute-start.18 = (bf16[256,512]{1,0:T(8,128)(2,1)}, bf16[256,512]{1,0:T(8,128)(2,1)S(1)}, u32[]{:S(2)}, u32[]{:S(2)}) collective-permute-start(bf16[256,512]{1,0:T(8,128)(2,1)} %refs_0_.5), channel_id=1, source_target_pairs={{8,0},{16,8},{24,16},{28,24},{20,28},{12,20},{4,12},{0,4},{9,1},{1... | collective-permute-start | bytes 786440 | tf_op jit(solution)/shard_map/ppermute | solution.py:66
  12.5 1.6 %collective-permute-start.2 = (bf16[256,512]{1,0:T(8,128)(2,1)S(1)}, bf16[256,512]{1,0:T(8,128)(2,1)S(1)}, u32[]{:S(2)}, u32[]{:S(2)}) collective-permute-start(bf16[256,512]{1,0:T(8,128)(2,1)S(1)} %collective-permute-done.refs_1_), channel_id=1, source_target_pairs={{0,8},{8,16},{16,24},{24,28},{28,20},{20,12},{12,4},{4,0},{1,9},{9... | collective-permute-start | bytes 786440 | tf_op jit(solution)/shard_map/ppermute | solution.py:66
  14.0 1.9 %collective-permute-done.7.refs_9_ = bf16[256,512]{1,0:T(8,128)(2,1)S(1)} collective-permute-done((bf16[256,512]{1,0:T(8,128)(2,1)}, bf16[256,512]{1,0:T(8,128)(2,1)S(1)}, u32[]{:S(2)}, u32[]{:S(2)}) %collective-permute-start.7) | collective-permute-done | bytes 262176 | tf_op jit(solution)/shard_map/ppermute | solution.py:66
  15.9 2.1 %collective-permute-start.3 = (bf16[256,512]{1,0:T(8,128)(2,1)S(1)}, bf16[256,512]{1,0:T(8,128)(2,1)S(1)}, u32[]{:S(2)}, u32[]{:S(2)}) collective-permute-start(bf16[256,512]{1,0:T(8,128)(2,1)S(1)} %collective-permute-done.1.refs_2_), channel_id=1, source_target_pairs={{8,0},{16,8},{24,16},{28,24},{20,28},{12,20},{4,12},{0,4},{9,1},{1... | collective-permute-start | bytes 786440 | tf_op jit(solution)/shard_map/ppermute | solution.py:66
  18.1 1.6 %collective-permute-start.9 = (bf16[256,512]{1,0:T(8,128)(2,1)S(1)}, bf16[256,512]{1,0:T(8,128)(2,1)S(1)}, u32[]{:S(2)}, u32[]{:S(2)}) collective-permute-start(bf16[256,512]{1,0:T(8,128)(2,1)S(1)} %collective-permute-done.7.refs_9_), channel_id=1, source_target_pairs={{0,8},{8,16},{16,24},{24,28},{28,20},{20,12},{12,4},{4,0},{1,9},{9... | collective-permute-start | bytes 786440 | tf_op jit(solution)/shard_map/ppermute | solution.py:66
  19.7 1.9 %collective-permute-done.17.refs_1_ = bf16[256,512]{1,0:T(8,128)(2,1)S(1)} collective-permute-done((bf16[256,512]{1,0:T(8,128)(2,1)}, bf16[256,512]{1,0:T(8,128)(2,1)S(1)}, u32[]{:S(2)}, u32[]{:S(2)}) %collective-permute-start.17) | collective-permute-done | bytes 262176 | tf_op jit(solution)/shard_map/ppermute | solution.py:66
  21.5 2.1 %collective-permute-start.10 = (bf16[256,512]{1,0:T(8,128)(2,1)S(1)}, bf16[256,512]{1,0:T(8,128)(2,1)S(1)}, u32[]{:S(2)}, u32[]{:S(2)}) collective-permute-start(bf16[256,512]{1,0:T(8,128)(2,1)S(1)} %collective-permute-done.8.refs_10_), channel_id=1, source_target_pairs={{8,0},{16,8},{24,16},{28,24},{20,28},{12,20},{4,12},{0,4},{9,1},{1... | collective-permute-start | bytes 786440 | tf_op jit(solution)/shard_map/ppermute | solution.py:66
  23.7 1.6 %collective-permute-start.19 = (bf16[256,512]{1,0:T(8,128)(2,1)S(1)}, bf16[256,512]{1,0:T(8,128)(2,1)S(1)}, u32[]{:S(2)}, u32[]{:S(2)}) collective-permute-start(bf16[256,512]{1,0:T(8,128)(2,1)S(1)} %collective-permute-done.17.refs_1_), channel_id=1, source_target_pairs={{0,8},{8,16},{16,24},{24,28},{28,20},{20,12},{12,4},{4,0},{1,9},{9... | collective-permute-start | bytes 786440 | tf_op jit(solution)/shard_map/ppermute | solution.py:66
  25.3 1.9 %collective-permute-done.2.refs_3_ = bf16[256,512]{1,0:T(8,128)(2,1)S(1)} collective-permute-done((bf16[256,512]{1,0:T(8,128)(2,1)S(1)}, bf16[256,512]{1,0:T(8,128)(2,1)S(1)}, u32[]{:S(2)}, u32[]{:S(2)}) %collective-permute-start.2) | collective-permute-done | bytes 262176 | tf_op jit(solution)/shard_map/ppermute | solution.py:66
  27.2 2.1 %collective-permute-start.25 = (bf16[512,256]{1,0:T(8,128)(2,1)}, bf16[512,256]{1,0:T(8,128)(2,1)S(1)}, u32[]{:S(2)}, u32[]{:S(2)}) collective-permute-start(bf16[512,256]{1,0:T(8,128)(2,1)} %refs_0_.7), channel_id=1, source_target_pairs={{8,0},{16,8},{24,16},{28,24},{20,28},{12,20},{4,12},{0,4},{9,1},{1... | collective-permute-start | bytes 786440 | tf_op jit(solution)/shard_map/ppermute | solution.py:66
  29.2 2.3 %copy.7 = f32[4,13,512]{1,2,0:T(8,128)} copy(f32[4,13,512]{2,0,1:T(4,128)} %param.11) | data formatting | bytes 212992 | tf_op args[5]
  31.5 4.5 %shard_map.64.mixing = bf16[4,512,512]{2,1,0:T(8,128)(2,1)} custom-call(f32[4,512,13]{2,1,0:T(8,128)} %bitcast.22), custom_call_target="tpu_custom_call" | custom-call | flops 1 | bytes 8814592 | tf_op jit(solution)/shard_map/pallas_call | solution.py:22
  36.2 2.0 %collective-permute-start.4 = (bf16[256,512]{1,0:T(8,128)(2,1)S(1)}, bf16[256,512]{1,0:T(8,128)(2,1)S(1)}, u32[]{:S(2)}, u32[]{:S(2)}) collective-permute-start(bf16[256,512]{1,0:T(8,128)(2,1)S(1)} %collective-permute-done.2.refs_3_), channel_id=1, source_target_pairs={{0,8},{8,16},{16,24},{24,28},{28,20},{20,12},{12,4},{4,0},{1,9},{9... | collective-permute-start | bytes 786440 | tf_op jit(solution)/shard_map/ppermute | solution.py:66
  38.4 2.1 %collective-permute-start.5 = (bf16[256,512]{1,0:T(8,128)(2,1)S(1)}, bf16[256,512]{1,0:T(8,128)(2,1)S(1)}, u32[]{:S(2)}, u32[]{:S(2)}) collective-permute-start(bf16[256,512]{1,0:T(8,128)(2,1)S(1)} %collective-permute-done.3.refs_4_), channel_id=1, source_target_pairs={{8,0},{16,8},{24,16},{28,24},{20,28},{12,20},{4,12},{0,4},{9,1},{1... | collective-permute-start | bytes 786440 | tf_op jit(solution)/shard_map/ppermute | solution.py:66
  40.5 1.6 %collective-permute-start.27 = (bf16[512,256]{1,0:T(8,128)(2,1)S(1)}, bf16[512,256]{1,0:T(8,128)(2,1)S(1)}, u32[]{:S(2)}, u32[]{:S(2)}) collective-permute-start(bf16[512,256]{1,0:T(8,128)(2,1)S(1)} %collective-permute-done.25.refs_2_), channel_id=1, source_target_pairs={{8,0},{16,8},{24,16},{28,24},{20,28},{12,20},{4,12},{0,4},{9,1},{1... | collective-permute-start | bytes 786440 | tf_op jit(solution)/shard_map/ppermute | solution.py:66
  42.0 3.3 %collective-permute-done.24.refs_1_ = bf16[512,256]{1,0:T(8,128)(2,1)S(1)} collective-permute-done((bf16[512,256]{1,0:T(8,128)(2,1)S(1)}, bf16[512,256]{1,0:T(8,128)(2,1)S(1)}, u32[]{:S(2)}, u32[]{:S(2)}) %collective-permute-start.24) | collective-permute-done | bytes 262176 | tf_op jit(solution)/shard_map/ppermute | solution.py:66
  45.3 0.8 collective-permute-start.11
  46.1 4.8 %collective-permute-done.4.refs_5_ = bf16[256,512]{1,0:T(8,128)(2,1)S(1)} collective-permute-done((bf16[256,512]{1,0:T(8,128)(2,1)S(1)}, bf16[256,512]{1,0:T(8,128)(2,1)S(1)}, u32[]{:S(2)}, u32[]{:S(2)}) %collective-permute-start.4) | collective-permute-done | bytes 262176 | tf_op jit(solution)/shard_map/ppermute | solution.py:66
  50.9 0.8 collective-permute-start.6
  51.8 1.2 collective-permute-start.13
  53.1 1.5 %collective-permute-start.20 = (bf16[256,512]{1,0:T(8,128)(2,1)S(1)}, bf16[256,512]{1,0:T(8,128)(2,1)S(1)}, u32[]{:S(2)}, u32[]{:S(2)}) collective-permute-start(bf16[256,512]{1,0:T(8,128)(2,1)S(1)} %collective-permute-done.18.refs_2_), channel_id=1, source_target_pairs={{8,0},{16,8},{24,16},{28,24},{20,28},{12,20},{4,12},{0,4},{9,1},{1... | collective-permute-start | bytes 786440 | tf_op jit(solution)/shard_map/ppermute | solution.py:66
  54.6 4.1 %collective-permute-done.27.refs_4_ = bf16[512,256]{1,0:T(8,128)(2,1)S(1)} collective-permute-done((bf16[512,256]{1,0:T(8,128)(2,1)S(1)}, bf16[512,256]{1,0:T(8,128)(2,1)S(1)}, u32[]{:S(2)}, u32[]{:S(2)}) %collective-permute-start.27) | collective-permute-done | bytes 262176 | tf_op jit(solution)/shard_map/ppermute | solution.py:66
  58.8 2.0 %collective-permute-start.21 = (bf16[256,512]{1,0:T(8,128)(2,1)S(1)}, bf16[256,512]{1,0:T(8,128)(2,1)S(1)}, u32[]{:S(2)}, u32[]{:S(2)}) collective-permute-start(bf16[256,512]{1,0:T(8,128)(2,1)S(1)} %collective-permute-done.19.refs_3_), channel_id=1, source_target_pairs={{0,8},{8,16},{16,24},{24,28},{28,20},{20,12},{12,4},{4,0},{1,9},{9... | collective-permute-start | bytes 786440 | tf_op jit(solution)/shard_map/ppermute | solution.py:66
  60.8 1.4 %collective-permute-done.6.refs_7_ = bf16[256,512]{1,0:T(8,128)(2,1)S(1)} collective-permute-done((bf16[256,512]{1,0:T(8,128)(2,1)S(1)}, bf16[256,512]{1,0:T(8,128)(2,1)S(1)}, u32[]{:S(2)}, u32[]{:S(2)}) %collective-permute-start.6) | collective-permute-done | bytes 262176 | tf_op jit(solution)/shard_map/ppermute | solution.py:66
  62.2 0.8 collective-permute-start.26
  63.7 0.7 collective-permute-done.13.refs_15_
  64.4 6.9 %shard_map.65 = (bf16[512,512]{1,0:T(8,128)(2,1)}, bf16[512,512]{1,0:T(8,128)(2,1)}, f32[4,128,128]{2,1,0:T(8,128)}, bf16[4,128,128]{2,1,0:T(8,128)(2,1)}) custom-call(s32[2,8]{1,0:T(2,128)} %stack.103.starts, bf16[512,2048]{1,0:T(8,128)(2,1)} %tokens.2, bf16[256,512]{1,0:T(8,128)(2,1)} %refs_0_.4, bf16[256,512]{1,0:T(8,128)(2,1)} %copy-done.18, ...), custom_call_target="tpu_custom_call" | custom-call | flops 1 | bytes 30933248 | tf_op jit(solution)/shard_map/pallas_call | solution.py:22
  71.4 1.8 %collective-permute-start.16 = (bf16[4,128,128]{2,1,0:T(8,128)(2,1)}, bf16[4,128,128]{2,1,0:T(8,128)(2,1)S(1)}, u32[]{:S(2)}, u32[]{:S(2)}) collective-permute-start(bf16[4,128,128]{2,1,0:T(8,128)(2,1)} %get-tuple-element.25), channel_id=1, source_target_pairs={{0,12},{4,8},{8,4},{12,0},{16,28},{20,24},{24,20},{28,16},{1,13},{... | collective-permute-start | bytes 393224 | tf_op jit(solution)/shard_map/ppermute | solution.py:384
  73.6 1.0 collective-permute-done.29.refs_6_
  74.9 1.7 %collective-permute-start.22 = (bf16[256,512]{1,0:T(8,128)(2,1)S(1)}, bf16[256,512]{1,0:T(8,128)(2,1)S(1)}, u32[]{:S(2)}, u32[]{:S(2)}) collective-permute-start(bf16[256,512]{1,0:T(8,128)(2,1)S(1)} %collective-permute-done.20.refs_4_), channel_id=1, source_target_pairs={{8,0},{16,8},{24,16},{28,24},{20,28},{12,20},{4,12},{0,4},{9,1},{1... | collective-permute-start | bytes 786440 | tf_op jit(solution)/shard_map/ppermute | solution.py:66
  77.0 2.0 %collective-permute-done.16.refs_10_ = bf16[4,128,128]{2,1,0:T(8,128)(2,1)S(1)} collective-permute-done((bf16[4,128,128]{2,1,0:T(8,128)(2,1)}, bf16[4,128,128]{2,1,0:T(8,128)(2,1)S(1)}, u32[]{:S(2)}, u32[]{:S(2)}) %collective-permute-start.16) | collective-permute-done | bytes 131104 | tf_op jit(solution)/shard_map/ppermute | solution.py:384
  79.0 1.6 %collective-permute-start.28 = (bf16[512,256]{1,0:T(8,128)(2,1)S(1)}, bf16[512,256]{1,0:T(8,128)(2,1)S(1)}, u32[]{:S(2)}, u32[]{:S(2)}) collective-permute-start(bf16[512,256]{1,0:T(8,128)(2,1)S(1)} %collective-permute-done.26.refs_3_), channel_id=1, source_target_pairs={{0,8},{8,16},{16,24},{24,28},{28,20},{20,12},{12,4},{4,0},{1,9},{9... | collective-permute-start | bytes 786440 | tf_op jit(solution)/shard_map/ppermute | solution.py:66
  81.0 1.3 %collective-permute-start.30 = (bf16[512,256]{1,0:T(8,128)(2,1)S(1)}, bf16[512,256]{1,0:T(8,128)(2,1)S(1)}, u32[]{:S(2)}, u32[]{:S(2)}) collective-permute-start(bf16[512,256]{1,0:T(8,128)(2,1)S(1)} %collective-permute-done.29.refs_6_), channel_id=1, source_target_pairs={{8,0},{16,8},{24,16},{28,24},{20,28},{12,20},{4,12},{0,4},{9,1},{1... | collective-permute-start | bytes 786440 | tf_op jit(solution)/shard_map/ppermute | solution.py:66
  82.3 1.1 convert_add_fusion
  83.4 1.8 %collective-permute-start.31 = (bf16[4,128,128]{2,1,0:T(8,128)(2,1)S(1)}, bf16[4,128,128]{2,1,0:T(8,128)(2,1)S(1)}, u32[]{:S(2)}, u32[]{:S(2)}) collective-permute-start(bf16[4,128,128]{2,1,0:T(8,128)(2,1)S(1)} %convert_add_fusion), channel_id=1, source_target_pairs={{0,16},{4,20},{8,24},{12,28},{16,0},{20,4},{24,8},{28,12},{1,17},{... | collective-permute-start | bytes 393224 | tf_op jit(solution)/shard_map/ppermute | solution.py:384
  86.4 1.6 %collective-permute-done.22.refs_6_ = bf16[256,512]{1,0:T(8,128)(2,1)S(1)} collective-permute-done((bf16[256,512]{1,0:T(8,128)(2,1)S(1)}, bf16[256,512]{1,0:T(8,128)(2,1)S(1)}, u32[]{:S(2)}, u32[]{:S(2)}) %collective-permute-start.22) | collective-permute-done | bytes 262176 | tf_op jit(solution)/shard_map/ppermute | solution.py:66
  88.9 7.2 %shard_map.66 = (bf16[512,512]{1,0:T(8,128)(2,1)}, f32[512,512]{1,0:T(8,128)}) custom-call(s32[2,8]{1,0:T(2,128)} %stack.103.starts, bf16[512,2048]{1,0:T(8,128)(2,1)} %tokens.2, bf16[512,512]{1,0:T(8,128)(2,1)} %get-tuple-element.27.keys, bf16[512,512]{1,0:T(8,128)(2,1)} %get-tuple-element.28.values, bf16[4,512,512]{2,1,0:T(8,128)(2,1)} %shard_map.64.mixing, ...), custom_call_target="tpu_custom_call" | custom-call | flops 1 | bytes 35651840 | tf_op jit(solution)/shard_map/pallas_call | solution.py:22
  96.9 6.6 %shard_map.67 = (bf16[512,512]{1,0:T(8,128)(2,1)}, bf16[512,512]{1,0:T(8,128)(2,1)}, bf16[512,512]{1,0:T(8,128)(2,1)}) custom-call(f32[3]{0:T(128)} %add_convert_fusion.2.upper, s32[2,8]{1,0:T(2,128)} %stack.88.starts, bf16[512,512]{1,0:T(8,128)(2,1)} %get-tuple-element.29.queries, f32[512,512]{1,0:T(8,128)} %get-tuple-element.30.local, ...), custom_call_target="tpu_custom_call" | custom-call | flops 1 | bytes 23494960 | tf_op jit(solution)/shard_map/pallas_call | solution.py:22
  103.6 2.1 %collective-permute-done.32 = bf16[512,512]{1,0:T(8,128)(2,1)S(1)} collective-permute-done((bf16[512,512]{1,0:T(8,128)(2,1)}, bf16[512,512]{1,0:T(8,128)(2,1)S(1)}, u32[]{:S(2)}, u32[]{:S(2)}) %collective-permute-start.32) | collective-permute-done | bytes 524320 | tf_op jit(solution)/shard_map/ppermute | solution.py:411
  105.7 1.2 add_convert_fusion.1
  106.9 1.6 %collective-permute-start.34 = (bf16[512,512]{1,0:T(8,128)(2,1)S(1)}, bf16[512,512]{1,0:T(8,128)(2,1)S(1)}, u32[]{:S(2)}, u32[]{:S(2)}) collective-permute-start(bf16[512,512]{1,0:T(8,128)(2,1)S(1)} %add_convert_fusion.1), channel_id=1, source_target_pairs={{0,2},{1,3},{2,0},{3,1},{4,6},{5,7},{6,4},{7,5},{8,10},{9,11},{10,... | collective-permute-start | bytes 1572872 | tf_op jit(solution)/shard_map/ppermute | solution.py:411
  108.5 3.8 %shard_map.68 = (bf16[512,512]{1,0:T(8,128)(2,1)}, bf16[512,512]{1,0:T(8,128)(2,1)}) custom-call(s32[2,8]{1,0:T(2,128)} %stack.88.starts, bf16[512,512]{1,0:T(8,128)(2,1)} %get-tuple-element.36.attended, bf16[512,256]{1,0:T(8,128)(2,1)} %refs_0_.7, bf16[512,256]{1,0:T(8,128)(2,1)} %copy-done.2, bf16[512,256]{1,0:T(8,128)(2,1)} %copy-done.1, ...), custom_call_target="tpu_custom_call" | custom-call | flops 1 | bytes 14680320 | tf_op jit(solution)/shard_map/pallas_call | solution.py:22
  112.4 8.5 %collective-permute-done.34 = bf16[512,512]{1,0:T(8,128)(2,1)S(1)} collective-permute-done((bf16[512,512]{1,0:T(8,128)(2,1)S(1)}, bf16[512,512]{1,0:T(8,128)(2,1)S(1)}, u32[]{:S(2)}, u32[]{:S(2)}) %collective-permute-start.34) | collective-permute-done | bytes 524320 | tf_op jit(solution)/shard_map/ppermute | solution.py:411
  120.9 2.0 %add_convert_fusion = bf16[512,512]{1,0:T(8,128)(2,1)} fusion(bf16[512,512]{1,0:T(8,128)(2,1)S(1)} %collective-permute-done.34, bf16[512,512]{1,0:T(8,128)(2,1)S(1)} %collective-permute-done.33, bf16[512,512]{1,0:T(8,128)(2,1)} %get-tuple-element.37), kind=kLoop, calls=%fused_computation | loop fusion | flops 1572864 | bytes 2097152 | tf_op jit(solution)/shard_map/convert_element_type | solution.py:430
  (100 shorter events, 6.3 us)
Async XLA Ops:
  0.0 36.0 %copy-start = (bf16[512,256]{1,0:T(8,128)(2,1)S(1)}, bf16[512,256]{1,0:T(8,128)(2,1)}, u32[]{:S(2)}) copy-start(bf16[512,256]{1,0:T(8,128)(2,1)} %refs_0_.7) | copy-start | bytes 786436
  0.0 10.3 %collective-permute-start = (bf16[256,512]{1,0:T(8,128)(2,1)}, bf16[256,512]{1,0:T(8,128)(2,1)S(1)}, u32[]{:S(2)}, u32[]{:S(2)}) collective-permute-start(bf16[256,512]{1,0:T(8,128)(2,1)} %refs_0_.4), channel_id=1, source_target_pairs={{0,8},{8,16},{16,24},{24,28},{28,20},{20,12},{12,4},{4,0},{1,9},{9... | collective-permute-start | bytes 786440 | tf_op jit(solution)/shard_map/ppermute | solution.py:66
  3.0 9.4 %collective-permute-start.1 = (bf16[256,512]{1,0:T(8,128)(2,1)}, bf16[256,512]{1,0:T(8,128)(2,1)S(1)}, u32[]{:S(2)}, u32[]{:S(2)}) collective-permute-start(bf16[256,512]{1,0:T(8,128)(2,1)} %refs_0_.4), channel_id=1, source_target_pairs={{8,0},{16,8},{24,16},{28,24},{20,28},{12,20},{4,12},{0,4},{9,1},{1... | collective-permute-start | bytes 786440 | tf_op jit(solution)/shard_map/ppermute | solution.py:66
  3.0 12.9 %collective-permute-start.7 = (bf16[256,512]{1,0:T(8,128)(2,1)}, bf16[256,512]{1,0:T(8,128)(2,1)S(1)}, u32[]{:S(2)}, u32[]{:S(2)}) collective-permute-start(bf16[256,512]{1,0:T(8,128)(2,1)} %refs_8_.1), channel_id=1, source_target_pairs={{0,8},{8,16},{16,24},{24,28},{28,20},{20,12},{12,4},{4,0},{1,9},{9... | collective-permute-start | bytes 786440 | tf_op jit(solution)/shard_map/ppermute | solution.py:66
  5.1 13.0 %collective-permute-start.8 = (bf16[256,512]{1,0:T(8,128)(2,1)}, bf16[256,512]{1,0:T(8,128)(2,1)S(1)}, u32[]{:S(2)}, u32[]{:S(2)}) collective-permute-start(bf16[256,512]{1,0:T(8,128)(2,1)} %refs_8_.1), channel_id=1, source_target_pairs={{8,0},{16,8},{24,16},{28,24},{20,28},{12,20},{4,12},{0,4},{9,1},{1... | collective-permute-start | bytes 786440 | tf_op jit(solution)/shard_map/ppermute | solution.py:66
  5.1 16.5 %collective-permute-start.17 = (bf16[256,512]{1,0:T(8,128)(2,1)}, bf16[256,512]{1,0:T(8,128)(2,1)S(1)}, u32[]{:S(2)}, u32[]{:S(2)}) collective-permute-start(bf16[256,512]{1,0:T(8,128)(2,1)} %refs_0_.5), channel_id=1, source_target_pairs={{0,8},{8,16},{16,24},{24,28},{28,20},{20,12},{12,4},{4,0},{1,9},{9... | collective-permute-start | bytes 786440 | tf_op jit(solution)/shard_map/ppermute | solution.py:66
  10.3 25.6 %copy-start.18 = (bf16[256,512]{1,0:T(8,128)(2,1)}, bf16[256,512]{1,0:T(8,128)(2,1)S(1)}, u32[]{:S(2)}) copy-start(bf16[256,512]{1,0:T(8,128)(2,1)S(1)} %collective-permute-done.refs_1_) | copy-start | bytes 786436
  10.3 13.4 %collective-permute-start.18 = (bf16[256,512]{1,0:T(8,128)(2,1)}, bf16[256,512]{1,0:T(8,128)(2,1)S(1)}, u32[]{:S(2)}, u32[]{:S(2)}) collective-permute-start(bf16[256,512]{1,0:T(8,128)(2,1)} %refs_0_.5), channel_id=1, source_target_pairs={{8,0},{16,8},{24,16},{28,24},{20,28},{12,20},{4,12},{0,4},{9,1},{1... | collective-permute-start | bytes 786440 | tf_op jit(solution)/shard_map/ppermute | solution.py:66
  12.5 23.5 %copy-start.19 = (bf16[256,512]{1,0:T(8,128)(2,1)}, bf16[256,512]{1,0:T(8,128)(2,1)S(1)}, u32[]{:S(2)}) copy-start(bf16[256,512]{1,0:T(8,128)(2,1)S(1)} %collective-permute-done.1.refs_2_) | copy-start | bytes 786436
  12.5 14.7 %collective-permute-start.2 = (bf16[256,512]{1,0:T(8,128)(2,1)S(1)}, bf16[256,512]{1,0:T(8,128)(2,1)S(1)}, u32[]{:S(2)}, u32[]{:S(2)}) collective-permute-start(bf16[256,512]{1,0:T(8,128)(2,1)S(1)} %collective-permute-done.refs_1_), channel_id=1, source_target_pairs={{0,8},{8,16},{16,24},{24,28},{28,20},{20,12},{12,4},{4,0},{1,9},{9... | collective-permute-start | bytes 786440 | tf_op jit(solution)/shard_map/ppermute | solution.py:66
  15.9 20.0 %copy-start.20 = (bf16[256,512]{1,0:T(8,128)(2,1)}, bf16[256,512]{1,0:T(8,128)(2,1)S(1)}, u32[]{:S(2)}) copy-start(bf16[256,512]{1,0:T(8,128)(2,1)S(1)} %collective-permute-done.7.refs_9_) | copy-start | bytes 786436
  15.9 20.0 %collective-permute-start.3 = (bf16[256,512]{1,0:T(8,128)(2,1)S(1)}, bf16[256,512]{1,0:T(8,128)(2,1)S(1)}, u32[]{:S(2)}, u32[]{:S(2)}) collective-permute-start(bf16[256,512]{1,0:T(8,128)(2,1)S(1)} %collective-permute-done.1.refs_2_), channel_id=1, source_target_pairs={{8,0},{16,8},{24,16},{28,24},{20,28},{12,20},{4,12},{0,4},{9,1},{1... | collective-permute-start | bytes 786440 | tf_op jit(solution)/shard_map/ppermute | solution.py:66
  18.1 18.1 %collective-permute-start.9 = (bf16[256,512]{1,0:T(8,128)(2,1)S(1)}, bf16[256,512]{1,0:T(8,128)(2,1)S(1)}, u32[]{:S(2)}, u32[]{:S(2)}) collective-permute-start(bf16[256,512]{1,0:T(8,128)(2,1)S(1)} %collective-permute-done.7.refs_9_), channel_id=1, source_target_pairs={{0,8},{8,16},{16,24},{24,28},{28,20},{20,12},{12,4},{4,0},{1,9},{9... | collective-permute-start | bytes 786440 | tf_op jit(solution)/shard_map/ppermute | solution.py:66
  21.5 16.7 %collective-permute-start.10 = (bf16[256,512]{1,0:T(8,128)(2,1)S(1)}, bf16[256,512]{1,0:T(8,128)(2,1)S(1)}, u32[]{:S(2)}, u32[]{:S(2)}) collective-permute-start(bf16[256,512]{1,0:T(8,128)(2,1)S(1)} %collective-permute-done.8.refs_10_), channel_id=1, source_target_pairs={{8,0},{16,8},{24,16},{28,24},{20,28},{12,20},{4,12},{0,4},{9,1},{1... | collective-permute-start | bytes 786440 | tf_op jit(solution)/shard_map/ppermute | solution.py:66
  23.7 29.4 %copy-start.12 = (bf16[256,512]{1,0:T(8,128)(2,1)}, bf16[256,512]{1,0:T(8,128)(2,1)S(1)}, u32[]{:S(2)}) copy-start(bf16[256,512]{1,0:T(8,128)(2,1)S(1)} %collective-permute-done.18.refs_2_) | copy-start | bytes 786436
  23.7 14.7 %collective-permute-start.19 = (bf16[256,512]{1,0:T(8,128)(2,1)S(1)}, bf16[256,512]{1,0:T(8,128)(2,1)S(1)}, u32[]{:S(2)}, u32[]{:S(2)}) collective-permute-start(bf16[256,512]{1,0:T(8,128)(2,1)S(1)} %collective-permute-done.17.refs_1_), channel_id=1, source_target_pairs={{0,8},{8,16},{16,24},{24,28},{28,20},{20,12},{12,4},{4,0},{1,9},{9... | collective-permute-start | bytes 786440 | tf_op jit(solution)/shard_map/ppermute | solution.py:66
  27.2 13.3 %collective-permute-start.25 = (bf16[512,256]{1,0:T(8,128)(2,1)}, bf16[512,256]{1,0:T(8,128)(2,1)S(1)}, u32[]{:S(2)}, u32[]{:S(2)}) collective-permute-start(bf16[512,256]{1,0:T(8,128)(2,1)} %refs_0_.7), channel_id=1, source_target_pairs={{8,0},{16,8},{24,16},{28,24},{20,28},{12,20},{4,12},{0,4},{9,1},{1... | collective-permute-start | bytes 786440 | tf_op jit(solution)/shard_map/ppermute | solution.py:66
  36.0 22.8 %copy-start.23 = (bf16[256,512]{1,0:T(8,128)(2,1)}, bf16[256,512]{1,0:T(8,128)(2,1)S(1)}, u32[]{:S(2)}) copy-start(bf16[256,512]{1,0:T(8,128)(2,1)S(1)} %collective-permute-done.3.refs_4_) | copy-start | bytes 786436
  36.0 9.3 %collective-permute-start.24 = (bf16[512,256]{1,0:T(8,128)(2,1)S(1)}, bf16[512,256]{1,0:T(8,128)(2,1)S(1)}, u32[]{:S(2)}, u32[]{:S(2)}) collective-permute-start(bf16[512,256]{1,0:T(8,128)(2,1)S(1)} %copy-done), channel_id=1, source_target_pairs={{0,8},{8,16},{16,24},{24,28},{28,20},{20,12},{12,4},{4,0},{1,9},{9... | collective-permute-start | bytes 786440 | tf_op jit(solution)/shard_map/ppermute | solution.py:66
  36.2 28.2 %copy-start.24 = (bf16[256,512]{1,0:T(8,128)(2,1)}, bf16[256,512]{1,0:T(8,128)(2,1)S(1)}, u32[]{:S(2)}) copy-start(bf16[256,512]{1,0:T(8,128)(2,1)S(1)} %collective-permute-done.9.refs_11_) | copy-start | bytes 786436
  36.2 14.7 %collective-permute-start.4 = (bf16[256,512]{1,0:T(8,128)(2,1)S(1)}, bf16[256,512]{1,0:T(8,128)(2,1)S(1)}, u32[]{:S(2)}, u32[]{:S(2)}) collective-permute-start(bf16[256,512]{1,0:T(8,128)(2,1)S(1)} %collective-permute-done.2.refs_3_), channel_id=1, source_target_pairs={{0,8},{8,16},{16,24},{24,28},{28,20},{20,12},{12,4},{4,0},{1,9},{9... | collective-permute-start | bytes 786440 | tf_op jit(solution)/shard_map/ppermute | solution.py:66
  38.2 26.2 %copy-start.25 = (bf16[256,512]{1,0:T(8,128)(2,1)}, bf16[256,512]{1,0:T(8,128)(2,1)S(1)}, u32[]{:S(2)}) copy-start(bf16[256,512]{1,0:T(8,128)(2,1)S(1)} %collective-permute-done.10.refs_12_) | copy-start | bytes 786436
  38.2 13.6 %collective-permute-start.12 = (bf16[256,512]{1,0:T(8,128)(2,1)S(1)}, bf16[256,512]{1,0:T(8,128)(2,1)S(1)}, u32[]{:S(2)}, u32[]{:S(2)}) collective-permute-start(bf16[256,512]{1,0:T(8,128)(2,1)S(1)} %collective-permute-done.10.refs_12_), channel_id=1, source_target_pairs={{8,0},{16,8},{24,16},{28,24},{20,28},{12,20},{4,12},{0,4},{9,1},{1... | collective-permute-start | bytes 786440 | tf_op jit(solution)/shard_map/ppermute | solution.py:66
  38.4 32.9 %copy-start.13 = (bf16[256,512]{1,0:T(8,128)(2,1)}, bf16[256,512]{1,0:T(8,128)(2,1)S(1)}, u32[]{:S(2)}) copy-start(bf16[256,512]{1,0:T(8,128)(2,1)S(1)} %collective-permute-done.19.refs_3_) | copy-start | bytes 786436
  38.4 14.7 %collective-permute-start.5 = (bf16[256,512]{1,0:T(8,128)(2,1)S(1)}, bf16[256,512]{1,0:T(8,128)(2,1)S(1)}, u32[]{:S(2)}, u32[]{:S(2)}) collective-permute-start(bf16[256,512]{1,0:T(8,128)(2,1)S(1)} %collective-permute-done.3.refs_4_), channel_id=1, source_target_pairs={{8,0},{16,8},{24,16},{28,24},{20,28},{12,20},{4,12},{0,4},{9,1},{1... | collective-permute-start | bytes 786440 | tf_op jit(solution)/shard_map/ppermute | solution.py:66
  40.5 30.9 %copy-start.1 = (bf16[512,256]{1,0:T(8,128)(2,1)}, bf16[512,256]{1,0:T(8,128)(2,1)S(1)}, u32[]{:S(2)}) copy-start(bf16[512,256]{1,0:T(8,128)(2,1)S(1)} %collective-permute-done.25.refs_2_) | copy-start | bytes 786436
  40.5 18.2 %collective-permute-start.27 = (bf16[512,256]{1,0:T(8,128)(2,1)S(1)}, bf16[512,256]{1,0:T(8,128)(2,1)S(1)}, u32[]{:S(2)}, u32[]{:S(2)}) collective-permute-start(bf16[512,256]{1,0:T(8,128)(2,1)S(1)} %collective-permute-done.25.refs_2_), channel_id=1, source_target_pairs={{8,0},{16,8},{24,16},{28,24},{20,28},{12,20},{4,12},{0,4},{9,1},{1... | collective-permute-start | bytes 786440 | tf_op jit(solution)/shard_map/ppermute | solution.py:66
  45.3 26.0 %copy-start.2 = (bf16[512,256]{1,0:T(8,128)(2,1)}, bf16[512,256]{1,0:T(8,128)(2,1)S(1)}, u32[]{:S(2)}) copy-start(bf16[512,256]{1,0:T(8,128)(2,1)S(1)} %collective-permute-done.24.refs_1_) | copy-start | bytes 786436
  45.3 13.5 %collective-permute-start.11 = (bf16[256,512]{1,0:T(8,128)(2,1)S(1)}, bf16[256,512]{1,0:T(8,128)(2,1)S(1)}, u32[]{:S(2)}, u32[]{:S(2)}) collective-permute-start(bf16[256,512]{1,0:T(8,128)(2,1)S(1)} %collective-permute-done.9.refs_11_), channel_id=1, source_target_pairs={{0,8},{8,16},{16,24},{24,28},{28,20},{20,12},{12,4},{4,0},{1,9},{9... | collective-permute-start | bytes 786440 | tf_op jit(solution)/shard_map/ppermute | solution.py:66
  50.9 11.2 %collective-permute-start.6 = (bf16[256,512]{1,0:T(8,128)(2,1)S(1)}, bf16[256,512]{1,0:T(8,128)(2,1)S(1)}, u32[]{:S(2)}, u32[]{:S(2)}) collective-permute-start(bf16[256,512]{1,0:T(8,128)(2,1)S(1)} %collective-permute-done.4.refs_5_), channel_id=1, source_target_pairs={{0,8},{8,16},{16,24},{24,28},{28,20},{20,12},{12,4},{4,0},{1,9},{9... | collective-permute-start | bytes 786440 | tf_op jit(solution)/shard_map/ppermute | solution.py:66
  51.8 12.6 %collective-permute-start.13 = (bf16[256,512]{1,0:T(8,128)(2,1)S(1)}, bf16[256,512]{1,0:T(8,128)(2,1)}, u32[]{:S(2)}, u32[]{:S(2)}) collective-permute-start(bf16[256,512]{1,0:T(8,128)(2,1)S(1)} %collective-permute-done.12.refs_14_), channel_id=1, source_target_pairs={{8,0},{16,8},{24,16},{28,24},{20,28},{12,20},{4,12},{0,4},{9,1},{1... | collective-permute-start | bytes 786440 | tf_op jit(solution)/shard_map/ppermute | solution.py:66
  53.1 20.1 %collective-permute-start.20 = (bf16[256,512]{1,0:T(8,128)(2,1)S(1)}, bf16[256,512]{1,0:T(8,128)(2,1)S(1)}, u32[]{:S(2)}, u32[]{:S(2)}) collective-permute-start(bf16[256,512]{1,0:T(8,128)(2,1)S(1)} %collective-permute-done.18.refs_2_), channel_id=1, source_target_pairs={{8,0},{16,8},{24,16},{28,24},{20,28},{12,20},{4,12},{0,4},{9,1},{1... | collective-permute-start | bytes 786440 | tf_op jit(solution)/shard_map/ppermute | solution.py:66
  58.7 15.9 %collective-permute-start.29 = (bf16[512,256]{1,0:T(8,128)(2,1)S(1)}, bf16[512,256]{1,0:T(8,128)(2,1)S(1)}, u32[]{:S(2)}, u32[]{:S(2)}) collective-permute-start(bf16[512,256]{1,0:T(8,128)(2,1)S(1)} %collective-permute-done.27.refs_4_), channel_id=1, source_target_pairs={{8,0},{16,8},{24,16},{28,24},{20,28},{12,20},{4,12},{0,4},{9,1},{1... | collective-permute-start | bytes 786440 | tf_op jit(solution)/shard_map/ppermute | solution.py:66
  58.8 16.1 %collective-permute-start.21 = (bf16[256,512]{1,0:T(8,128)(2,1)S(1)}, bf16[256,512]{1,0:T(8,128)(2,1)S(1)}, u32[]{:S(2)}, u32[]{:S(2)}) collective-permute-start(bf16[256,512]{1,0:T(8,128)(2,1)S(1)} %collective-permute-done.19.refs_3_), channel_id=1, source_target_pairs={{0,8},{8,16},{16,24},{24,28},{28,20},{20,12},{12,4},{4,0},{1,9},{9... | collective-permute-start | bytes 786440 | tf_op jit(solution)/shard_map/ppermute | solution.py:66
  62.2 14.4 %collective-permute-start.26 = (bf16[512,256]{1,0:T(8,128)(2,1)S(1)}, bf16[512,256]{1,0:T(8,128)(2,1)S(1)}, u32[]{:S(2)}, u32[]{:S(2)}) collective-permute-start(bf16[512,256]{1,0:T(8,128)(2,1)S(1)} %collective-permute-done.24.refs_1_), channel_id=1, source_target_pairs={{0,8},{8,16},{16,24},{24,28},{28,20},{20,12},{12,4},{4,0},{1,9},{9... | collective-permute-start | bytes 786440 | tf_op jit(solution)/shard_map/ppermute | solution.py:66
  71.4 7.6 %collective-permute-start.16 = (bf16[4,128,128]{2,1,0:T(8,128)(2,1)}, bf16[4,128,128]{2,1,0:T(8,128)(2,1)S(1)}, u32[]{:S(2)}, u32[]{:S(2)}) collective-permute-start(bf16[4,128,128]{2,1,0:T(8,128)(2,1)} %get-tuple-element.25), channel_id=1, source_target_pairs={{0,12},{4,8},{8,4},{12,0},{16,28},{20,24},{24,20},{28,16},{1,13},{... | collective-permute-start | bytes 393224 | tf_op jit(solution)/shard_map/ppermute | solution.py:384
  73.1 7.9 %collective-permute-start.15 = (bf16[4,128,128]{2,1,0:T(8,128)(2,1)}, bf16[4,128,128]{2,1,0:T(8,128)(2,1)S(1)}, u32[]{:S(2)}, u32[]{:S(2)}) collective-permute-start(bf16[4,128,128]{2,1,0:T(8,128)(2,1)} %get-tuple-element.25), channel_id=1, source_target_pairs={{0,8},{4,12},{8,0},{12,4},{16,24},{20,28},{24,16},{28,20},{1,9},{5... | collective-permute-start | bytes 393224 | tf_op jit(solution)/shard_map/ppermute | solution.py:384
  74.5 21.5 %copy-start.4 = (bf16[512,256]{1,0:T(8,128)(2,1)}, bf16[512,256]{1,0:T(8,128)(2,1)S(1)}, u32[]{:S(2)}) copy-start(bf16[512,256]{1,0:T(8,128)(2,1)S(1)} %collective-permute-done.29.refs_6_) | copy-start | bytes 786436
  74.6 7.8 %collective-permute-start.14 = (bf16[4,128,128]{2,1,0:T(8,128)(2,1)}, bf16[4,128,128]{2,1,0:T(8,128)(2,1)S(1)}, u32[]{:S(2)}, u32[]{:S(2)}) collective-permute-start(bf16[4,128,128]{2,1,0:T(8,128)(2,1)} %get-tuple-element.25), channel_id=1, source_target_pairs={{0,4},{4,0},{8,12},{12,8},{16,20},{20,16},{24,28},{28,24},{1,5},{5... | collective-permute-start | bytes 393224 | tf_op jit(solution)/shard_map/ppermute | solution.py:384
  74.9 13.1 %collective-permute-start.22 = (bf16[256,512]{1,0:T(8,128)(2,1)S(1)}, bf16[256,512]{1,0:T(8,128)(2,1)S(1)}, u32[]{:S(2)}, u32[]{:S(2)}) collective-permute-start(bf16[256,512]{1,0:T(8,128)(2,1)S(1)} %collective-permute-done.20.refs_4_), channel_id=1, source_target_pairs={{8,0},{16,8},{24,16},{28,24},{20,28},{12,20},{4,12},{0,4},{9,1},{1... | collective-permute-start | bytes 786440 | tf_op jit(solution)/shard_map/ppermute | solution.py:66
  76.6 19.5 %copy-start.5 = (bf16[512,256]{1,0:T(8,128)(2,1)}, bf16[512,256]{1,0:T(8,128)(2,1)S(1)}, u32[]{:S(2)}) copy-start(bf16[512,256]{1,0:T(8,128)(2,1)S(1)} %collective-permute-done.26.refs_3_) | copy-start | bytes 786436
  76.6 11.4 %collective-permute-start.23 = (bf16[256,512]{1,0:T(8,128)(2,1)S(1)}, bf16[256,512]{1,0:T(8,128)(2,1)S(1)}, u32[]{:S(2)}, u32[]{:S(2)}) collective-permute-start(bf16[256,512]{1,0:T(8,128)(2,1)S(1)} %collective-permute-done.21.refs_5_), channel_id=1, source_target_pairs={{0,8},{8,16},{16,24},{24,28},{28,20},{20,12},{12,4},{4,0},{1,9},{9... | collective-permute-start | bytes 786440 | tf_op jit(solution)/shard_map/ppermute | solution.py:66
  79.0 17.1 %collective-permute-start.28 = (bf16[512,256]{1,0:T(8,128)(2,1)S(1)}, bf16[512,256]{1,0:T(8,128)(2,1)S(1)}, u32[]{:S(2)}, u32[]{:S(2)}) collective-permute-start(bf16[512,256]{1,0:T(8,128)(2,1)S(1)} %collective-permute-done.26.refs_3_), channel_id=1, source_target_pairs={{0,8},{8,16},{16,24},{24,28},{28,20},{20,12},{12,4},{4,0},{1,9},{9... | collective-permute-start | bytes 786440 | tf_op jit(solution)/shard_map/ppermute | solution.py:66
  81.0 15.1 %collective-permute-start.30 = (bf16[512,256]{1,0:T(8,128)(2,1)S(1)}, bf16[512,256]{1,0:T(8,128)(2,1)S(1)}, u32[]{:S(2)}, u32[]{:S(2)}) collective-permute-start(bf16[512,256]{1,0:T(8,128)(2,1)S(1)} %collective-permute-done.29.refs_6_), channel_id=1, source_target_pairs={{8,0},{16,8},{24,16},{28,24},{20,28},{12,20},{4,12},{0,4},{9,1},{1... | collective-permute-start | bytes 786440 | tf_op jit(solution)/shard_map/ppermute | solution.py:66
  83.4 12.7 %collective-permute-start.31 = (bf16[4,128,128]{2,1,0:T(8,128)(2,1)S(1)}, bf16[4,128,128]{2,1,0:T(8,128)(2,1)S(1)}, u32[]{:S(2)}, u32[]{:S(2)}) collective-permute-start(bf16[4,128,128]{2,1,0:T(8,128)(2,1)S(1)} %convert_add_fusion), channel_id=1, source_target_pairs={{0,16},{4,20},{8,24},{12,28},{16,0},{20,4},{24,8},{28,12},{1,17},{... | collective-permute-start | bytes 393224 | tf_op jit(solution)/shard_map/ppermute | solution.py:384
  103.5 2.2 %collective-permute-start.32 = (bf16[512,512]{1,0:T(8,128)(2,1)}, bf16[512,512]{1,0:T(8,128)(2,1)S(1)}, u32[]{:S(2)}, u32[]{:S(2)}) collective-permute-start(bf16[512,512]{1,0:T(8,128)(2,1)} %get-tuple-element.35), channel_id=1, source_target_pairs={{0,1},{1,0},{2,3},{3,2},{4,5},{5,4},{6,7},{7,6},{8,9},{9,8},{10,11... | collective-permute-start | bytes 1572872 | tf_op jit(solution)/shard_map/ppermute | solution.py:411
  106.9 14.0 %collective-permute-start.34 = (bf16[512,512]{1,0:T(8,128)(2,1)S(1)}, bf16[512,512]{1,0:T(8,128)(2,1)S(1)}, u32[]{:S(2)}, u32[]{:S(2)}) collective-permute-start(bf16[512,512]{1,0:T(8,128)(2,1)S(1)} %add_convert_fusion.1), channel_id=1, source_target_pairs={{0,2},{1,3},{2,0},{3,1},{4,6},{5,7},{6,4},{7,5},{8,10},{9,11},{10,... | collective-permute-start | bytes 1572872 | tf_op jit(solution)/shard_map/ppermute | solution.py:411
  112.4 8.6 %collective-permute-start.33 = (bf16[512,512]{1,0:T(8,128)(2,1)}, bf16[512,512]{1,0:T(8,128)(2,1)S(1)}, u32[]{:S(2)}, u32[]{:S(2)}) collective-permute-start(bf16[512,512]{1,0:T(8,128)(2,1)} %get-tuple-element.38), channel_id=1, source_target_pairs={{0,1},{1,0},{2,3},{3,2},{4,5},{5,4},{6,7},{7,6},{8,9},{9,8},{10,11... | collective-permute-start | bytes 1572872 | tf_op jit(solution)/shard_map/ppermute | solution.py:411
  (19 other events, 169.8 us)

commit v4 on v3

--- a/solution.py
+++ b/solution.py
@@ -44,15 +44,22 @@
     return jnp.where(position < n // 2, 2 * position, 2 * (n - 1 - position) + 1)
 
 
+def piece_owners(n):
+    here = ring_position(lax.axis_index("seq"), n)
+    owners = [lax.axis_index("seq")]
+    for step in range(1, n // 2):
+        owners += [ring_owner(here - step, n), ring_owner(here + step, n)]
+    return owners + [ring_owner(here + n // 2, n)]
+
+
 class Ring:
     def __init__(self, piece, n, opposite):
         order = ring_order(n)
         self.n, self.opposite, self.step = n, opposite, 0
         self.onward = [(order[i], order[(i + 1) % n]) for i in range(n)]
         self.back = [(b, a) for a, b in self.onward]
-        self.here = ring_position(lax.axis_index("seq"), n)
         self.ways = [piece, piece]
-        self.pieces = [(piece, lax.axis_index("seq"))]
+        self.pieces = [piece]
         self.gate = ()
 
     def advance(self, *gate):
@@ -64,8 +71,7 @@
                 continue
             piece = self.ways[way]
             self.ways[way] = lax.ppermute(after(piece, gate), "seq", pairs)
-            owner = ring_owner(self.here + (self.step if way else -self.step), self.n)
-            self.pieces.append((self.ways[way], owner))
+            self.pieces.append(self.ways[way])
 
 
 def after(array, others):
@@ -359,18 +365,25 @@
     upper = jnp.stack([here >> bit & 1 for bit in range(bits)]).astype(F32)
     weights_by_token = level_weights.transpose(0, 2, 1)
     if ringed:
+        owners = piece_owners(n)
         key, value, query, out = [
             Ring(w, n, i % 2) for i, w in enumerate((w_key, w_value, w_query, w_out))
         ]
+        starts = table([(owner * depth, 0) for owner in owners])
+        out_starts = table(
+            [(0, ((g // share ^ group) * share + g % share) * width) for g in owners]
+        )
         mixing = mixing_matrix(weights_by_token, local_bits)
+        mixing, starts, out_starts, upper = lax.optimization_barrier(
+            (mixing, starts, out_starts, upper)
+        )
         for step in range(1, n // 2 + 1):
-            key.advance(*((mixing,) if step == 3 else ()))
+            key.advance(*((mixing,) if step == 2 else ()))
             value.advance()
             query.advance()
             if step > 1:
                 out.advance(*(key.gate if step == 2 else ()))
-        pieces = [[a for a, _ in ring.pieces] for ring in (key, value, query)]
-        starts = table([(owner * depth, 0) for _, owner in key.pieces])
+        pieces = [ring.pieces for ring in (key, value, query)]
     else:
         mixing = mixing_matrix(weights_by_token, local_bits)
         pieces = [
@@ -392,18 +405,14 @@
     queries, local = attend_locally(tokens, starts, query_pieces, keys, values, mixing)
     if ringed:
         out.advance(rounded)
-        out_pieces = [a for a, _ in out.pieces]
-        out_starts = [
-            (0, ((owner // share ^ group) * share + owner % share) * width)
-            for _, owner in out.pieces
-        ]
+        out_pieces = out.pieces
     else:
         whole = lax.all_gather(w_out, "seq", axis=1, tiled=True)
         width *= share
         out_pieces = [
             lax.dynamic_slice_in_dim(whole, (group ^ k) * width, width, 1) for k in range(groups)
         ]
-        out_starts = [(0, k * width) for k in range(groups)]
+        out_starts = table([(0, k * width) for k in range(groups)])
 
     far = groups.bit_length() - 2
 
@@ -419,13 +428,12 @@
         (total,) = shares.values()
         return total
 
-    starts = table(out_starts)
     attended, *shares = finish(
-        queries, local, weights_by_token, upper, terms, starts, out_pieces, groups
+        queries, local, weights_by_token, upper, terms, out_starts, out_pieces, groups
     )
     away = sum_near({groups // 2 + k: a for k, a in enumerate(shares)}, BF16)
     theirs = from_group(away, far)
-    shares = output(after(attended, [away]), starts, out_pieces, groups)
+    shares = output(after(attended, [away]), out_starts, out_pieces, groups)
     ours = sum_near(dict(enumerate(shares)), F32)
     return (ours.astype(F32) + theirs.astype(F32)).astype(BF16)
 

time: 123 us -> 124 us (level)
    unnamed x65 -> x69, local copies, waits for them, and re-layouts: 3.96 us -> 4.66 us
  transfers between devices with their start and end apart: 35 -> 35, of which waited for: 20 -> 19; matrix products, arithmetic and copies ran while one was open for 4% -> 4% of each run, Pallas kernels for 18% -> 18%
where the time goes in v4:
time: 124 us; the launch traced here: 123 us
  starting transfers between devices  43.5 us (35%)
  waiting for transfers between devices  39.5 us (32%)
  Pallas kernels  29 us (23%)
  local copies, waits for them, and re-layouts  5.94 us (5%)
  other arithmetic  4.89 us (4%)
    ppermute x28, starting transfers between devices, advance(): self.ways[way] = lax.ppermute(after(piece, gate), 'seq', pairs)  37.4 us
    pallas_call x5, Pallas kernels, call(): pl.pallas_call(kernel, out_shape=outs, scratch_shapes=list(scratch), comp...  29 us
    ppermute x28, waiting for transfers between devices, advance(): self.ways[way] = lax.ppermute(after(piece, gate), 'seq', pairs)  27.2 us
    ppermute x3, waiting for transfers between devices, from_group(): lax.ppermute(array, 'head', [(g, g ^ 1 << bit) for g in range(groups)])  10.4 us
    unnamed x69, local copies, waits for them, and re-layouts  4.66 us
    ppermute x4, starting transfers between devices, from_partner(): return lax.ppermute(array, 'seq', [(i, i ^ apart) for i in range(n)])  4.07 us
  transfers between devices with their start and end apart: 35, of which 19 were waited for; matrix products, arithmetic and copies ran while one was open for 4% of the time, Pallas kernels for 18%

profile of v4, /device:TPU:0, one launch (start us, length us, event | category | flops | bytes accessed | tf_op | source)
XLA Modules:
  0.0 123.2 jit_solution(18407874141303614055)
XLA Ops:
  0.0 3.0 %collective-permute-start = (bf16[256,512]{1,0:T(8,128)(2,1)}, bf16[256,512]{1,0:T(8,128)(2,1)S(1)}, u32[]{:S(2)}, u32[]{:S(2)}) collective-permute-start(bf16[256,512]{1,0:T(8,128)(2,1)} %refs_0_.4), channel_id=1, source_target_pairs={{0,8},{8,16},{16,24},{24,28},{28,20},{20,12},{12,4},{4,0},{1,9},{9... | collective-permute-start | bytes 786440 | tf_op jit(solution)/shard_map/ppermute | solution.py:73
  3.0 2.0 %collective-permute-start.7 = (bf16[256,512]{1,0:T(8,128)(2,1)}, bf16[256,512]{1,0:T(8,128)(2,1)S(1)}, u32[]{:S(2)}, u32[]{:S(2)}) collective-permute-start(bf16[256,512]{1,0:T(8,128)(2,1)} %refs_8_.1), channel_id=1, source_target_pairs={{0,8},{8,16},{16,24},{24,28},{28,20},{20,12},{12,4},{4,0},{1,9},{9... | collective-permute-start | bytes 786440 | tf_op jit(solution)/shard_map/ppermute | solution.py:73
  5.1 2.0 %collective-permute-start.17 = (bf16[256,512]{1,0:T(8,128)(2,1)}, bf16[256,512]{1,0:T(8,128)(2,1)S(1)}, u32[]{:S(2)}, u32[]{:S(2)}) collective-permute-start(bf16[256,512]{1,0:T(8,128)(2,1)} %refs_0_.5), channel_id=1, source_target_pairs={{0,8},{8,16},{16,24},{24,28},{28,20},{20,12},{12,4},{4,0},{1,9},{9... | collective-permute-start | bytes 786440 | tf_op jit(solution)/shard_map/ppermute | solution.py:73
  7.1 2.2 %copy.7 = f32[4,13,512]{1,2,0:T(8,128)} copy(f32[4,13,512]{2,0,1:T(4,128)} %param.11) | data formatting | bytes 212992 | tf_op args[5]
  9.3 4.5 %shard_map.64.mixing = bf16[4,512,512]{2,1,0:T(8,128)(2,1)} custom-call(f32[4,512,13]{2,1,0:T(8,128)} %bitcast.22), custom_call_target="tpu_custom_call" | custom-call | flops 1 | bytes 8814592 | tf_op jit(solution)/shard_map/pallas_call | solution.py:22
  15.8 2.0 %collective-permute-start.2 = (bf16[256,512]{1,0:T(8,128)(2,1)S(1)}, bf16[256,512]{1,0:T(8,128)(2,1)S(1)}, u32[]{:S(2)}, u32[]{:S(2)}) collective-permute-start(bf16[256,512]{1,0:T(8,128)(2,1)S(1)} %collective-permute-done.refs_1_), channel_id=1, source_target_pairs={{0,8},{8,16},{16,24},{24,28},{28,20},{20,12},{12,4},{4,0},{1,9},{9... | collective-permute-start | bytes 786440 | tf_op jit(solution)/shard_map/ppermute | solution.py:73
  18.0 1.9 %collective-permute-start.9 = (bf16[256,512]{1,0:T(8,128)(2,1)S(1)}, bf16[256,512]{1,0:T(8,128)(2,1)S(1)}, u32[]{:S(2)}, u32[]{:S(2)}) collective-permute-start(bf16[256,512]{1,0:T(8,128)(2,1)S(1)} %collective-permute-done.7.refs_9_), channel_id=1, source_target_pairs={{0,8},{8,16},{16,24},{24,28},{28,20},{20,12},{12,4},{4,0},{1,9},{9... | collective-permute-start | bytes 786440 | tf_op jit(solution)/shard_map/ppermute | solution.py:73
  19.9 1.7 %collective-permute-done.17.refs_1_ = bf16[256,512]{1,0:T(8,128)(2,1)S(1)} collective-permute-done((bf16[256,512]{1,0:T(8,128)(2,1)}, bf16[256,512]{1,0:T(8,128)(2,1)S(1)}, u32[]{:S(2)}, u32[]{:S(2)}) %collective-permute-start.17) | collective-permute-done | bytes 262176 | tf_op jit(solution)/shard_map/ppermute | solution.py:73
  21.5 2.1 %collective-permute-start.10 = (bf16[256,512]{1,0:T(8,128)(2,1)S(1)}, bf16[256,512]{1,0:T(8,128)(2,1)S(1)}, u32[]{:S(2)}, u32[]{:S(2)}) collective-permute-start(bf16[256,512]{1,0:T(8,128)(2,1)S(1)} %collective-permute-done.8.refs_10_), channel_id=1, source_target_pairs={{8,0},{16,8},{24,16},{28,24},{20,28},{12,20},{4,12},{0,4},{9,1},{1... | collective-permute-start | bytes 786440 | tf_op jit(solution)/shard_map/ppermute | solution.py:73
  23.6 1.4 %collective-permute-done.18.refs_2_ = bf16[256,512]{1,0:T(8,128)(2,1)S(1)} collective-permute-done((bf16[256,512]{1,0:T(8,128)(2,1)S(1)}, bf16[256,512]{1,0:T(8,128)(2,1)S(1)}, u32[]{:S(2)}, u32[]{:S(2)}) %collective-permute-start.18) | collective-permute-done | bytes 262176 | tf_op jit(solution)/shard_map/ppermute | solution.py:73
  25.1 1.6 %collective-permute-start.19 = (bf16[256,512]{1,0:T(8,128)(2,1)S(1)}, bf16[256,512]{1,0:T(8,128)(2,1)S(1)}, u32[]{:S(2)}, u32[]{:S(2)}) collective-permute-start(bf16[256,512]{1,0:T(8,128)(2,1)S(1)} %collective-permute-done.17.refs_1_), channel_id=1, source_target_pairs={{0,8},{8,16},{16,24},{24,28},{28,20},{20,12},{12,4},{4,0},{1,9},{9... | collective-permute-start | bytes 786440 | tf_op jit(solution)/shard_map/ppermute | solution.py:73
  27.2 2.1 %collective-permute-start.25 = (bf16[512,256]{1,0:T(8,128)(2,1)S(1)}, bf16[512,256]{1,0:T(8,128)(2,1)S(1)}, u32[]{:S(2)}, u32[]{:S(2)}) collective-permute-start(bf16[512,256]{1,0:T(8,128)(2,1)S(1)} %copy-done), channel_id=1, source_target_pairs={{8,0},{16,8},{24,16},{28,24},{20,28},{12,20},{4,12},{0,4},{9,1},{1... | collective-permute-start | bytes 786440 | tf_op jit(solution)/shard_map/ppermute | solution.py:73
  29.2 1.4 %collective-permute-done.3.refs_4_ = bf16[256,512]{1,0:T(8,128)(2,1)S(1)} collective-permute-done((bf16[256,512]{1,0:T(8,128)(2,1)S(1)}, bf16[256,512]{1,0:T(8,128)(2,1)S(1)}, u32[]{:S(2)}, u32[]{:S(2)}) %collective-permute-start.3) | collective-permute-done | bytes 262176 | tf_op jit(solution)/shard_map/ppermute | solution.py:73
  30.7 1.6 %collective-permute-start.24 = (bf16[512,256]{1,0:T(8,128)(2,1)S(1)}, bf16[512,256]{1,0:T(8,128)(2,1)S(1)}, u32[]{:S(2)}, u32[]{:S(2)}) collective-permute-start(bf16[512,256]{1,0:T(8,128)(2,1)S(1)} %copy-done), channel_id=1, source_target_pairs={{0,8},{8,16},{16,24},{24,28},{28,20},{20,12},{12,4},{4,0},{1,9},{9... | collective-permute-start | bytes 786440 | tf_op jit(solution)/shard_map/ppermute | solution.py:73
  32.8 2.1 %collective-permute-start.4 = (bf16[256,512]{1,0:T(8,128)(2,1)S(1)}, bf16[256,512]{1,0:T(8,128)(2,1)S(1)}, u32[]{:S(2)}, u32[]{:S(2)}) collective-permute-start(bf16[256,512]{1,0:T(8,128)(2,1)S(1)} %collective-permute-done.2.refs_3_), channel_id=1, source_target_pairs={{0,8},{8,16},{16,24},{24,28},{28,20},{20,12},{12,4},{4,0},{1,9},{9... | collective-permute-start | bytes 786440 | tf_op jit(solution)/shard_map/ppermute | solution.py:73
  34.9 1.4 %collective-permute-done.10.refs_12_ = bf16[256,512]{1,0:T(8,128)(2,1)S(1)} collective-permute-done((bf16[256,512]{1,0:T(8,128)(2,1)S(1)}, bf16[256,512]{1,0:T(8,128)(2,1)S(1)}, u32[]{:S(2)}, u32[]{:S(2)}) %collective-permute-start.10) | collective-permute-done | bytes 262176 | tf_op jit(solution)/shard_map/ppermute | solution.py:73
  36.3 2.1 %collective-permute-done.19.refs_3_ = bf16[256,512]{1,0:T(8,128)(2,1)S(1)} collective-permute-done((bf16[256,512]{1,0:T(8,128)(2,1)S(1)}, bf16[256,512]{1,0:T(8,128)(2,1)S(1)}, u32[]{:S(2)}, u32[]{:S(2)}) %collective-permute-start.19) | collective-permute-done | bytes 262176 | tf_op jit(solution)/shard_map/ppermute | solution.py:73
  38.4 2.1 %collective-permute-start.5 = (bf16[256,512]{1,0:T(8,128)(2,1)S(1)}, bf16[256,512]{1,0:T(8,128)(2,1)S(1)}, u32[]{:S(2)}, u32[]{:S(2)}) collective-permute-start(bf16[256,512]{1,0:T(8,128)(2,1)S(1)} %collective-permute-done.3.refs_4_), channel_id=1, source_target_pairs={{8,0},{16,8},{24,16},{28,24},{20,28},{12,20},{4,12},{0,4},{9,1},{1... | collective-permute-start | bytes 786440 | tf_op jit(solution)/shard_map/ppermute | solution.py:73
  40.5 1.4 %collective-permute-done.25.refs_2_ = bf16[512,256]{1,0:T(8,128)(2,1)S(1)} collective-permute-done((bf16[512,256]{1,0:T(8,128)(2,1)S(1)}, bf16[512,256]{1,0:T(8,128)(2,1)S(1)}, u32[]{:S(2)}, u32[]{:S(2)}) %collective-permute-start.25) | collective-permute-done | bytes 262176 | tf_op jit(solution)/shard_map/ppermute | solution.py:73
  42.0 2.0 %collective-permute-done.24.refs_1_ = bf16[512,256]{1,0:T(8,128)(2,1)S(1)} collective-permute-done((bf16[512,256]{1,0:T(8,128)(2,1)S(1)}, bf16[512,256]{1,0:T(8,128)(2,1)S(1)}, u32[]{:S(2)}, u32[]{:S(2)}) %collective-permute-start.24) | collective-permute-done | bytes 262176 | tf_op jit(solution)/shard_map/ppermute | solution.py:73
  44.0 2.1 %collective-permute-start.11 = (bf16[256,512]{1,0:T(8,128)(2,1)S(1)}, bf16[256,512]{1,0:T(8,128)(2,1)S(1)}, u32[]{:S(2)}, u32[]{:S(2)}) collective-permute-start(bf16[256,512]{1,0:T(8,128)(2,1)S(1)} %collective-permute-done.9.refs_11_), channel_id=1, source_target_pairs={{0,8},{8,16},{16,24},{24,28},{28,20},{20,12},{12,4},{4,0},{1,9},{9... | collective-permute-start | bytes 786440 | tf_op jit(solution)/shard_map/ppermute | solution.py:73
  46.1 3.5 %collective-permute-done.4.refs_5_ = bf16[256,512]{1,0:T(8,128)(2,1)S(1)} collective-permute-done((bf16[256,512]{1,0:T(8,128)(2,1)S(1)}, bf16[256,512]{1,0:T(8,128)(2,1)S(1)}, u32[]{:S(2)}, u32[]{:S(2)}) %collective-permute-start.4) | collective-permute-done | bytes 262176 | tf_op jit(solution)/shard_map/ppermute | solution.py:73
  49.6 2.1 %collective-permute-start.6 = (bf16[256,512]{1,0:T(8,128)(2,1)S(1)}, bf16[256,512]{1,0:T(8,128)(2,1)S(1)}, u32[]{:S(2)}, u32[]{:S(2)}) collective-permute-start(bf16[256,512]{1,0:T(8,128)(2,1)S(1)} %collective-permute-done.4.refs_5_), channel_id=1, source_target_pairs={{0,8},{8,16},{16,24},{24,28},{28,20},{20,12},{12,4},{4,0},{1,9},{9... | collective-permute-start | bytes 786440 | tf_op jit(solution)/shard_map/ppermute | solution.py:73
  51.8 1.4 %collective-permute-done.5.refs_6_ = bf16[256,512]{1,0:T(8,128)(2,1)S(1)} collective-permute-done((bf16[256,512]{1,0:T(8,128)(2,1)S(1)}, bf16[256,512]{1,0:T(8,128)(2,1)S(1)}, u32[]{:S(2)}, u32[]{:S(2)}) %collective-permute-start.5) | collective-permute-done | bytes 262176 | tf_op jit(solution)/shard_map/ppermute | solution.py:73
  53.7 5.0 %collective-permute-done.27.refs_4_ = bf16[512,256]{1,0:T(8,128)(2,1)S(1)} collective-permute-done((bf16[512,256]{1,0:T(8,128)(2,1)S(1)}, bf16[512,256]{1,0:T(8,128)(2,1)S(1)}, u32[]{:S(2)}, u32[]{:S(2)}) %collective-permute-start.27) | collective-permute-done | bytes 262176 | tf_op jit(solution)/shard_map/ppermute | solution.py:73
  58.8 2.0 %collective-permute-start.21 = (bf16[256,512]{1,0:T(8,128)(2,1)S(1)}, bf16[256,512]{1,0:T(8,128)(2,1)S(1)}, u32[]{:S(2)}, u32[]{:S(2)}) collective-permute-start(bf16[256,512]{1,0:T(8,128)(2,1)S(1)} %collective-permute-done.19.refs_3_), channel_id=1, source_target_pairs={{0,8},{8,16},{16,24},{24,28},{28,20},{20,12},{12,4},{4,0},{1,9},{9... | collective-permute-start | bytes 786440 | tf_op jit(solution)/shard_map/ppermute | solution.py:73
  60.9 2.1 %collective-permute-start.26 = (bf16[512,256]{1,0:T(8,128)(2,1)S(1)}, bf16[512,256]{1,0:T(8,128)(2,1)S(1)}, u32[]{:S(2)}, u32[]{:S(2)}) collective-permute-start(bf16[512,256]{1,0:T(8,128)(2,1)S(1)} %collective-permute-done.24.refs_1_), channel_id=1, source_target_pairs={{0,8},{8,16},{16,24},{24,28},{28,20},{20,12},{12,4},{4,0},{1,9},{9... | collective-permute-start | bytes 786440 | tf_op jit(solution)/shard_map/ppermute | solution.py:73
  63.0 1.4 %collective-permute-done.13.refs_15_ = bf16[256,512]{1,0:T(8,128)(2,1)S(1)} collective-permute-done((bf16[256,512]{1,0:T(8,128)(2,1)S(1)}, bf16[256,512]{1,0:T(8,128)(2,1)S(1)}, u32[]{:S(2)}, u32[]{:S(2)}) %collective-permute-start.13) | collective-permute-done | bytes 262176 | tf_op jit(solution)/shard_map/ppermute | solution.py:73
  65.2 6.9 %shard_map.65 = (bf16[512,512]{1,0:T(8,128)(2,1)}, bf16[512,512]{1,0:T(8,128)(2,1)}, f32[4,128,128]{2,1,0:T(8,128)}, bf16[4,128,128]{2,1,0:T(8,128)(2,1)}) custom-call(s32[2,8]{1,0:T(2,128)} %stack.88.starts, bf16[512,2048]{1,0:T(8,128)(2,1)} %tokens.2, bf16[256,512]{1,0:T(8,128)(2,1)} %refs_0_.4, bf16[256,512]{1,0:T(8,128)(2,1)} %copy-done.19, ...), custom_call_target="tpu_custom_call" | custom-call | flops 1 | bytes 30933248 | tf_op jit(solution)/shard_map/pallas_call | solution.py:22
  72.1 1.5 %collective-permute-start.16 = (bf16[4,128,128]{2,1,0:T(8,128)(2,1)}, bf16[4,128,128]{2,1,0:T(8,128)(2,1)S(1)}, u32[]{:S(2)}, u32[]{:S(2)}) collective-permute-start(bf16[4,128,128]{2,1,0:T(8,128)(2,1)} %get-tuple-element.33), channel_id=1, source_target_pairs={{0,12},{4,8},{8,4},{12,0},{16,28},{20,24},{24,20},{28,16},{1,13},{... | collective-permute-start | bytes 393224 | tf_op jit(solution)/shard_map/ppermute | solution.py:397
  74.6 1.1 collective-permute-start.14
  75.7 0.9 collective-permute-start.22
  76.6 1.1 collective-permute-start.23
  77.7 2.0 %collective-permute-done.16.refs_10_ = bf16[4,128,128]{2,1,0:T(8,128)(2,1)S(1)} collective-permute-done((bf16[4,128,128]{2,1,0:T(8,128)(2,1)}, bf16[4,128,128]{2,1,0:T(8,128)(2,1)S(1)}, u32[]{:S(2)}, u32[]{:S(2)}) %collective-permute-start.16) | collective-permute-done | bytes 131104 | tf_op jit(solution)/shard_map/ppermute | solution.py:397
  79.7 1.6 %collective-permute-start.28 = (bf16[512,256]{1,0:T(8,128)(2,1)S(1)}, bf16[512,256]{1,0:T(8,128)(2,1)S(1)}, u32[]{:S(2)}, u32[]{:S(2)}) collective-permute-start(bf16[512,256]{1,0:T(8,128)(2,1)S(1)} %collective-permute-done.26.refs_3_), channel_id=1, source_target_pairs={{0,8},{8,16},{16,24},{24,28},{28,20},{20,12},{12,4},{4,0},{1,9},{9... | collective-permute-start | bytes 786440 | tf_op jit(solution)/shard_map/ppermute | solution.py:73
  81.3 2.1 %collective-permute-start.30 = (bf16[512,256]{1,0:T(8,128)(2,1)S(1)}, bf16[512,256]{1,0:T(8,128)(2,1)S(1)}, u32[]{:S(2)}, u32[]{:S(2)}) collective-permute-start(bf16[512,256]{1,0:T(8,128)(2,1)S(1)} %collective-permute-done.29.refs_6_), channel_id=1, source_target_pairs={{8,0},{16,8},{24,16},{28,24},{20,28},{12,20},{4,12},{0,4},{9,1},{1... | collective-permute-start | bytes 786440 | tf_op jit(solution)/shard_map/ppermute | solution.py:73
  83.4 1.1 convert_add_fusion
  84.5 1.2 collective-permute-start.31
  85.7 2.6 %collective-permute-done.22.refs_6_ = bf16[256,512]{1,0:T(8,128)(2,1)S(1)} collective-permute-done((bf16[256,512]{1,0:T(8,128)(2,1)S(1)}, bf16[256,512]{1,0:T(8,128)(2,1)S(1)}, u32[]{:S(2)}, u32[]{:S(2)}) %collective-permute-start.22) | collective-permute-done | bytes 262176 | tf_op jit(solution)/shard_map/ppermute | solution.py:73
  88.3 0.7 copy-done.17
  89.1 7.1 %shard_map.66 = (bf16[512,512]{1,0:T(8,128)(2,1)}, f32[512,512]{1,0:T(8,128)}) custom-call(s32[2,8]{1,0:T(2,128)} %stack.88.starts, bf16[512,2048]{1,0:T(8,128)(2,1)} %tokens.2, bf16[512,512]{1,0:T(8,128)(2,1)} %get-tuple-element.35.keys, bf16[512,512]{1,0:T(8,128)(2,1)} %get-tuple-element.36.values, bf16[4,512,512]{2,1,0:T(8,128)(2,1)} %shard_map.64.mixing, ...), custom_call_target="tpu_custom_call" | custom-call | flops 1 | bytes 35651840 | tf_op jit(solution)/shard_map/pallas_call | solution.py:22
  97.1 6.6 %shard_map.67 = (bf16[512,512]{1,0:T(8,128)(2,1)}, bf16[512,512]{1,0:T(8,128)(2,1)}, bf16[512,512]{1,0:T(8,128)(2,1)}) custom-call(f32[3]{0:T(128)} %add_convert_fusion.2.upper, s32[2,8]{1,0:T(2,128)} %stack.99.starts, bf16[512,512]{1,0:T(8,128)(2,1)} %get-tuple-element.37.queries, f32[512,512]{1,0:T(8,128)} %get-tuple-element.38.local, ...), custom_call_target="tpu_custom_call" | custom-call | flops 1 | bytes 23494960 | tf_op jit(solution)/shard_map/pallas_call | solution.py:22
  103.8 2.1 %collective-permute-done.32 = bf16[512,512]{1,0:T(8,128)(2,1)S(1)} collective-permute-done((bf16[512,512]{1,0:T(8,128)(2,1)}, bf16[512,512]{1,0:T(8,128)(2,1)S(1)}, u32[]{:S(2)}, u32[]{:S(2)}) %collective-permute-start.32) | collective-permute-done | bytes 524320 | tf_op jit(solution)/shard_map/ppermute | solution.py:420
  105.9 1.2 add_convert_fusion.1
  107.1 1.9 %collective-permute-start.34 = (bf16[512,512]{1,0:T(8,128)(2,1)S(1)}, bf16[512,512]{1,0:T(8,128)(2,1)S(1)}, u32[]{:S(2)}, u32[]{:S(2)}) collective-permute-start(bf16[512,512]{1,0:T(8,128)(2,1)S(1)} %add_convert_fusion.1), channel_id=1, source_target_pairs={{0,2},{1,3},{2,0},{3,1},{4,6},{5,7},{6,4},{7,5},{8,10},{9,11},{10,... | collective-permute-start | bytes 1572872 | tf_op jit(solution)/shard_map/ppermute | solution.py:420
  109.0 3.8 %shard_map.68 = (bf16[512,512]{1,0:T(8,128)(2,1)}, bf16[512,512]{1,0:T(8,128)(2,1)}) custom-call(s32[2,8]{1,0:T(2,128)} %stack.99.starts, bf16[512,512]{1,0:T(8,128)(2,1)} %get-tuple-element.44.attended, bf16[512,256]{1,0:T(8,128)(2,1)} %refs_0_.7, bf16[512,256]{1,0:T(8,128)(2,1)} %copy-done.2, bf16[512,256]{1,0:T(8,128)(2,1)} %copy-done.1, ...), custom_call_target="tpu_custom_call" | custom-call | flops 1 | bytes 14680320 | tf_op jit(solution)/shard_map/pallas_call | solution.py:22
  112.9 8.3 %collective-permute-done.34 = bf16[512,512]{1,0:T(8,128)(2,1)S(1)} collective-permute-done((bf16[512,512]{1,0:T(8,128)(2,1)S(1)}, bf16[512,512]{1,0:T(8,128)(2,1)S(1)}, u32[]{:S(2)}, u32[]{:S(2)}) %collective-permute-start.34) | collective-permute-done | bytes 524320 | tf_op jit(solution)/shard_map/ppermute | solution.py:420
  121.2 2.0 %add_convert_fusion = bf16[512,512]{1,0:T(8,128)(2,1)} fusion(bf16[512,512]{1,0:T(8,128)(2,1)S(1)} %collective-permute-done.34, bf16[512,512]{1,0:T(8,128)(2,1)S(1)} %collective-permute-done.33, bf16[512,512]{1,0:T(8,128)(2,1)} %get-tuple-element.45), kind=kLoop, calls=%fused_computation | loop fusion | flops 1572864 | bytes 2097152 | tf_op jit(solution)/shard_map/convert_element_type | solution.py:438
  (104 shorter events, 6.8 us)
Async XLA Ops:
  0.0 15.8 %collective-permute-start = (bf16[256,512]{1,0:T(8,128)(2,1)}, bf16[256,512]{1,0:T(8,128)(2,1)S(1)}, u32[]{:S(2)}, u32[]{:S(2)}) collective-permute-start(bf16[256,512]{1,0:T(8,128)(2,1)} %refs_0_.4), channel_id=1, source_target_pairs={{0,8},{8,16},{16,24},{24,28},{28,20},{20,12},{12,4},{4,0},{1,9},{9... | collective-permute-start | bytes 786440 | tf_op jit(solution)/shard_map/ppermute | solution.py:73
  3.0 12.8 %collective-permute-start.1 = (bf16[256,512]{1,0:T(8,128)(2,1)}, bf16[256,512]{1,0:T(8,128)(2,1)S(1)}, u32[]{:S(2)}, u32[]{:S(2)}) collective-permute-start(bf16[256,512]{1,0:T(8,128)(2,1)} %refs_0_.4), channel_id=1, source_target_pairs={{8,0},{16,8},{24,16},{28,24},{20,28},{12,20},{4,12},{0,4},{9,1},{1... | collective-permute-start | bytes 786440 | tf_op jit(solution)/shard_map/ppermute | solution.py:73
  3.0 14.8 %collective-permute-start.7 = (bf16[256,512]{1,0:T(8,128)(2,1)}, bf16[256,512]{1,0:T(8,128)(2,1)S(1)}, u32[]{:S(2)}, u32[]{:S(2)}) collective-permute-start(bf16[256,512]{1,0:T(8,128)(2,1)} %refs_8_.1), channel_id=1, source_target_pairs={{0,8},{8,16},{16,24},{24,28},{28,20},{20,12},{12,4},{4,0},{1,9},{9... | collective-permute-start | bytes 786440 | tf_op jit(solution)/shard_map/ppermute | solution.py:73
  5.1 12.9 %collective-permute-start.8 = (bf16[256,512]{1,0:T(8,128)(2,1)}, bf16[256,512]{1,0:T(8,128)(2,1)S(1)}, u32[]{:S(2)}, u32[]{:S(2)}) collective-permute-start(bf16[256,512]{1,0:T(8,128)(2,1)} %refs_8_.1), channel_id=1, source_target_pairs={{8,0},{16,8},{24,16},{28,24},{20,28},{12,20},{4,12},{0,4},{9,1},{1... | collective-permute-start | bytes 786440 | tf_op jit(solution)/shard_map/ppermute | solution.py:73
  5.1 16.5 %collective-permute-start.17 = (bf16[256,512]{1,0:T(8,128)(2,1)}, bf16[256,512]{1,0:T(8,128)(2,1)S(1)}, u32[]{:S(2)}, u32[]{:S(2)}) collective-permute-start(bf16[256,512]{1,0:T(8,128)(2,1)} %refs_0_.5), channel_id=1, source_target_pairs={{0,8},{8,16},{16,24},{24,28},{28,20},{20,12},{12,4},{4,0},{1,9},{9... | collective-permute-start | bytes 786440 | tf_op jit(solution)/shard_map/ppermute | solution.py:73
  15.8 48.6 %copy-start.19 = (bf16[256,512]{1,0:T(8,128)(2,1)}, bf16[256,512]{1,0:T(8,128)(2,1)S(1)}, u32[]{:S(2)}) copy-start(bf16[256,512]{1,0:T(8,128)(2,1)S(1)} %collective-permute-done.refs_1_) | copy-start | bytes 786436
  15.8 9.3 %collective-permute-start.18 = (bf16[256,512]{1,0:T(8,128)(2,1)S(1)}, bf16[256,512]{1,0:T(8,128)(2,1)S(1)}, u32[]{:S(2)}, u32[]{:S(2)}) collective-permute-start(bf16[256,512]{1,0:T(8,128)(2,1)S(1)} %copy-done.11), channel_id=1, source_target_pairs={{8,0},{16,8},{24,16},{28,24},{20,28},{12,20},{4,12},{0,4},{9,1},{1... | collective-permute-start | bytes 786440 | tf_op jit(solution)/shard_map/ppermute | solution.py:73
  15.8 48.6 %copy-start.20 = (bf16[256,512]{1,0:T(8,128)(2,1)}, bf16[256,512]{1,0:T(8,128)(2,1)S(1)}, u32[]{:S(2)}) copy-start(bf16[256,512]{1,0:T(8,128)(2,1)S(1)} %collective-permute-done.1.refs_2_) | copy-start | bytes 786436
  15.8 11.3 %collective-permute-start.2 = (bf16[256,512]{1,0:T(8,128)(2,1)S(1)}, bf16[256,512]{1,0:T(8,128)(2,1)S(1)}, u32[]{:S(2)}, u32[]{:S(2)}) collective-permute-start(bf16[256,512]{1,0:T(8,128)(2,1)S(1)} %collective-permute-done.refs_1_), channel_id=1, source_target_pairs={{0,8},{8,16},{16,24},{24,28},{28,20},{20,12},{12,4},{4,0},{1,9},{9... | collective-permute-start | bytes 786440 | tf_op jit(solution)/shard_map/ppermute | solution.py:73
  17.8 46.5 %copy-start.21 = (bf16[256,512]{1,0:T(8,128)(2,1)}, bf16[256,512]{1,0:T(8,128)(2,1)S(1)}, u32[]{:S(2)}) copy-start(bf16[256,512]{1,0:T(8,128)(2,1)S(1)} %collective-permute-done.7.refs_9_) | copy-start | bytes 786436
  17.8 12.8 %collective-permute-start.3 = (bf16[256,512]{1,0:T(8,128)(2,1)S(1)}, bf16[256,512]{1,0:T(8,128)(2,1)S(1)}, u32[]{:S(2)}, u32[]{:S(2)}) collective-permute-start(bf16[256,512]{1,0:T(8,128)(2,1)S(1)} %collective-permute-done.1.refs_2_), channel_id=1, source_target_pairs={{8,0},{16,8},{24,16},{28,24},{20,28},{12,20},{4,12},{0,4},{9,1},{1... | collective-permute-start | bytes 786440 | tf_op jit(solution)/shard_map/ppermute | solution.py:73
  18.0 46.4 %copy-start.22 = (bf16[256,512]{1,0:T(8,128)(2,1)}, bf16[256,512]{1,0:T(8,128)(2,1)S(1)}, u32[]{:S(2)}) copy-start(bf16[256,512]{1,0:T(8,128)(2,1)S(1)} %collective-permute-done.8.refs_10_) | copy-start | bytes 786436
  18.0 14.8 %collective-permute-start.9 = (bf16[256,512]{1,0:T(8,128)(2,1)S(1)}, bf16[256,512]{1,0:T(8,128)(2,1)S(1)}, u32[]{:S(2)}, u32[]{:S(2)}) collective-permute-start(bf16[256,512]{1,0:T(8,128)(2,1)S(1)} %collective-permute-done.7.refs_9_), channel_id=1, source_target_pairs={{0,8},{8,16},{16,24},{24,28},{28,20},{20,12},{12,4},{4,0},{1,9},{9... | collective-permute-start | bytes 786440 | tf_op jit(solution)/shard_map/ppermute | solution.py:73
  21.5 50.5 %copy-start.12 = (bf16[256,512]{1,0:T(8,128)(2,1)}, bf16[256,512]{1,0:T(8,128)(2,1)S(1)}, u32[]{:S(2)}) copy-start(bf16[256,512]{1,0:T(8,128)(2,1)S(1)} %collective-permute-done.17.refs_1_) | copy-start | bytes 786436
  21.5 14.7 %collective-permute-start.10 = (bf16[256,512]{1,0:T(8,128)(2,1)S(1)}, bf16[256,512]{1,0:T(8,128)(2,1)S(1)}, u32[]{:S(2)}, u32[]{:S(2)}) collective-permute-start(bf16[256,512]{1,0:T(8,128)(2,1)S(1)} %collective-permute-done.8.refs_10_), channel_id=1, source_target_pairs={{8,0},{16,8},{24,16},{28,24},{20,28},{12,20},{4,12},{0,4},{9,1},{1... | collective-permute-start | bytes 786440 | tf_op jit(solution)/shard_map/ppermute | solution.py:73
  25.1 47.0 %copy-start.13 = (bf16[256,512]{1,0:T(8,128)(2,1)}, bf16[256,512]{1,0:T(8,128)(2,1)S(1)}, u32[]{:S(2)}) copy-start(bf16[256,512]{1,0:T(8,128)(2,1)S(1)} %collective-permute-done.18.refs_2_) | copy-start | bytes 786436
  25.1 13.3 %collective-permute-start.19 = (bf16[256,512]{1,0:T(8,128)(2,1)S(1)}, bf16[256,512]{1,0:T(8,128)(2,1)S(1)}, u32[]{:S(2)}, u32[]{:S(2)}) collective-permute-start(bf16[256,512]{1,0:T(8,128)(2,1)S(1)} %collective-permute-done.17.refs_1_), channel_id=1, source_target_pairs={{0,8},{8,16},{16,24},{24,28},{28,20},{20,12},{12,4},{4,0},{1,9},{9... | collective-permute-start | bytes 786440 | tf_op jit(solution)/shard_map/ppermute | solution.py:73
  27.2 37.2 %copy-start.23 = (bf16[256,512]{1,0:T(8,128)(2,1)}, bf16[256,512]{1,0:T(8,128)(2,1)S(1)}, u32[]{:S(2)}) copy-start(bf16[256,512]{1,0:T(8,128)(2,1)S(1)} %collective-permute-done.2.refs_3_) | copy-start | bytes 786436
  27.2 14.7 %collective-permute-start.25 = (bf16[512,256]{1,0:T(8,128)(2,1)S(1)}, bf16[512,256]{1,0:T(8,128)(2,1)S(1)}, u32[]{:S(2)}, u32[]{:S(2)}) collective-permute-start(bf16[512,256]{1,0:T(8,128)(2,1)S(1)} %copy-done), channel_id=1, source_target_pairs={{8,0},{16,8},{24,16},{28,24},{20,28},{12,20},{4,12},{0,4},{9,1},{1... | collective-permute-start | bytes 786440 | tf_op jit(solution)/shard_map/ppermute | solution.py:73
  30.7 33.7 %copy-start.24 = (bf16[256,512]{1,0:T(8,128)(2,1)}, bf16[256,512]{1,0:T(8,128)(2,1)S(1)}, u32[]{:S(2)}) copy-start(bf16[256,512]{1,0:T(8,128)(2,1)S(1)} %collective-permute-done.3.refs_4_) | copy-start | bytes 786436
  30.7 13.3 %collective-permute-start.24 = (bf16[512,256]{1,0:T(8,128)(2,1)S(1)}, bf16[512,256]{1,0:T(8,128)(2,1)S(1)}, u32[]{:S(2)}, u32[]{:S(2)}) collective-permute-start(bf16[512,256]{1,0:T(8,128)(2,1)S(1)} %copy-done), channel_id=1, source_target_pairs={{0,8},{8,16},{16,24},{24,28},{28,20},{20,12},{12,4},{4,0},{1,9},{9... | collective-permute-start | bytes 786440 | tf_op jit(solution)/shard_map/ppermute | solution.py:73
  32.8 31.6 %copy-start.25 = (bf16[256,512]{1,0:T(8,128)(2,1)}, bf16[256,512]{1,0:T(8,128)(2,1)S(1)}, u32[]{:S(2)}) copy-start(bf16[256,512]{1,0:T(8,128)(2,1)S(1)} %collective-permute-done.9.refs_11_) | copy-start | bytes 786436
  32.8 16.9 %collective-permute-start.4 = (bf16[256,512]{1,0:T(8,128)(2,1)S(1)}, bf16[256,512]{1,0:T(8,128)(2,1)S(1)}, u32[]{:S(2)}, u32[]{:S(2)}) collective-permute-start(bf16[256,512]{1,0:T(8,128)(2,1)S(1)} %collective-permute-done.2.refs_3_), channel_id=1, source_target_pairs={{0,8},{8,16},{16,24},{24,28},{28,20},{20,12},{12,4},{4,0},{1,9},{9... | collective-permute-start | bytes 786440 | tf_op jit(solution)/shard_map/ppermute | solution.py:73
  36.3 28.1 %copy-start.26 = (bf16[256,512]{1,0:T(8,128)(2,1)}, bf16[256,512]{1,0:T(8,128)(2,1)S(1)}, u32[]{:S(2)}) copy-start(bf16[256,512]{1,0:T(8,128)(2,1)S(1)} %collective-permute-done.10.refs_12_) | copy-start | bytes 786436
  36.3 15.5 %collective-permute-start.12 = (bf16[256,512]{1,0:T(8,128)(2,1)S(1)}, bf16[256,512]{1,0:T(8,128)(2,1)S(1)}, u32[]{:S(2)}, u32[]{:S(2)}) collective-permute-start(bf16[256,512]{1,0:T(8,128)(2,1)S(1)} %collective-permute-done.10.refs_12_), channel_id=1, source_target_pairs={{8,0},{16,8},{24,16},{28,24},{20,28},{12,20},{4,12},{0,4},{9,1},{1... | collective-permute-start | bytes 786440 | tf_op jit(solution)/shard_map/ppermute | solution.py:73
  38.4 33.7 %copy-start.14 = (bf16[256,512]{1,0:T(8,128)(2,1)}, bf16[256,512]{1,0:T(8,128)(2,1)S(1)}, u32[]{:S(2)}) copy-start(bf16[256,512]{1,0:T(8,128)(2,1)S(1)} %collective-permute-done.19.refs_3_) | copy-start | bytes 786436
  38.4 14.7 %collective-permute-start.5 = (bf16[256,512]{1,0:T(8,128)(2,1)S(1)}, bf16[256,512]{1,0:T(8,128)(2,1)S(1)}, u32[]{:S(2)}, u32[]{:S(2)}) collective-permute-start(bf16[256,512]{1,0:T(8,128)(2,1)S(1)} %collective-permute-done.3.refs_4_), channel_id=1, source_target_pairs={{8,0},{16,8},{24,16},{28,24},{20,28},{12,20},{4,12},{0,4},{9,1},{1... | collective-permute-start | bytes 786440 | tf_op jit(solution)/shard_map/ppermute | solution.py:73
  41.9 30.2 %copy-start.1 = (bf16[512,256]{1,0:T(8,128)(2,1)}, bf16[512,256]{1,0:T(8,128)(2,1)S(1)}, u32[]{:S(2)}) copy-start(bf16[512,256]{1,0:T(8,128)(2,1)S(1)} %collective-permute-done.25.refs_2_) | copy-start | bytes 786436
  41.9 16.9 %collective-permute-start.27 = (bf16[512,256]{1,0:T(8,128)(2,1)S(1)}, bf16[512,256]{1,0:T(8,128)(2,1)S(1)}, u32[]{:S(2)}, u32[]{:S(2)}) collective-permute-start(bf16[512,256]{1,0:T(8,128)(2,1)S(1)} %collective-permute-done.25.refs_2_), channel_id=1, source_target_pairs={{8,0},{16,8},{24,16},{28,24},{20,28},{12,20},{4,12},{0,4},{9,1},{1... | collective-permute-start | bytes 786440 | tf_op jit(solution)/shard_map/ppermute | solution.py:73
  44.0 28.1 %copy-start.2 = (bf16[512,256]{1,0:T(8,128)(2,1)}, bf16[512,256]{1,0:T(8,128)(2,1)S(1)}, u32[]{:S(2)}) copy-start(bf16[512,256]{1,0:T(8,128)(2,1)S(1)} %collective-permute-done.24.refs_1_) | copy-start | bytes 786436
  44.0 14.7 %collective-permute-start.11 = (bf16[256,512]{1,0:T(8,128)(2,1)S(1)}, bf16[256,512]{1,0:T(8,128)(2,1)S(1)}, u32[]{:S(2)}, u32[]{:S(2)}) collective-permute-start(bf16[256,512]{1,0:T(8,128)(2,1)S(1)} %collective-permute-done.9.refs_11_), channel_id=1, source_target_pairs={{0,8},{8,16},{16,24},{24,28},{28,20},{20,12},{12,4},{4,0},{1,9},{9... | collective-permute-start | bytes 786440 | tf_op jit(solution)/shard_map/ppermute | solution.py:73
  49.6 11.2 %collective-permute-start.6 = (bf16[256,512]{1,0:T(8,128)(2,1)S(1)}, bf16[256,512]{1,0:T(8,128)(2,1)S(1)}, u32[]{:S(2)}, u32[]{:S(2)}) collective-permute-start(bf16[256,512]{1,0:T(8,128)(2,1)S(1)} %collective-permute-done.4.refs_5_), channel_id=1, source_target_pairs={{0,8},{8,16},{16,24},{24,28},{28,20},{20,12},{12,4},{4,0},{1,9},{9... | collective-permute-start | bytes 786440 | tf_op jit(solution)/shard_map/ppermute | solution.py:73
  51.8 12.6 %collective-permute-start.13 = (bf16[256,512]{1,0:T(8,128)(2,1)S(1)}, bf16[256,512]{1,0:T(8,128)(2,1)S(1)}, u32[]{:S(2)}, u32[]{:S(2)}) collective-permute-start(bf16[256,512]{1,0:T(8,128)(2,1)S(1)} %collective-permute-done.12.refs_14_), channel_id=1, source_target_pairs={{8,0},{16,8},{24,16},{28,24},{20,28},{12,20},{4,12},{0,4},{9,1},{1... | collective-permute-start | bytes 786440 | tf_op jit(solution)/shard_map/ppermute | solution.py:73
  53.1 20.5 %collective-permute-start.20 = (bf16[256,512]{1,0:T(8,128)(2,1)S(1)}, bf16[256,512]{1,0:T(8,128)(2,1)S(1)}, u32[]{:S(2)}, u32[]{:S(2)}) collective-permute-start(bf16[256,512]{1,0:T(8,128)(2,1)S(1)} %collective-permute-done.18.refs_2_), channel_id=1, source_target_pairs={{8,0},{16,8},{24,16},{28,24},{20,28},{12,20},{4,12},{0,4},{9,1},{1... | collective-permute-start | bytes 786440 | tf_op jit(solution)/shard_map/ppermute | solution.py:73
  58.8 15.8 %collective-permute-start.29 = (bf16[512,256]{1,0:T(8,128)(2,1)S(1)}, bf16[512,256]{1,0:T(8,128)(2,1)S(1)}, u32[]{:S(2)}, u32[]{:S(2)}) collective-permute-start(bf16[512,256]{1,0:T(8,128)(2,1)S(1)} %collective-permute-done.27.refs_4_), channel_id=1, source_target_pairs={{8,0},{16,8},{24,16},{28,24},{20,28},{12,20},{4,12},{0,4},{9,1},{1... | collective-permute-start | bytes 786440 | tf_op jit(solution)/shard_map/ppermute | solution.py:73
  58.8 16.9 %collective-permute-start.21 = (bf16[256,512]{1,0:T(8,128)(2,1)S(1)}, bf16[256,512]{1,0:T(8,128)(2,1)S(1)}, u32[]{:S(2)}, u32[]{:S(2)}) collective-permute-start(bf16[256,512]{1,0:T(8,128)(2,1)S(1)} %collective-permute-done.19.refs_3_), channel_id=1, source_target_pairs={{0,8},{8,16},{16,24},{24,28},{28,20},{20,12},{12,4},{4,0},{1,9},{9... | collective-permute-start | bytes 786440 | tf_op jit(solution)/shard_map/ppermute | solution.py:73
  60.9 15.7 %collective-permute-start.26 = (bf16[512,256]{1,0:T(8,128)(2,1)S(1)}, bf16[512,256]{1,0:T(8,128)(2,1)S(1)}, u32[]{:S(2)}, u32[]{:S(2)}) collective-permute-start(bf16[512,256]{1,0:T(8,128)(2,1)S(1)} %collective-permute-done.24.refs_1_), channel_id=1, source_target_pairs={{0,8},{8,16},{16,24},{24,28},{28,20},{20,12},{12,4},{4,0},{1,9},{9... | collective-permute-start | bytes 786440 | tf_op jit(solution)/shard_map/ppermute | solution.py:73
  72.1 7.6 %collective-permute-start.16 = (bf16[4,128,128]{2,1,0:T(8,128)(2,1)}, bf16[4,128,128]{2,1,0:T(8,128)(2,1)S(1)}, u32[]{:S(2)}, u32[]{:S(2)}) collective-permute-start(bf16[4,128,128]{2,1,0:T(8,128)(2,1)} %get-tuple-element.33), channel_id=1, source_target_pairs={{0,12},{4,8},{8,4},{12,0},{16,28},{20,24},{24,20},{28,16},{1,13},{... | collective-permute-start | bytes 393224 | tf_op jit(solution)/shard_map/ppermute | solution.py:397
  73.6 7.7 %collective-permute-start.15 = (bf16[4,128,128]{2,1,0:T(8,128)(2,1)}, bf16[4,128,128]{2,1,0:T(8,128)(2,1)S(1)}, u32[]{:S(2)}, u32[]{:S(2)}) collective-permute-start(bf16[4,128,128]{2,1,0:T(8,128)(2,1)} %get-tuple-element.33), channel_id=1, source_target_pairs={{0,8},{4,12},{8,0},{12,4},{16,24},{20,28},{24,16},{28,20},{1,9},{5... | collective-permute-start | bytes 393224 | tf_op jit(solution)/shard_map/ppermute | solution.py:397
  74.6 8.8 %collective-permute-start.14 = (bf16[4,128,128]{2,1,0:T(8,128)(2,1)}, bf16[4,128,128]{2,1,0:T(8,128)(2,1)S(1)}, u32[]{:S(2)}, u32[]{:S(2)}) collective-permute-start(bf16[4,128,128]{2,1,0:T(8,128)(2,1)} %get-tuple-element.33), channel_id=1, source_target_pairs={{0,4},{4,0},{8,12},{12,8},{16,20},{20,16},{24,28},{28,24},{1,5},{5... | collective-permute-start | bytes 393224 | tf_op jit(solution)/shard_map/ppermute | solution.py:397
  75.7 12.5 %collective-permute-start.22 = (bf16[256,512]{1,0:T(8,128)(2,1)S(1)}, bf16[256,512]{1,0:T(8,128)(2,1)S(1)}, u32[]{:S(2)}, u32[]{:S(2)}) collective-permute-start(bf16[256,512]{1,0:T(8,128)(2,1)S(1)} %collective-permute-done.20.refs_4_), channel_id=1, source_target_pairs={{8,0},{16,8},{24,16},{28,24},{20,28},{12,20},{4,12},{0,4},{9,1},{1... | collective-permute-start | bytes 786440 | tf_op jit(solution)/shard_map/ppermute | solution.py:73
  76.6 11.6 %collective-permute-start.23 = (bf16[256,512]{1,0:T(8,128)(2,1)S(1)}, bf16[256,512]{1,0:T(8,128)(2,1)S(1)}, u32[]{:S(2)}, u32[]{:S(2)}) collective-permute-start(bf16[256,512]{1,0:T(8,128)(2,1)S(1)} %collective-permute-done.21.refs_5_), channel_id=1, source_target_pairs={{0,8},{8,16},{16,24},{24,28},{28,20},{20,12},{12,4},{4,0},{1,9},{9... | collective-permute-start | bytes 786440 | tf_op jit(solution)/shard_map/ppermute | solution.py:73
  79.7 16.6 %collective-permute-start.28 = (bf16[512,256]{1,0:T(8,128)(2,1)S(1)}, bf16[512,256]{1,0:T(8,128)(2,1)S(1)}, u32[]{:S(2)}, u32[]{:S(2)}) collective-permute-start(bf16[512,256]{1,0:T(8,128)(2,1)S(1)} %collective-permute-done.26.refs_3_), channel_id=1, source_target_pairs={{0,8},{8,16},{16,24},{24,28},{28,20},{20,12},{12,4},{4,0},{1,9},{9... | collective-permute-start | bytes 786440 | tf_op jit(solution)/shard_map/ppermute | solution.py:73
  81.3 15.0 %collective-permute-start.30 = (bf16[512,256]{1,0:T(8,128)(2,1)S(1)}, bf16[512,256]{1,0:T(8,128)(2,1)S(1)}, u32[]{:S(2)}, u32[]{:S(2)}) collective-permute-start(bf16[512,256]{1,0:T(8,128)(2,1)S(1)} %collective-permute-done.29.refs_6_), channel_id=1, source_target_pairs={{8,0},{16,8},{24,16},{28,24},{20,28},{12,20},{4,12},{0,4},{9,1},{1... | collective-permute-start | bytes 786440 | tf_op jit(solution)/shard_map/ppermute | solution.py:73
  84.5 11.8 %collective-permute-start.31 = (bf16[4,128,128]{2,1,0:T(8,128)(2,1)S(1)}, bf16[4,128,128]{2,1,0:T(8,128)(2,1)S(1)}, u32[]{:S(2)}, u32[]{:S(2)}) collective-permute-start(bf16[4,128,128]{2,1,0:T(8,128)(2,1)S(1)} %convert_add_fusion), channel_id=1, source_target_pairs={{0,16},{4,20},{8,24},{12,28},{16,0},{20,4},{24,8},{28,12},{1,17},{... | collective-permute-start | bytes 393224 | tf_op jit(solution)/shard_map/ppermute | solution.py:397
  103.7 2.2 %collective-permute-start.32 = (bf16[512,512]{1,0:T(8,128)(2,1)}, bf16[512,512]{1,0:T(8,128)(2,1)S(1)}, u32[]{:S(2)}, u32[]{:S(2)}) collective-permute-start(bf16[512,512]{1,0:T(8,128)(2,1)} %get-tuple-element.43), channel_id=1, source_target_pairs={{0,1},{1,0},{2,3},{3,2},{4,5},{5,4},{6,7},{7,6},{8,9},{9,8},{10,11... | collective-permute-start | bytes 1572872 | tf_op jit(solution)/shard_map/ppermute | solution.py:420
  107.1 14.1 %collective-permute-start.34 = (bf16[512,512]{1,0:T(8,128)(2,1)S(1)}, bf16[512,512]{1,0:T(8,128)(2,1)S(1)}, u32[]{:S(2)}, u32[]{:S(2)}) collective-permute-start(bf16[512,512]{1,0:T(8,128)(2,1)S(1)} %add_convert_fusion.1), channel_id=1, source_target_pairs={{0,2},{1,3},{2,0},{3,1},{4,6},{5,7},{6,4},{7,5},{8,10},{9,11},{10,... | collective-permute-start | bytes 1572872 | tf_op jit(solution)/shard_map/ppermute | solution.py:420
  112.8 8.4 %collective-permute-start.33 = (bf16[512,512]{1,0:T(8,128)(2,1)}, bf16[512,512]{1,0:T(8,128)(2,1)S(1)}, u32[]{:S(2)}, u32[]{:S(2)}) collective-permute-start(bf16[512,512]{1,0:T(8,128)(2,1)} %get-tuple-element.46), channel_id=1, source_target_pairs={{0,1},{1,0},{2,3},{3,2},{4,5},{5,4},{6,7},{7,6},{8,9},{9,8},{10,11... | collective-permute-start | bytes 1572872 | tf_op jit(solution)/shard_map/ppermute | solution.py:420
  (21 other events, 203.2 us)

commit v5 on v3

--- a/solution.py
+++ b/solution.py
@@ -11,19 +11,20 @@
 LONGEST_RING = 16
 SLOWER = 4
 VMEM_BYTES = 56 * 2**20
+END_BYTES = 24 * 2**20
 VMEM = pl.BlockSpec(memory_space=pltpu.VMEM)
 HBM = pl.BlockSpec(memory_space=pl.ANY)
 WHOLE = lambda shape: pl.BlockSpec(shape, lambda *_: (0,) * len(shape))
 SMEM = pl.BlockSpec(memory_space=pltpu.SMEM)
 
 
-def call(kernel, outs, operands, scratch=(), **grid):
+def call(kernel, outs, operands, scratch=(), grant=VMEM_BYTES, **grid):
     nbytes = sum(a.size * a.dtype.itemsize for a in (*operands, *outs))
     return pl.pallas_call(
         kernel,
         out_shape=outs,
         scratch_shapes=list(scratch),
-        compiler_params=pltpu.CompilerParams(vmem_limit_bytes=VMEM_BYTES),
+        compiler_params=pltpu.CompilerParams(vmem_limit_bytes=grant),
         cost_estimate=pl.CostEstimate(
             flops=1, bytes_accessed=SLOWER * nbytes, transcendentals=0
         ),
@@ -318,6 +319,7 @@
         ],
         in_specs=[SMEM] * 2 + [HBM] * (3 + len(pieces) + len(terms)),
         out_specs=[WHOLE(queries.shape)] + [WHOLE((rows, width))] * count,
+        grant=END_BYTES,
         grid=(1,),
     )
 
@@ -340,6 +342,7 @@
         [pltpu.VMEM((inner, width * count), BF16), *semaphores(len(pieces))],
         in_specs=[SMEM, WHOLE((rows, inner))] + [HBM] * len(pieces),
         out_specs=[WHOLE((rows, width))] * count,
+        grant=END_BYTES,
         grid=(1,),
     )
 

time: 123 us -> 120 us (0.976)
  Pallas kernels: 28.9 us -> 24.6 us
  waiting for transfers between devices: 39.3 us -> 43 us
  other arithmetic: 4.83 us -> 2.23 us
    pallas_call x5, Pallas kernels: 28.9 us -> 24.6 us  [call(): pl.pallas_call(kernel, out_shape=outs, scratch_shapes=list(scratch), comp...]
    ppermute x3, waiting for transfers between devices: 10.6 us -> 12.8 us  [from_group(): lax.ppermute(array, 'head', [(g, g ^ 1 << bit) for g in range(groups)])]
    ppermute x28, waiting for transfers between devices: 26.2 us -> 28 us  [advance(): self.ways[way] = lax.ppermute(after(piece, gate), 'seq', pairs)]
    unnamed x65 -> x43, local copies, waits for them, and re-layouts: 3.96 us -> 5.34 us
  transfers between devices with their start and end apart: 35 -> 35, of which waited for: 20 -> 20; matrix products, arithmetic and copies ran while one was open for 4% -> 3% of each run, Pallas kernels for 18% -> 17%
where the time goes in v5:
time: 120 us
  starting transfers between devices  43.8 us (36%)
  waiting for transfers between devices  43 us (36%)
  Pallas kernels  24.6 us (20%)
  local copies, waits for them, and re-layouts  6.12 us (5%)
  other arithmetic  2.23 us (2%)
    ppermute x28, starting transfers between devices, advance(): self.ways[way] = lax.ppermute(after(piece, gate), 'seq', pairs)  38 us
    ppermute x28, waiting for transfers between devices, advance(): self.ways[way] = lax.ppermute(after(piece, gate), 'seq', pairs)  28 us
    pallas_call x5, Pallas kernels, call(): pl.pallas_call(kernel, out_shape=outs, scratch_shapes=list(scratch), comp...  24.6 us
    ppermute x3, waiting for transfers between devices, from_group(): lax.ppermute(array, 'head', [(g, g ^ 1 << bit) for g in range(groups)])  12.8 us
    unnamed x43, local copies, waits for them, and re-layouts  5.34 us
    ppermute x4, starting transfers between devices, from_partner(): return lax.ppermute(array, 'seq', [(i, i ^ apart) for i in range(n)])  4.17 us
  transfers between devices with their start and end apart: 35, of which 20 were waited for; matrix products, arithmetic and copies ran while one was open for 3% of the time, Pallas kernels for 17%

profile of v5, /device:TPU:0, one launch (start us, length us, event | category | flops | bytes accessed | tf_op | source)
XLA Modules:
  0.0 120.0 jit_solution(1394319023795336668)
XLA Ops:
  0.0 3.0 %collective-permute-start = (bf16[256,512]{1,0:T(8,128)(2,1)}, bf16[256,512]{1,0:T(8,128)(2,1)S(1)}, u32[]{:S(2)}, u32[]{:S(2)}) collective-permute-start(bf16[256,512]{1,0:T(8,128)(2,1)} %refs_0_.4), channel_id=1, source_target_pairs={{0,8},{8,16},{16,24},{24,28},{28,20},{20,12},{12,4},{4,0},{1,9},{9... | collective-permute-start | bytes 786440 | tf_op jit(solution)/shard_map/ppermute | solution.py:67
  3.0 2.0 %collective-permute-start.7 = (bf16[256,512]{1,0:T(8,128)(2,1)}, bf16[256,512]{1,0:T(8,128)(2,1)S(1)}, u32[]{:S(2)}, u32[]{:S(2)}) collective-permute-start(bf16[256,512]{1,0:T(8,128)(2,1)} %refs_8_.1), channel_id=1, source_target_pairs={{0,8},{8,16},{16,24},{24,28},{28,20},{20,12},{12,4},{4,0},{1,9},{9... | collective-permute-start | bytes 786440 | tf_op jit(solution)/shard_map/ppermute | solution.py:67
  5.1 2.0 %collective-permute-start.17 = (bf16[256,512]{1,0:T(8,128)(2,1)}, bf16[256,512]{1,0:T(8,128)(2,1)S(1)}, u32[]{:S(2)}, u32[]{:S(2)}) collective-permute-start(bf16[256,512]{1,0:T(8,128)(2,1)} %refs_0_.5), channel_id=1, source_target_pairs={{0,8},{8,16},{16,24},{24,28},{28,20},{20,12},{12,4},{4,0},{1,9},{9... | collective-permute-start | bytes 786440 | tf_op jit(solution)/shard_map/ppermute | solution.py:67
  7.1 3.2 %collective-permute-done.refs_1_ = bf16[256,512]{1,0:T(8,128)(2,1)S(1)} collective-permute-done((bf16[256,512]{1,0:T(8,128)(2,1)}, bf16[256,512]{1,0:T(8,128)(2,1)S(1)}, u32[]{:S(2)}, u32[]{:S(2)}) %collective-permute-start) | collective-permute-done | bytes 262176 | tf_op jit(solution)/shard_map/ppermute | solution.py:67
  10.3 2.1 %collective-permute-start.18 = (bf16[256,512]{1,0:T(8,128)(2,1)}, bf16[256,512]{1,0:T(8,128)(2,1)S(1)}, u32[]{:S(2)}, u32[]{:S(2)}) collective-permute-start(bf16[256,512]{1,0:T(8,128)(2,1)} %refs_0_.5), channel_id=1, source_target_pairs={{8,0},{16,8},{24,16},{28,24},{20,28},{12,20},{4,12},{0,4},{9,1},{1... | collective-permute-start | bytes 786440 | tf_op jit(solution)/shard_map/ppermute | solution.py:67
  12.5 1.6 %collective-permute-start.2 = (bf16[256,512]{1,0:T(8,128)(2,1)S(1)}, bf16[256,512]{1,0:T(8,128)(2,1)S(1)}, u32[]{:S(2)}, u32[]{:S(2)}) collective-permute-start(bf16[256,512]{1,0:T(8,128)(2,1)S(1)} %collective-permute-done.refs_1_), channel_id=1, source_target_pairs={{0,8},{8,16},{16,24},{24,28},{28,20},{20,12},{12,4},{4,0},{1,9},{9... | collective-permute-start | bytes 786440 | tf_op jit(solution)/shard_map/ppermute | solution.py:67
  14.0 1.9 %collective-permute-done.7.refs_9_ = bf16[256,512]{1,0:T(8,128)(2,1)S(1)} collective-permute-done((bf16[256,512]{1,0:T(8,128)(2,1)}, bf16[256,512]{1,0:T(8,128)(2,1)S(1)}, u32[]{:S(2)}, u32[]{:S(2)}) %collective-permute-start.7) | collective-permute-done | bytes 262176 | tf_op jit(solution)/shard_map/ppermute | solution.py:67
  15.9 2.1 %collective-permute-start.3 = (bf16[256,512]{1,0:T(8,128)(2,1)S(1)}, bf16[256,512]{1,0:T(8,128)(2,1)S(1)}, u32[]{:S(2)}, u32[]{:S(2)}) collective-permute-start(bf16[256,512]{1,0:T(8,128)(2,1)S(1)} %collective-permute-done.1.refs_2_), channel_id=1, source_target_pairs={{8,0},{16,8},{24,16},{28,24},{20,28},{12,20},{4,12},{0,4},{9,1},{1... | collective-permute-start | bytes 786440 | tf_op jit(solution)/shard_map/ppermute | solution.py:67
  18.1 1.6 %collective-permute-start.9 = (bf16[256,512]{1,0:T(8,128)(2,1)S(1)}, bf16[256,512]{1,0:T(8,128)(2,1)S(1)}, u32[]{:S(2)}, u32[]{:S(2)}) collective-permute-start(bf16[256,512]{1,0:T(8,128)(2,1)S(1)} %collective-permute-done.7.refs_9_), channel_id=1, source_target_pairs={{0,8},{8,16},{16,24},{24,28},{28,20},{20,12},{12,4},{4,0},{1,9},{9... | collective-permute-start | bytes 786440 | tf_op jit(solution)/shard_map/ppermute | solution.py:67
  19.7 1.9 %collective-permute-done.17.refs_1_ = bf16[256,512]{1,0:T(8,128)(2,1)S(1)} collective-permute-done((bf16[256,512]{1,0:T(8,128)(2,1)}, bf16[256,512]{1,0:T(8,128)(2,1)S(1)}, u32[]{:S(2)}, u32[]{:S(2)}) %collective-permute-start.17) | collective-permute-done | bytes 262176 | tf_op jit(solution)/shard_map/ppermute | solution.py:67
  21.5 2.1 %collective-permute-start.10 = (bf16[256,512]{1,0:T(8,128)(2,1)S(1)}, bf16[256,512]{1,0:T(8,128)(2,1)}, u32[]{:S(2)}, u32[]{:S(2)}) collective-permute-start(bf16[256,512]{1,0:T(8,128)(2,1)S(1)} %collective-permute-done.8.refs_10_), channel_id=1, source_target_pairs={{8,0},{16,8},{24,16},{28,24},{20,28},{12,20},{4,12},{0,4},{9,1},{1... | collective-permute-start | bytes 786440 | tf_op jit(solution)/shard_map/ppermute | solution.py:67
  23.7 1.6 %collective-permute-start.19 = (bf16[256,512]{1,0:T(8,128)(2,1)S(1)}, bf16[256,512]{1,0:T(8,128)(2,1)S(1)}, u32[]{:S(2)}, u32[]{:S(2)}) collective-permute-start(bf16[256,512]{1,0:T(8,128)(2,1)S(1)} %collective-permute-done.17.refs_1_), channel_id=1, source_target_pairs={{0,8},{8,16},{16,24},{24,28},{28,20},{20,12},{12,4},{4,0},{1,9},{9... | collective-permute-start | bytes 786440 | tf_op jit(solution)/shard_map/ppermute | solution.py:67
  25.3 1.9 %collective-permute-done.2.refs_3_ = bf16[256,512]{1,0:T(8,128)(2,1)S(1)} collective-permute-done((bf16[256,512]{1,0:T(8,128)(2,1)S(1)}, bf16[256,512]{1,0:T(8,128)(2,1)S(1)}, u32[]{:S(2)}, u32[]{:S(2)}) %collective-permute-start.2) | collective-permute-done | bytes 262176 | tf_op jit(solution)/shard_map/ppermute | solution.py:67
  27.2 2.1 %collective-permute-start.25 = (bf16[512,256]{1,0:T(8,128)(2,1)}, bf16[512,256]{1,0:T(8,128)(2,1)S(1)}, u32[]{:S(2)}, u32[]{:S(2)}) collective-permute-start(bf16[512,256]{1,0:T(8,128)(2,1)} %refs_0_.7), channel_id=1, source_target_pairs={{8,0},{16,8},{24,16},{28,24},{20,28},{12,20},{4,12},{0,4},{9,1},{1... | collective-permute-start | bytes 786440 | tf_op jit(solution)/shard_map/ppermute | solution.py:67
  29.2 2.2 %copy.7 = f32[4,13,512]{1,2,0:T(8,128)} copy(f32[4,13,512]{2,0,1:T(4,128)} %param.11) | data formatting | bytes 212992 | tf_op args[5]
  31.5 4.5 %shard_map.64.mixing = bf16[4,512,512]{2,1,0:T(8,128)(2,1)} custom-call(f32[4,512,13]{2,1,0:T(8,128)} %bitcast.22), custom_call_target="tpu_custom_call" | custom-call | flops 1 | bytes 8814592 | tf_op jit(solution)/shard_map/pallas_call | solution.py:23
  36.2 2.0 %collective-permute-start.4 = (bf16[256,512]{1,0:T(8,128)(2,1)S(1)}, bf16[256,512]{1,0:T(8,128)(2,1)S(1)}, u32[]{:S(2)}, u32[]{:S(2)}) collective-permute-start(bf16[256,512]{1,0:T(8,128)(2,1)S(1)} %collective-permute-done.2.refs_3_), channel_id=1, source_target_pairs={{0,8},{8,16},{16,24},{24,28},{28,20},{20,12},{12,4},{4,0},{1,9},{9... | collective-permute-start | bytes 786440 | tf_op jit(solution)/shard_map/ppermute | solution.py:67
  38.4 2.1 %collective-permute-start.5 = (bf16[256,512]{1,0:T(8,128)(2,1)S(1)}, bf16[256,512]{1,0:T(8,128)(2,1)}, u32[]{:S(2)}, u32[]{:S(2)}) collective-permute-start(bf16[256,512]{1,0:T(8,128)(2,1)S(1)} %collective-permute-done.3.refs_4_), channel_id=1, source_target_pairs={{8,0},{16,8},{24,16},{28,24},{20,28},{12,20},{4,12},{0,4},{9,1},{1... | collective-permute-start | bytes 786440 | tf_op jit(solution)/shard_map/ppermute | solution.py:67
  40.5 1.6 %collective-permute-start.27 = (bf16[512,256]{1,0:T(8,128)(2,1)S(1)}, bf16[512,256]{1,0:T(8,128)(2,1)S(1)}, u32[]{:S(2)}, u32[]{:S(2)}) collective-permute-start(bf16[512,256]{1,0:T(8,128)(2,1)S(1)} %collective-permute-done.25.refs_2_), channel_id=1, source_target_pairs={{8,0},{16,8},{24,16},{28,24},{20,28},{12,20},{4,12},{0,4},{9,1},{1... | collective-permute-start | bytes 786440 | tf_op jit(solution)/shard_map/ppermute | solution.py:67
  42.0 3.2 %collective-permute-done.24.refs_1_ = bf16[512,256]{1,0:T(8,128)(2,1)S(1)} collective-permute-done((bf16[512,256]{1,0:T(8,128)(2,1)S(1)}, bf16[512,256]{1,0:T(8,128)(2,1)S(1)}, u32[]{:S(2)}, u32[]{:S(2)}) %collective-permute-start.24) | collective-permute-done | bytes 262176 | tf_op jit(solution)/shard_map/ppermute | solution.py:67
  46.1 4.8 %collective-permute-done.4.refs_5_ = bf16[256,512]{1,0:T(8,128)(2,1)S(1)} collective-permute-done((bf16[256,512]{1,0:T(8,128)(2,1)S(1)}, bf16[256,512]{1,0:T(8,128)(2,1)S(1)}, u32[]{:S(2)}, u32[]{:S(2)}) %collective-permute-start.4) | collective-permute-done | bytes 262176 | tf_op jit(solution)/shard_map/ppermute | solution.py:67
  50.9 0.9 collective-permute-start.6
  51.8 1.2 collective-permute-start.13
  53.4 1.2 collective-permute-start.20
  54.5 4.4 %collective-permute-done.27.refs_4_ = bf16[512,256]{1,0:T(8,128)(2,1)S(1)} collective-permute-done((bf16[512,256]{1,0:T(8,128)(2,1)S(1)}, bf16[512,256]{1,0:T(8,128)(2,1)S(1)}, u32[]{:S(2)}, u32[]{:S(2)}) %collective-permute-start.27) | collective-permute-done | bytes 262176 | tf_op jit(solution)/shard_map/ppermute | solution.py:67
  59.0 1.9 %collective-permute-start.21 = (bf16[256,512]{1,0:T(8,128)(2,1)S(1)}, bf16[256,512]{1,0:T(8,128)(2,1)}, u32[]{:S(2)}, u32[]{:S(2)}) collective-permute-start(bf16[256,512]{1,0:T(8,128)(2,1)S(1)} %collective-permute-done.19.refs_3_), channel_id=1, source_target_pairs={{0,8},{8,16},{16,24},{24,28},{28,20},{20,12},{12,4},{4,0},{1,9},{9... | collective-permute-start | bytes 786440 | tf_op jit(solution)/shard_map/ppermute | solution.py:67
  60.9 1.2 %collective-permute-done.6.refs_7_ = bf16[256,512]{1,0:T(8,128)(2,1)S(1)} collective-permute-done((bf16[256,512]{1,0:T(8,128)(2,1)S(1)}, bf16[256,512]{1,0:T(8,128)(2,1)S(1)}, u32[]{:S(2)}, u32[]{:S(2)}) %collective-permute-start.6) | collective-permute-done | bytes 262176 | tf_op jit(solution)/shard_map/ppermute | solution.py:67
  62.1 0.9 collective-permute-start.26
  63.7 0.9 collective-permute-done.13.refs_15_
  64.6 6.9 %shard_map.65 = (bf16[512,512]{1,0:T(8,128)(2,1)}, bf16[512,512]{1,0:T(8,128)(2,1)}, f32[4,128,128]{2,1,0:T(8,128)}, bf16[4,128,128]{2,1,0:T(8,128)(2,1)}) custom-call(s32[2,8]{1,0:T(2,128)} %stack.103.starts, bf16[512,2048]{1,0:T(8,128)(2,1)} %tokens.2, bf16[256,512]{1,0:T(8,128)(2,1)} %refs_0_.4, bf16[256,512]{1,0:T(8,128)(2,1)} %copy-done.10, ...), custom_call_target="tpu_custom_call" | custom-call | flops 1 | bytes 30933248 | tf_op jit(solution)/shard_map/pallas_call | solution.py:23
  71.5 1.6 %collective-permute-start.16 = (bf16[4,128,128]{2,1,0:T(8,128)(2,1)}, bf16[4,128,128]{2,1,0:T(8,128)(2,1)S(1)}, u32[]{:S(2)}, u32[]{:S(2)}) collective-permute-start(bf16[4,128,128]{2,1,0:T(8,128)(2,1)} %get-tuple-element.25), channel_id=1, source_target_pairs={{0,12},{4,8},{8,4},{12,0},{16,28},{20,24},{24,20},{28,16},{1,13},{... | collective-permute-start | bytes 393224 | tf_op jit(solution)/shard_map/ppermute | solution.py:387
  73.6 1.0 collective-permute-done.29.refs_6_
  75.1 1.6 %collective-permute-start.22 = (bf16[256,512]{1,0:T(8,128)(2,1)S(1)}, bf16[256,512]{1,0:T(8,128)(2,1)S(1)}, u32[]{:S(2)}, u32[]{:S(2)}) collective-permute-start(bf16[256,512]{1,0:T(8,128)(2,1)S(1)} %collective-permute-done.20.refs_4_), channel_id=1, source_target_pairs={{8,0},{16,8},{24,16},{28,24},{20,28},{12,20},{4,12},{0,4},{9,1},{1... | collective-permute-start | bytes 786440 | tf_op jit(solution)/shard_map/ppermute | solution.py:67
  77.1 2.0 %collective-permute-done.16.refs_10_ = bf16[4,128,128]{2,1,0:T(8,128)(2,1)S(1)} collective-permute-done((bf16[4,128,128]{2,1,0:T(8,128)(2,1)}, bf16[4,128,128]{2,1,0:T(8,128)(2,1)S(1)}, u32[]{:S(2)}, u32[]{:S(2)}) %collective-permute-start.16) | collective-permute-done | bytes 131104 | tf_op jit(solution)/shard_map/ppermute | solution.py:387
  79.1 1.6 %collective-permute-start.28 = (bf16[512,256]{1,0:T(8,128)(2,1)S(1)}, bf16[512,256]{1,0:T(8,128)(2,1)S(1)}, u32[]{:S(2)}, u32[]{:S(2)}) collective-permute-start(bf16[512,256]{1,0:T(8,128)(2,1)S(1)} %collective-permute-done.26.refs_3_), channel_id=1, source_target_pairs={{0,8},{8,16},{16,24},{24,28},{28,20},{20,12},{12,4},{4,0},{1,9},{9... | collective-permute-start | bytes 786440 | tf_op jit(solution)/shard_map/ppermute | solution.py:67
  81.0 1.5 %collective-permute-start.30 = (bf16[512,256]{1,0:T(8,128)(2,1)S(1)}, bf16[512,256]{1,0:T(8,128)(2,1)S(1)}, u32[]{:S(2)}, u32[]{:S(2)}) collective-permute-start(bf16[512,256]{1,0:T(8,128)(2,1)S(1)} %collective-permute-done.29.refs_6_), channel_id=1, source_target_pairs={{8,0},{16,8},{24,16},{28,24},{20,28},{12,20},{4,12},{0,4},{9,1},{1... | collective-permute-start | bytes 786440 | tf_op jit(solution)/shard_map/ppermute | solution.py:67
  82.5 1.0 convert_add_fusion
  83.5 1.6 %collective-permute-start.31 = (bf16[4,128,128]{2,1,0:T(8,128)(2,1)S(1)}, bf16[4,128,128]{2,1,0:T(8,128)(2,1)S(1)}, u32[]{:S(2)}, u32[]{:S(2)}) collective-permute-start(bf16[4,128,128]{2,1,0:T(8,128)(2,1)S(1)} %convert_add_fusion), channel_id=1, source_target_pairs={{0,16},{4,20},{8,24},{12,28},{16,0},{20,4},{24,8},{28,12},{1,17},{... | collective-permute-start | bytes 393224 | tf_op jit(solution)/shard_map/ppermute | solution.py:387
  85.3 2.7 %collective-permute-done.22.refs_6_ = bf16[256,512]{1,0:T(8,128)(2,1)S(1)} collective-permute-done((bf16[256,512]{1,0:T(8,128)(2,1)S(1)}, bf16[256,512]{1,0:T(8,128)(2,1)S(1)}, u32[]{:S(2)}, u32[]{:S(2)}) %collective-permute-start.22) | collective-permute-done | bytes 262176 | tf_op jit(solution)/shard_map/ppermute | solution.py:67
  88.8 7.3 %shard_map.66 = (bf16[512,512]{1,0:T(8,128)(2,1)}, f32[512,512]{1,0:T(8,128)}) custom-call(s32[2,8]{1,0:T(2,128)} %stack.103.starts, bf16[512,2048]{1,0:T(8,128)(2,1)} %tokens.2, bf16[512,512]{1,0:T(8,128)(2,1)} %get-tuple-element.27.keys, bf16[512,512]{1,0:T(8,128)(2,1)} %get-tuple-element.28.values, bf16[4,512,512]{2,1,0:T(8,128)(2,1)} %shard_map.64.mixing, ...), custom_call_target="tpu_custom_call" | custom-call | flops 1 | bytes 35651840 | tf_op jit(solution)/shard_map/pallas_call | solution.py:23
  96.1 1.2 %copy-done.2 = f32[512,512]{1,0:T(8,128)S(1)} copy-done((f32[512,512]{1,0:T(8,128)S(1)}, f32[512,512]{1,0:T(8,128)}, u32[]{:S(2)}) %copy-start.2) | copy-done | bytes 1048600
  97.4 1.0 copy-done.3
  98.4 4.5 %shard_map.67 = (bf16[512,512]{1,0:T(8,128)(2,1)S(1)}, bf16[512,512]{1,0:T(8,128)(2,1)S(1)}, bf16[512,512]{1,0:T(8,128)(2,1)S(1)}) custom-call(f32[3]{0:T(128)S(1)} %add_convert_fusion.2.upper, s32[2,8]{1,0:T(2,128)S(1)} %stack.88.starts, bf16[512,512]{1,0:T(8,128)(2,1)S(1)} %copy-done.3, f32[512,512]{1,0:T(8,128)S(1)} %copy-done.2, ...), custom_call_target="tpu_custom_call" | custom-call | flops 1 | bytes 23494960 | tf_op jit(solution)/shard_map/pallas_call | solution.py:23
  103.0 1.9 %collective-permute-done.32 = bf16[512,512]{1,0:T(8,128)(2,1)S(1)} collective-permute-done((bf16[512,512]{1,0:T(8,128)(2,1)S(1)}, bf16[512,512]{1,0:T(8,128)(2,1)S(1)}, u32[]{:S(2)}, u32[]{:S(2)}) %collective-permute-start.32) | collective-permute-done | bytes 524320 | tf_op jit(solution)/shard_map/ppermute | solution.py:414
  105.0 1.5 %collective-permute-start.34 = (bf16[512,512]{1,0:T(8,128)(2,1)S(1)}, bf16[512,512]{1,0:T(8,128)(2,1)S(1)}, u32[]{:S(2)}, u32[]{:S(2)}) collective-permute-start(bf16[512,512]{1,0:T(8,128)(2,1)S(1)} %add_convert_fusion.1), channel_id=1, source_target_pairs={{0,2},{1,3},{2,0},{3,1},{4,6},{5,7},{6,4},{7,5},{8,10},{9,11},{10,... | collective-permute-start | bytes 1572872 | tf_op jit(solution)/shard_map/ppermute | solution.py:414
  106.5 1.5 %shard_map.68 = (bf16[512,512]{1,0:T(8,128)(2,1)S(1)}, bf16[512,512]{1,0:T(8,128)(2,1)S(1)}) custom-call(s32[2,8]{1,0:T(2,128)S(1)} %stack.88.starts, bf16[512,512]{1,0:T(8,128)(2,1)S(1)} %get-tuple-element.36.attended, bf16[512,256]{1,0:T(8,128)(2,1)S(1)} %copy-done.1, bf16[512,256]{1,0:T(8,128)(2,1)S(1)} %collective-permute-done.24.refs_1_, ...), custom_call_target="tpu_custom_call" | custom-call | flops 1 | bytes 14680320 | tf_op jit(solution)/shard_map/pallas_call | solution.py:23
  108.2 10.9 %collective-permute-done.34 = bf16[512,512]{1,0:T(8,128)(2,1)S(1)} collective-permute-done((bf16[512,512]{1,0:T(8,128)(2,1)S(1)}, bf16[512,512]{1,0:T(8,128)(2,1)S(1)}, u32[]{:S(2)}, u32[]{:S(2)}) %collective-permute-start.34) | collective-permute-done | bytes 524320 | tf_op jit(solution)/shard_map/ppermute | solution.py:414
  119.0 1.0 add_convert_fusion
  (78 shorter events, 5.8 us)
Async XLA Ops:
  0.0 36.0 %copy-start.1 = (bf16[512,256]{1,0:T(8,128)(2,1)S(1)}, bf16[512,256]{1,0:T(8,128)(2,1)}, u32[]{:S(2)}) copy-start(bf16[512,256]{1,0:T(8,128)(2,1)} %refs_0_.7) | copy-start | bytes 786436
  0.0 10.3 %collective-permute-start = (bf16[256,512]{1,0:T(8,128)(2,1)}, bf16[256,512]{1,0:T(8,128)(2,1)S(1)}, u32[]{:S(2)}, u32[]{:S(2)}) collective-permute-start(bf16[256,512]{1,0:T(8,128)(2,1)} %refs_0_.4), channel_id=1, source_target_pairs={{0,8},{8,16},{16,24},{24,28},{28,20},{20,12},{12,4},{4,0},{1,9},{9... | collective-permute-start | bytes 786440 | tf_op jit(solution)/shard_map/ppermute | solution.py:67
  3.0 9.4 %collective-permute-start.1 = (bf16[256,512]{1,0:T(8,128)(2,1)}, bf16[256,512]{1,0:T(8,128)(2,1)S(1)}, u32[]{:S(2)}, u32[]{:S(2)}) collective-permute-start(bf16[256,512]{1,0:T(8,128)(2,1)} %refs_0_.4), channel_id=1, source_target_pairs={{8,0},{16,8},{24,16},{28,24},{20,28},{12,20},{4,12},{0,4},{9,1},{1... | collective-permute-start | bytes 786440 | tf_op jit(solution)/shard_map/ppermute | solution.py:67
  3.0 12.9 %collective-permute-start.7 = (bf16[256,512]{1,0:T(8,128)(2,1)}, bf16[256,512]{1,0:T(8,128)(2,1)S(1)}, u32[]{:S(2)}, u32[]{:S(2)}) collective-permute-start(bf16[256,512]{1,0:T(8,128)(2,1)} %refs_8_.1), channel_id=1, source_target_pairs={{0,8},{8,16},{16,24},{24,28},{28,20},{20,12},{12,4},{4,0},{1,9},{9... | collective-permute-start | bytes 786440 | tf_op jit(solution)/shard_map/ppermute | solution.py:67
  5.1 13.0 %collective-permute-start.8 = (bf16[256,512]{1,0:T(8,128)(2,1)}, bf16[256,512]{1,0:T(8,128)(2,1)S(1)}, u32[]{:S(2)}, u32[]{:S(2)}) collective-permute-start(bf16[256,512]{1,0:T(8,128)(2,1)} %refs_8_.1), channel_id=1, source_target_pairs={{8,0},{16,8},{24,16},{28,24},{20,28},{12,20},{4,12},{0,4},{9,1},{1... | collective-permute-start | bytes 786440 | tf_op jit(solution)/shard_map/ppermute | solution.py:67
  5.1 16.5 %collective-permute-start.17 = (bf16[256,512]{1,0:T(8,128)(2,1)}, bf16[256,512]{1,0:T(8,128)(2,1)S(1)}, u32[]{:S(2)}, u32[]{:S(2)}) collective-permute-start(bf16[256,512]{1,0:T(8,128)(2,1)} %refs_0_.5), channel_id=1, source_target_pairs={{0,8},{8,16},{16,24},{24,28},{28,20},{20,12},{12,4},{4,0},{1,9},{9... | collective-permute-start | bytes 786440 | tf_op jit(solution)/shard_map/ppermute | solution.py:67
  10.3 25.6 %copy-start.10 = (bf16[256,512]{1,0:T(8,128)(2,1)}, bf16[256,512]{1,0:T(8,128)(2,1)S(1)}, u32[]{:S(2)}) copy-start(bf16[256,512]{1,0:T(8,128)(2,1)S(1)} %collective-permute-done.refs_1_) | copy-start | bytes 786436
  10.3 13.4 %collective-permute-start.18 = (bf16[256,512]{1,0:T(8,128)(2,1)}, bf16[256,512]{1,0:T(8,128)(2,1)S(1)}, u32[]{:S(2)}, u32[]{:S(2)}) collective-permute-start(bf16[256,512]{1,0:T(8,128)(2,1)} %refs_0_.5), channel_id=1, source_target_pairs={{8,0},{16,8},{24,16},{28,24},{20,28},{12,20},{4,12},{0,4},{9,1},{1... | collective-permute-start | bytes 786440 | tf_op jit(solution)/shard_map/ppermute | solution.py:67
  12.5 23.5 %copy-start.11 = (bf16[256,512]{1,0:T(8,128)(2,1)}, bf16[256,512]{1,0:T(8,128)(2,1)S(1)}, u32[]{:S(2)}) copy-start(bf16[256,512]{1,0:T(8,128)(2,1)S(1)} %collective-permute-done.1.refs_2_) | copy-start | bytes 786436
  12.5 14.7 %collective-permute-start.2 = (bf16[256,512]{1,0:T(8,128)(2,1)S(1)}, bf16[256,512]{1,0:T(8,128)(2,1)S(1)}, u32[]{:S(2)}, u32[]{:S(2)}) collective-permute-start(bf16[256,512]{1,0:T(8,128)(2,1)S(1)} %collective-permute-done.refs_1_), channel_id=1, source_target_pairs={{0,8},{8,16},{16,24},{24,28},{28,20},{20,12},{12,4},{4,0},{1,9},{9... | collective-permute-start | bytes 786440 | tf_op jit(solution)/shard_map/ppermute | solution.py:67
  15.9 20.0 %copy-start.12 = (bf16[256,512]{1,0:T(8,128)(2,1)}, bf16[256,512]{1,0:T(8,128)(2,1)S(1)}, u32[]{:S(2)}) copy-start(bf16[256,512]{1,0:T(8,128)(2,1)S(1)} %collective-permute-done.7.refs_9_) | copy-start | bytes 786436
  15.9 20.0 %collective-permute-start.3 = (bf16[256,512]{1,0:T(8,128)(2,1)S(1)}, bf16[256,512]{1,0:T(8,128)(2,1)S(1)}, u32[]{:S(2)}, u32[]{:S(2)}) collective-permute-start(bf16[256,512]{1,0:T(8,128)(2,1)S(1)} %collective-permute-done.1.refs_2_), channel_id=1, source_target_pairs={{8,0},{16,8},{24,16},{28,24},{20,28},{12,20},{4,12},{0,4},{9,1},{1... | collective-permute-start | bytes 786440 | tf_op jit(solution)/shard_map/ppermute | solution.py:67
  18.1 17.9 %copy-start.13 = (bf16[256,512]{1,0:T(8,128)(2,1)}, bf16[256,512]{1,0:T(8,128)(2,1)S(1)}, u32[]{:S(2)}) copy-start(bf16[256,512]{1,0:T(8,128)(2,1)S(1)} %collective-permute-done.8.refs_10_) | copy-start | bytes 786436
  18.1 18.1 %collective-permute-start.9 = (bf16[256,512]{1,0:T(8,128)(2,1)S(1)}, bf16[256,512]{1,0:T(8,128)(2,1)S(1)}, u32[]{:S(2)}, u32[]{:S(2)}) collective-permute-start(bf16[256,512]{1,0:T(8,128)(2,1)S(1)} %collective-permute-done.7.refs_9_), channel_id=1, source_target_pairs={{0,8},{8,16},{16,24},{24,28},{28,20},{20,12},{12,4},{4,0},{1,9},{9... | collective-permute-start | bytes 786440 | tf_op jit(solution)/shard_map/ppermute | solution.py:67
  21.5 14.4 %copy-start.4 = (bf16[256,512]{1,0:T(8,128)(2,1)}, bf16[256,512]{1,0:T(8,128)(2,1)S(1)}, u32[]{:S(2)}) copy-start(bf16[256,512]{1,0:T(8,128)(2,1)S(1)} %collective-permute-done.17.refs_1_) | copy-start | bytes 786436
  21.5 16.6 %collective-permute-start.10 = (bf16[256,512]{1,0:T(8,128)(2,1)S(1)}, bf16[256,512]{1,0:T(8,128)(2,1)}, u32[]{:S(2)}, u32[]{:S(2)}) collective-permute-start(bf16[256,512]{1,0:T(8,128)(2,1)S(1)} %collective-permute-done.8.refs_10_), channel_id=1, source_target_pairs={{8,0},{16,8},{24,16},{28,24},{20,28},{12,20},{4,12},{0,4},{9,1},{1... | collective-permute-start | bytes 786440 | tf_op jit(solution)/shard_map/ppermute | solution.py:67
  23.7 29.7 %copy-start.5 = (bf16[256,512]{1,0:T(8,128)(2,1)}, bf16[256,512]{1,0:T(8,128)(2,1)S(1)}, u32[]{:S(2)}) copy-start(bf16[256,512]{1,0:T(8,128)(2,1)S(1)} %collective-permute-done.18.refs_2_) | copy-start | bytes 786436
  23.7 14.7 %collective-permute-start.19 = (bf16[256,512]{1,0:T(8,128)(2,1)S(1)}, bf16[256,512]{1,0:T(8,128)(2,1)S(1)}, u32[]{:S(2)}, u32[]{:S(2)}) collective-permute-start(bf16[256,512]{1,0:T(8,128)(2,1)S(1)} %collective-permute-done.17.refs_1_), channel_id=1, source_target_pairs={{0,8},{8,16},{16,24},{24,28},{28,20},{20,12},{12,4},{4,0},{1,9},{9... | collective-permute-start | bytes 786440 | tf_op jit(solution)/shard_map/ppermute | solution.py:67
  27.2 13.3 %collective-permute-start.25 = (bf16[512,256]{1,0:T(8,128)(2,1)}, bf16[512,256]{1,0:T(8,128)(2,1)S(1)}, u32[]{:S(2)}, u32[]{:S(2)}) collective-permute-start(bf16[512,256]{1,0:T(8,128)(2,1)} %refs_0_.7), channel_id=1, source_target_pairs={{8,0},{16,8},{24,16},{28,24},{20,28},{12,20},{4,12},{0,4},{9,1},{1... | collective-permute-start | bytes 786440 | tf_op jit(solution)/shard_map/ppermute | solution.py:67
  36.0 24.9 %copy-start.15 = (bf16[256,512]{1,0:T(8,128)(2,1)}, bf16[256,512]{1,0:T(8,128)(2,1)S(1)}, u32[]{:S(2)}) copy-start(bf16[256,512]{1,0:T(8,128)(2,1)S(1)} %collective-permute-done.3.refs_4_) | copy-start | bytes 786436
  36.0 9.3 %collective-permute-start.24 = (bf16[512,256]{1,0:T(8,128)(2,1)S(1)}, bf16[512,256]{1,0:T(8,128)(2,1)S(1)}, u32[]{:S(2)}, u32[]{:S(2)}) collective-permute-start(bf16[512,256]{1,0:T(8,128)(2,1)S(1)} %copy-done.1), channel_id=1, source_target_pairs={{0,8},{8,16},{16,24},{24,28},{28,20},{20,12},{12,4},{4,0},{1,9},{9... | collective-permute-start | bytes 786440 | tf_op jit(solution)/shard_map/ppermute | solution.py:67
  36.2 28.4 %copy-start.16 = (bf16[256,512]{1,0:T(8,128)(2,1)}, bf16[256,512]{1,0:T(8,128)(2,1)S(1)}, u32[]{:S(2)}) copy-start(bf16[256,512]{1,0:T(8,128)(2,1)S(1)} %collective-permute-done.9.refs_11_) | copy-start | bytes 786436
  36.2 14.7 %collective-permute-start.4 = (bf16[256,512]{1,0:T(8,128)(2,1)S(1)}, bf16[256,512]{1,0:T(8,128)(2,1)S(1)}, u32[]{:S(2)}, u32[]{:S(2)}) collective-permute-start(bf16[256,512]{1,0:T(8,128)(2,1)S(1)} %collective-permute-done.2.refs_3_), channel_id=1, source_target_pairs={{0,8},{8,16},{16,24},{24,28},{28,20},{20,12},{12,4},{4,0},{1,9},{9... | collective-permute-start | bytes 786440 | tf_op jit(solution)/shard_map/ppermute | solution.py:67
  38.2 13.6 %collective-permute-start.12 = (bf16[256,512]{1,0:T(8,128)(2,1)}, bf16[256,512]{1,0:T(8,128)(2,1)S(1)}, u32[]{:S(2)}, u32[]{:S(2)}) collective-permute-start(bf16[256,512]{1,0:T(8,128)(2,1)} %collective-permute-done.10.refs_12_), channel_id=1, source_target_pairs={{8,0},{16,8},{24,16},{28,24},{20,28},{12,20},{4,12},{0,4},{9,1},{1... | collective-permute-start | bytes 786440 | tf_op jit(solution)/shard_map/ppermute | solution.py:67
  38.4 33.1 %copy-start.6 = (bf16[256,512]{1,0:T(8,128)(2,1)}, bf16[256,512]{1,0:T(8,128)(2,1)S(1)}, u32[]{:S(2)}) copy-start(bf16[256,512]{1,0:T(8,128)(2,1)S(1)} %collective-permute-done.19.refs_3_) | copy-start | bytes 786436
  38.4 15.0 %collective-permute-start.5 = (bf16[256,512]{1,0:T(8,128)(2,1)S(1)}, bf16[256,512]{1,0:T(8,128)(2,1)}, u32[]{:S(2)}, u32[]{:S(2)}) collective-permute-start(bf16[256,512]{1,0:T(8,128)(2,1)S(1)} %collective-permute-done.3.refs_4_), channel_id=1, source_target_pairs={{8,0},{16,8},{24,16},{28,24},{20,28},{12,20},{4,12},{0,4},{9,1},{1... | collective-permute-start | bytes 786440 | tf_op jit(solution)/shard_map/ppermute | solution.py:67
  40.5 18.4 %collective-permute-start.27 = (bf16[512,256]{1,0:T(8,128)(2,1)S(1)}, bf16[512,256]{1,0:T(8,128)(2,1)S(1)}, u32[]{:S(2)}, u32[]{:S(2)}) collective-permute-start(bf16[512,256]{1,0:T(8,128)(2,1)S(1)} %collective-permute-done.25.refs_2_), channel_id=1, source_target_pairs={{8,0},{16,8},{24,16},{28,24},{20,28},{12,20},{4,12},{0,4},{9,1},{1... | collective-permute-start | bytes 786440 | tf_op jit(solution)/shard_map/ppermute | solution.py:67
  45.3 13.7 %collective-permute-start.11 = (bf16[256,512]{1,0:T(8,128)(2,1)S(1)}, bf16[256,512]{1,0:T(8,128)(2,1)S(1)}, u32[]{:S(2)}, u32[]{:S(2)}) collective-permute-start(bf16[256,512]{1,0:T(8,128)(2,1)S(1)} %collective-permute-done.9.refs_11_), channel_id=1, source_target_pairs={{0,8},{8,16},{16,24},{24,28},{28,20},{20,12},{12,4},{4,0},{1,9},{9... | collective-permute-start | bytes 786440 | tf_op jit(solution)/shard_map/ppermute | solution.py:67
  50.9 13.7 %copy-start.17 = (bf16[256,512]{1,0:T(8,128)(2,1)}, bf16[256,512]{1,0:T(8,128)(2,1)S(1)}, u32[]{:S(2)}) copy-start(bf16[256,512]{1,0:T(8,128)(2,1)S(1)} %collective-permute-done.4.refs_5_) | copy-start | bytes 786436
  50.9 11.2 %collective-permute-start.6 = (bf16[256,512]{1,0:T(8,128)(2,1)S(1)}, bf16[256,512]{1,0:T(8,128)(2,1)S(1)}, u32[]{:S(2)}, u32[]{:S(2)}) collective-permute-start(bf16[256,512]{1,0:T(8,128)(2,1)S(1)} %collective-permute-done.4.refs_5_), channel_id=1, source_target_pairs={{0,8},{8,16},{16,24},{24,28},{28,20},{20,12},{12,4},{4,0},{1,9},{9... | collective-permute-start | bytes 786440 | tf_op jit(solution)/shard_map/ppermute | solution.py:67
  51.8 12.8 %copy-start.18 = (bf16[256,512]{1,0:T(8,128)(2,1)}, bf16[256,512]{1,0:T(8,128)(2,1)S(1)}, u32[]{:S(2)}) copy-start(bf16[256,512]{1,0:T(8,128)(2,1)S(1)} %collective-permute-done.12.refs_14_) | copy-start | bytes 786436
  51.8 12.8 %collective-permute-start.13 = (bf16[256,512]{1,0:T(8,128)(2,1)S(1)}, bf16[256,512]{1,0:T(8,128)(2,1)}, u32[]{:S(2)}, u32[]{:S(2)}) collective-permute-start(bf16[256,512]{1,0:T(8,128)(2,1)S(1)} %collective-permute-done.12.refs_14_), channel_id=1, source_target_pairs={{8,0},{16,8},{24,16},{28,24},{20,28},{12,20},{4,12},{0,4},{9,1},{1... | collective-permute-start | bytes 786440 | tf_op jit(solution)/shard_map/ppermute | solution.py:67
  53.4 19.8 %collective-permute-start.20 = (bf16[256,512]{1,0:T(8,128)(2,1)S(1)}, bf16[256,512]{1,0:T(8,128)(2,1)S(1)}, u32[]{:S(2)}, u32[]{:S(2)}) collective-permute-start(bf16[256,512]{1,0:T(8,128)(2,1)S(1)} %collective-permute-done.18.refs_2_), channel_id=1, source_target_pairs={{8,0},{16,8},{24,16},{28,24},{20,28},{12,20},{4,12},{0,4},{9,1},{1... | collective-permute-start | bytes 786440 | tf_op jit(solution)/shard_map/ppermute | solution.py:67
  58.9 15.7 %collective-permute-start.29 = (bf16[512,256]{1,0:T(8,128)(2,1)S(1)}, bf16[512,256]{1,0:T(8,128)(2,1)S(1)}, u32[]{:S(2)}, u32[]{:S(2)}) collective-permute-start(bf16[512,256]{1,0:T(8,128)(2,1)S(1)} %collective-permute-done.27.refs_4_), channel_id=1, source_target_pairs={{8,0},{16,8},{24,16},{28,24},{20,28},{12,20},{4,12},{0,4},{9,1},{1... | collective-permute-start | bytes 786440 | tf_op jit(solution)/shard_map/ppermute | solution.py:67
  59.0 16.1 %collective-permute-start.21 = (bf16[256,512]{1,0:T(8,128)(2,1)S(1)}, bf16[256,512]{1,0:T(8,128)(2,1)}, u32[]{:S(2)}, u32[]{:S(2)}) collective-permute-start(bf16[256,512]{1,0:T(8,128)(2,1)S(1)} %collective-permute-done.19.refs_3_), channel_id=1, source_target_pairs={{0,8},{8,16},{16,24},{24,28},{28,20},{20,12},{12,4},{4,0},{1,9},{9... | collective-permute-start | bytes 786440 | tf_op jit(solution)/shard_map/ppermute | solution.py:67
  62.1 14.5 %collective-permute-start.26 = (bf16[512,256]{1,0:T(8,128)(2,1)S(1)}, bf16[512,256]{1,0:T(8,128)(2,1)S(1)}, u32[]{:S(2)}, u32[]{:S(2)}) collective-permute-start(bf16[512,256]{1,0:T(8,128)(2,1)S(1)} %collective-permute-done.24.refs_1_), channel_id=1, source_target_pairs={{0,8},{8,16},{16,24},{24,28},{28,20},{20,12},{12,4},{4,0},{1,9},{9... | collective-permute-start | bytes 786440 | tf_op jit(solution)/shard_map/ppermute | solution.py:67
  71.5 7.6 %collective-permute-start.16 = (bf16[4,128,128]{2,1,0:T(8,128)(2,1)}, bf16[4,128,128]{2,1,0:T(8,128)(2,1)S(1)}, u32[]{:S(2)}, u32[]{:S(2)}) collective-permute-start(bf16[4,128,128]{2,1,0:T(8,128)(2,1)} %get-tuple-element.25), channel_id=1, source_target_pairs={{0,12},{4,8},{8,4},{12,0},{16,28},{20,24},{24,20},{28,16},{1,13},{... | collective-permute-start | bytes 393224 | tf_op jit(solution)/shard_map/ppermute | solution.py:387
  73.1 14.9 %copy-start.7 = (bf16[256,512]{1,0:T(8,128)(2,1)}, bf16[256,512]{1,0:T(8,128)(2,1)S(1)}, u32[]{:S(2)}) copy-start(bf16[256,512]{1,0:T(8,128)(2,1)S(1)} %collective-permute-done.20.refs_4_) | copy-start | bytes 786436
  73.1 7.9 %collective-permute-start.15 = (bf16[4,128,128]{2,1,0:T(8,128)(2,1)}, bf16[4,128,128]{2,1,0:T(8,128)(2,1)S(1)}, u32[]{:S(2)}, u32[]{:S(2)}) collective-permute-start(bf16[4,128,128]{2,1,0:T(8,128)(2,1)} %get-tuple-element.25), channel_id=1, source_target_pairs={{0,8},{4,12},{8,0},{12,4},{16,24},{20,28},{24,16},{28,20},{1,9},{5... | collective-permute-start | bytes 393224 | tf_op jit(solution)/shard_map/ppermute | solution.py:387
  74.6 7.9 %collective-permute-start.14 = (bf16[4,128,128]{2,1,0:T(8,128)(2,1)}, bf16[4,128,128]{2,1,0:T(8,128)(2,1)S(1)}, u32[]{:S(2)}, u32[]{:S(2)}) collective-permute-start(bf16[4,128,128]{2,1,0:T(8,128)(2,1)} %get-tuple-element.25), channel_id=1, source_target_pairs={{0,4},{4,0},{8,12},{12,8},{16,20},{20,16},{24,28},{28,24},{1,5},{5... | collective-permute-start | bytes 393224 | tf_op jit(solution)/shard_map/ppermute | solution.py:387
  75.1 13.0 %collective-permute-start.22 = (bf16[256,512]{1,0:T(8,128)(2,1)S(1)}, bf16[256,512]{1,0:T(8,128)(2,1)S(1)}, u32[]{:S(2)}, u32[]{:S(2)}) collective-permute-start(bf16[256,512]{1,0:T(8,128)(2,1)S(1)} %collective-permute-done.20.refs_4_), channel_id=1, source_target_pairs={{8,0},{16,8},{24,16},{28,24},{20,28},{12,20},{4,12},{0,4},{9,1},{1... | collective-permute-start | bytes 786440 | tf_op jit(solution)/shard_map/ppermute | solution.py:67
  76.6 11.4 %collective-permute-start.23 = (bf16[256,512]{1,0:T(8,128)(2,1)}, bf16[256,512]{1,0:T(8,128)(2,1)S(1)}, u32[]{:S(2)}, u32[]{:S(2)}) collective-permute-start(bf16[256,512]{1,0:T(8,128)(2,1)} %collective-permute-done.21.refs_5_), channel_id=1, source_target_pairs={{0,8},{8,16},{16,24},{24,28},{28,20},{20,12},{12,4},{4,0},{1,9},{9... | collective-permute-start | bytes 786440 | tf_op jit(solution)/shard_map/ppermute | solution.py:67
  79.1 17.0 %collective-permute-start.28 = (bf16[512,256]{1,0:T(8,128)(2,1)S(1)}, bf16[512,256]{1,0:T(8,128)(2,1)S(1)}, u32[]{:S(2)}, u32[]{:S(2)}) collective-permute-start(bf16[512,256]{1,0:T(8,128)(2,1)S(1)} %collective-permute-done.26.refs_3_), channel_id=1, source_target_pairs={{0,8},{8,16},{16,24},{24,28},{28,20},{20,12},{12,4},{4,0},{1,9},{9... | collective-permute-start | bytes 786440 | tf_op jit(solution)/shard_map/ppermute | solution.py:67
  81.0 15.1 %collective-permute-start.30 = (bf16[512,256]{1,0:T(8,128)(2,1)S(1)}, bf16[512,256]{1,0:T(8,128)(2,1)S(1)}, u32[]{:S(2)}, u32[]{:S(2)}) collective-permute-start(bf16[512,256]{1,0:T(8,128)(2,1)S(1)} %collective-permute-done.29.refs_6_), channel_id=1, source_target_pairs={{8,0},{16,8},{24,16},{28,24},{20,28},{12,20},{4,12},{0,4},{9,1},{1... | collective-permute-start | bytes 786440 | tf_op jit(solution)/shard_map/ppermute | solution.py:67
  83.5 12.6 %collective-permute-start.31 = (bf16[4,128,128]{2,1,0:T(8,128)(2,1)S(1)}, bf16[4,128,128]{2,1,0:T(8,128)(2,1)S(1)}, u32[]{:S(2)}, u32[]{:S(2)}) collective-permute-start(bf16[4,128,128]{2,1,0:T(8,128)(2,1)S(1)} %convert_add_fusion), channel_id=1, source_target_pairs={{0,16},{4,20},{8,24},{12,28},{16,0},{20,4},{24,8},{28,12},{1,17},{... | collective-permute-start | bytes 393224 | tf_op jit(solution)/shard_map/ppermute | solution.py:387
  102.9 2.0 %collective-permute-start.32 = (bf16[512,512]{1,0:T(8,128)(2,1)S(1)}, bf16[512,512]{1,0:T(8,128)(2,1)S(1)}, u32[]{:S(2)}, u32[]{:S(2)}) collective-permute-start(bf16[512,512]{1,0:T(8,128)(2,1)S(1)} %get-tuple-element.35), channel_id=1, source_target_pairs={{0,1},{1,0},{2,3},{3,2},{4,5},{5,4},{6,7},{7,6},{8,9},{9,8},{10,11... | collective-permute-start | bytes 1572872 | tf_op jit(solution)/shard_map/ppermute | solution.py:414
  105.0 14.0 %collective-permute-start.34 = (bf16[512,512]{1,0:T(8,128)(2,1)S(1)}, bf16[512,512]{1,0:T(8,128)(2,1)S(1)}, u32[]{:S(2)}, u32[]{:S(2)}) collective-permute-start(bf16[512,512]{1,0:T(8,128)(2,1)S(1)} %add_convert_fusion.1), channel_id=1, source_target_pairs={{0,2},{1,3},{2,0},{3,1},{4,6},{5,7},{6,4},{7,5},{8,10},{9,11},{10,... | collective-permute-start | bytes 1572872 | tf_op jit(solution)/shard_map/ppermute | solution.py:414
  108.1 10.9 %collective-permute-start.33 = (bf16[512,512]{1,0:T(8,128)(2,1)S(1)}, bf16[512,512]{1,0:T(8,128)(2,1)S(1)}, u32[]{:S(2)}, u32[]{:S(2)}) collective-permute-start(bf16[512,512]{1,0:T(8,128)(2,1)S(1)} %get-tuple-element.38), channel_id=1, source_target_pairs={{0,1},{1,0},{2,3},{3,2},{4,5},{5,4},{6,7},{7,6},{8,9},{9,8},{10,11... | collective-permute-start | bytes 1572872 | tf_op jit(solution)/shard_map/ppermute | solution.py:414
  (8 other events, 24.1 us)

commit v6 on v5

--- a/solution.py
+++ b/solution.py
@@ -367,7 +367,7 @@
         ]
         mixing = mixing_matrix(weights_by_token, local_bits)
         for step in range(1, n // 2 + 1):
-            key.advance(*((mixing,) if step == 3 else ()))
+            key.advance(*((mixing,) if step == 2 else ()))
             value.advance()
             query.advance()
             if step > 1:

time: 120 us -> 119 us (level)
  waiting for transfers between devices: 43 us -> 37.4 us
  starting transfers between devices: 43.8 us -> 47.9 us
    ppermute x28, waiting for transfers between devices: 28 us -> 23.8 us  [advance(): self.ways[way] = lax.ppermute(after(piece, gate), 'seq', pairs)]
    ppermute x28, starting transfers between devices: 38 us -> 41.6 us  [advance(): self.ways[way] = lax.ppermute(after(piece, gate), 'seq', pairs)]
    ppermute x4, waiting for transfers between devices: 2.32 us -> 1.05 us  [from_partner(): return lax.ppermute(array, 'seq', [(i, i ^ apart) for i in range(n)])]
    unnamed x43 -> x45, local copies, waits for them, and re-layouts: 5.34 us -> 5.35 us
  transfers between devices with their start and end apart: 35 -> 35, of which waited for: 20 -> 18; matrix products, arithmetic and copies ran while one was open for 3% -> 3% of each run, Pallas kernels for 17% -> 17%
where the time goes in v6:
time: 119 us
  starting transfers between devices  47.9 us (40%)
  waiting for transfers between devices  37.4 us (31%)
  Pallas kernels  24.7 us (21%)
  local copies, waits for them, and re-layouts  6.14 us (5%)
  other arithmetic  2.22 us (2%)
    ppermute x28, starting transfers between devices, advance(): self.ways[way] = lax.ppermute(after(piece, gate), 'seq', pairs)  41.6 us
    pallas_call x5, Pallas kernels, call(): pl.pallas_call(kernel, out_shape=outs, scratch_shapes=list(scratch), comp...  24.7 us
    ppermute x28, waiting for transfers between devices, advance(): self.ways[way] = lax.ppermute(after(piece, gate), 'seq', pairs)  23.8 us
    ppermute x3, waiting for transfers between devices, from_group(): lax.ppermute(array, 'head', [(g, g ^ 1 << bit) for g in range(groups)])  12.6 us
    unnamed x45, local copies, waits for them, and re-layouts  5.35 us
    ppermute x4, starting transfers between devices, from_partner(): return lax.ppermute(array, 'seq', [(i, i ^ apart) for i in range(n)])  4.4 us
  transfers between devices with their start and end apart: 35, of which 18 were waited for; matrix products, arithmetic and copies ran while one was open for 3% of the time, Pallas kernels for 17%

profile of v6, /device:TPU:0, one launch (start us, length us, event | category | flops | bytes accessed | tf_op | source)
XLA Modules:
  0.0 118.7 jit_solution(9324496076736658246)
XLA Ops:
  0.0 3.0 %collective-permute-start = (bf16[256,512]{1,0:T(8,128)(2,1)}, bf16[256,512]{1,0:T(8,128)(2,1)S(1)}, u32[]{:S(2)}, u32[]{:S(2)}) collective-permute-start(bf16[256,512]{1,0:T(8,128)(2,1)} %refs_0_.4), channel_id=1, source_target_pairs={{0,8},{8,16},{16,24},{24,28},{28,20},{20,12},{12,4},{4,0},{1,9},{9... | collective-permute-start | bytes 786440 | tf_op jit(solution)/shard_map/ppermute | solution.py:67
  3.0 2.0 %collective-permute-start.7 = (bf16[256,512]{1,0:T(8,128)(2,1)}, bf16[256,512]{1,0:T(8,128)(2,1)S(1)}, u32[]{:S(2)}, u32[]{:S(2)}) collective-permute-start(bf16[256,512]{1,0:T(8,128)(2,1)} %refs_8_.1), channel_id=1, source_target_pairs={{0,8},{8,16},{16,24},{24,28},{28,20},{20,12},{12,4},{4,0},{1,9},{9... | collective-permute-start | bytes 786440 | tf_op jit(solution)/shard_map/ppermute | solution.py:67
  5.1 2.0 %collective-permute-start.17 = (bf16[256,512]{1,0:T(8,128)(2,1)}, bf16[256,512]{1,0:T(8,128)(2,1)S(1)}, u32[]{:S(2)}, u32[]{:S(2)}) collective-permute-start(bf16[256,512]{1,0:T(8,128)(2,1)} %refs_0_.5), channel_id=1, source_target_pairs={{0,8},{8,16},{16,24},{24,28},{28,20},{20,12},{12,4},{4,0},{1,9},{9... | collective-permute-start | bytes 786440 | tf_op jit(solution)/shard_map/ppermute | solution.py:67
  7.1 2.2 %copy.7 = f32[4,13,512]{1,2,0:T(8,128)} copy(f32[4,13,512]{2,0,1:T(4,128)} %param.11) | data formatting | bytes 212992 | tf_op args[5]
  9.3 4.5 %shard_map.64.mixing = bf16[4,512,512]{2,1,0:T(8,128)(2,1)} custom-call(f32[4,512,13]{2,1,0:T(8,128)} %bitcast.22), custom_call_target="tpu_custom_call" | custom-call | flops 1 | bytes 8814592 | tf_op jit(solution)/shard_map/pallas_call | solution.py:23
  13.9 2.0 %collective-permute-start.2 = (bf16[256,512]{1,0:T(8,128)(2,1)S(1)}, bf16[256,512]{1,0:T(8,128)(2,1)S(1)}, u32[]{:S(2)}, u32[]{:S(2)}) collective-permute-start(bf16[256,512]{1,0:T(8,128)(2,1)S(1)} %collective-permute-done.refs_1_), channel_id=1, source_target_pairs={{0,8},{8,16},{16,24},{24,28},{28,20},{20,12},{12,4},{4,0},{1,9},{9... | collective-permute-start | bytes 786440 | tf_op jit(solution)/shard_map/ppermute | solution.py:67
  15.9 2.1 %collective-permute-start.3 = (bf16[256,512]{1,0:T(8,128)(2,1)S(1)}, bf16[256,512]{1,0:T(8,128)(2,1)S(1)}, u32[]{:S(2)}, u32[]{:S(2)}) collective-permute-start(bf16[256,512]{1,0:T(8,128)(2,1)S(1)} %collective-permute-done.1.refs_2_), channel_id=1, source_target_pairs={{8,0},{16,8},{24,16},{28,24},{20,28},{12,20},{4,12},{0,4},{9,1},{1... | collective-permute-start | bytes 786440 | tf_op jit(solution)/shard_map/ppermute | solution.py:67
  18.1 1.6 %collective-permute-start.9 = (bf16[256,512]{1,0:T(8,128)(2,1)S(1)}, bf16[256,512]{1,0:T(8,128)(2,1)S(1)}, u32[]{:S(2)}, u32[]{:S(2)}) collective-permute-start(bf16[256,512]{1,0:T(8,128)(2,1)S(1)} %collective-permute-done.7.refs_9_), channel_id=1, source_target_pairs={{0,8},{8,16},{16,24},{24,28},{28,20},{20,12},{12,4},{4,0},{1,9},{9... | collective-permute-start | bytes 786440 | tf_op jit(solution)/shard_map/ppermute | solution.py:67
  19.7 1.9 %collective-permute-done.17.refs_1_ = bf16[256,512]{1,0:T(8,128)(2,1)S(1)} collective-permute-done((bf16[256,512]{1,0:T(8,128)(2,1)}, bf16[256,512]{1,0:T(8,128)(2,1)S(1)}, u32[]{:S(2)}, u32[]{:S(2)}) %collective-permute-start.17) | collective-permute-done | bytes 262176 | tf_op jit(solution)/shard_map/ppermute | solution.py:67
  21.6 2.1 %collective-permute-start.10 = (bf16[256,512]{1,0:T(8,128)(2,1)S(1)}, bf16[256,512]{1,0:T(8,128)(2,1)S(1)}, u32[]{:S(2)}, u32[]{:S(2)}) collective-permute-start(bf16[256,512]{1,0:T(8,128)(2,1)S(1)} %collective-permute-done.8.refs_10_), channel_id=1, source_target_pairs={{8,0},{16,8},{24,16},{28,24},{20,28},{12,20},{4,12},{0,4},{9,1},{1... | collective-permute-start | bytes 786440 | tf_op jit(solution)/shard_map/ppermute | solution.py:67
  23.7 1.6 %collective-permute-start.19 = (bf16[256,512]{1,0:T(8,128)(2,1)S(1)}, bf16[256,512]{1,0:T(8,128)(2,1)S(1)}, u32[]{:S(2)}, u32[]{:S(2)}) collective-permute-start(bf16[256,512]{1,0:T(8,128)(2,1)S(1)} %collective-permute-done.17.refs_1_), channel_id=1, source_target_pairs={{0,8},{8,16},{16,24},{24,28},{28,20},{20,12},{12,4},{4,0},{1,9},{9... | collective-permute-start | bytes 786440 | tf_op jit(solution)/shard_map/ppermute | solution.py:67
  25.3 1.9 %collective-permute-done.2.refs_3_ = bf16[256,512]{1,0:T(8,128)(2,1)S(1)} collective-permute-done((bf16[256,512]{1,0:T(8,128)(2,1)S(1)}, bf16[256,512]{1,0:T(8,128)(2,1)S(1)}, u32[]{:S(2)}, u32[]{:S(2)}) %collective-permute-start.2) | collective-permute-done | bytes 262176 | tf_op jit(solution)/shard_map/ppermute | solution.py:67
  27.2 2.1 %collective-permute-start.25 = (bf16[512,256]{1,0:T(8,128)(2,1)S(1)}, bf16[512,256]{1,0:T(8,128)(2,1)S(1)}, u32[]{:S(2)}, u32[]{:S(2)}) collective-permute-start(bf16[512,256]{1,0:T(8,128)(2,1)S(1)} %copy-done.1), channel_id=1, source_target_pairs={{8,0},{16,8},{24,16},{28,24},{20,28},{12,20},{4,12},{0,4},{9,1},{1... | collective-permute-start | bytes 786440 | tf_op jit(solution)/shard_map/ppermute | solution.py:67
  29.3 1.6 %collective-permute-start.24 = (bf16[512,256]{1,0:T(8,128)(2,1)S(1)}, bf16[512,256]{1,0:T(8,128)(2,1)S(1)}, u32[]{:S(2)}, u32[]{:S(2)}) collective-permute-start(bf16[512,256]{1,0:T(8,128)(2,1)S(1)} %copy-done.1), channel_id=1, source_target_pairs={{0,8},{8,16},{16,24},{24,28},{28,20},{20,12},{12,4},{4,0},{1,9},{9... | collective-permute-start | bytes 786440 | tf_op jit(solution)/shard_map/ppermute | solution.py:67
  30.9 1.9 %collective-permute-done.9.refs_11_ = bf16[256,512]{1,0:T(8,128)(2,1)S(1)} collective-permute-done((bf16[256,512]{1,0:T(8,128)(2,1)S(1)}, bf16[256,512]{1,0:T(8,128)(2,1)S(1)}, u32[]{:S(2)}, u32[]{:S(2)}) %collective-permute-start.9) | collective-permute-done | bytes 262176 | tf_op jit(solution)/shard_map/ppermute | solution.py:67
  32.8 2.1 %collective-permute-start.4 = (bf16[256,512]{1,0:T(8,128)(2,1)S(1)}, bf16[256,512]{1,0:T(8,128)(2,1)S(1)}, u32[]{:S(2)}, u32[]{:S(2)}) collective-permute-start(bf16[256,512]{1,0:T(8,128)(2,1)S(1)} %collective-permute-done.2.refs_3_), channel_id=1, source_target_pairs={{0,8},{8,16},{16,24},{24,28},{28,20},{20,12},{12,4},{4,0},{1,9},{9... | collective-permute-start | bytes 786440 | tf_op jit(solution)/shard_map/ppermute | solution.py:67
  34.9 3.5 %collective-permute-done.19.refs_3_ = bf16[256,512]{1,0:T(8,128)(2,1)S(1)} collective-permute-done((bf16[256,512]{1,0:T(8,128)(2,1)S(1)}, bf16[256,512]{1,0:T(8,128)(2,1)S(1)}, u32[]{:S(2)}, u32[]{:S(2)}) %collective-permute-start.19) | collective-permute-done | bytes 262176 | tf_op jit(solution)/shard_map/ppermute | solution.py:67
  38.4 2.1 %collective-permute-start.5 = (bf16[256,512]{1,0:T(8,128)(2,1)S(1)}, bf16[256,512]{1,0:T(8,128)(2,1)S(1)}, u32[]{:S(2)}, u32[]{:S(2)}) collective-permute-start(bf16[256,512]{1,0:T(8,128)(2,1)S(1)} %collective-permute-done.3.refs_4_), channel_id=1, source_target_pairs={{8,0},{16,8},{24,16},{28,24},{20,28},{12,20},{4,12},{0,4},{9,1},{1... | collective-permute-start | bytes 786440 | tf_op jit(solution)/shard_map/ppermute | solution.py:67
  40.6 1.5 %collective-permute-start.27 = (bf16[512,256]{1,0:T(8,128)(2,1)S(1)}, bf16[512,256]{1,0:T(8,128)(2,1)S(1)}, u32[]{:S(2)}, u32[]{:S(2)}) collective-permute-start(bf16[512,256]{1,0:T(8,128)(2,1)S(1)} %collective-permute-done.25.refs_2_), channel_id=1, source_target_pairs={{8,0},{16,8},{24,16},{28,24},{20,28},{12,20},{4,12},{0,4},{9,1},{1... | collective-permute-start | bytes 786440 | tf_op jit(solution)/shard_map/ppermute | solution.py:67
  42.0 2.0 %collective-permute-done.24.refs_1_ = bf16[512,256]{1,0:T(8,128)(2,1)S(1)} collective-permute-done((bf16[512,256]{1,0:T(8,128)(2,1)S(1)}, bf16[512,256]{1,0:T(8,128)(2,1)S(1)}, u32[]{:S(2)}, u32[]{:S(2)}) %collective-permute-start.24) | collective-permute-done | bytes 262176 | tf_op jit(solution)/shard_map/ppermute | solution.py:67
  44.0 2.1 %collective-permute-start.11 = (bf16[256,512]{1,0:T(8,128)(2,1)S(1)}, bf16[256,512]{1,0:T(8,128)(2,1)S(1)}, u32[]{:S(2)}, u32[]{:S(2)}) collective-permute-start(bf16[256,512]{1,0:T(8,128)(2,1)S(1)} %collective-permute-done.9.refs_11_), channel_id=1, source_target_pairs={{0,8},{8,16},{16,24},{24,28},{28,20},{20,12},{12,4},{4,0},{1,9},{9... | collective-permute-start | bytes 786440 | tf_op jit(solution)/shard_map/ppermute | solution.py:67
  46.1 3.5 %collective-permute-done.4.refs_5_ = bf16[256,512]{1,0:T(8,128)(2,1)S(1)} collective-permute-done((bf16[256,512]{1,0:T(8,128)(2,1)S(1)}, bf16[256,512]{1,0:T(8,128)(2,1)S(1)}, u32[]{:S(2)}, u32[]{:S(2)}) %collective-permute-start.4) | collective-permute-done | bytes 262176 | tf_op jit(solution)/shard_map/ppermute | solution.py:67
  49.6 2.1 %collective-permute-start.6 = (bf16[256,512]{1,0:T(8,128)(2,1)S(1)}, bf16[256,512]{1,0:T(8,128)(2,1)S(1)}, u32[]{:S(2)}, u32[]{:S(2)}) collective-permute-start(bf16[256,512]{1,0:T(8,128)(2,1)S(1)} %collective-permute-done.4.refs_5_), channel_id=1, source_target_pairs={{0,8},{8,16},{16,24},{24,28},{28,20},{20,12},{12,4},{4,0},{1,9},{9... | collective-permute-start | bytes 786440 | tf_op jit(solution)/shard_map/ppermute | solution.py:67
  51.8 1.9 %collective-permute-start.20 = (bf16[256,512]{1,0:T(8,128)(2,1)S(1)}, bf16[256,512]{1,0:T(8,128)(2,1)}, u32[]{:S(2)}, u32[]{:S(2)}) collective-permute-start(bf16[256,512]{1,0:T(8,128)(2,1)S(1)} %collective-permute-done.18.refs_2_), channel_id=1, source_target_pairs={{8,0},{16,8},{24,16},{28,24},{20,28},{12,20},{4,12},{0,4},{9,1},{1... | collective-permute-start | bytes 786440 | tf_op jit(solution)/shard_map/ppermute | solution.py:67
  53.7 3.7 %collective-permute-done.27.refs_4_ = bf16[512,256]{1,0:T(8,128)(2,1)S(1)} collective-permute-done((bf16[512,256]{1,0:T(8,128)(2,1)S(1)}, bf16[512,256]{1,0:T(8,128)(2,1)S(1)}, u32[]{:S(2)}, u32[]{:S(2)}) %collective-permute-start.27) | collective-permute-done | bytes 262176 | tf_op jit(solution)/shard_map/ppermute | solution.py:67
  57.4 2.0 %collective-permute-start.21 = (bf16[256,512]{1,0:T(8,128)(2,1)S(1)}, bf16[256,512]{1,0:T(8,128)(2,1)}, u32[]{:S(2)}, u32[]{:S(2)}) collective-permute-start(bf16[256,512]{1,0:T(8,128)(2,1)S(1)} %collective-permute-done.19.refs_3_), channel_id=1, source_target_pairs={{0,8},{8,16},{16,24},{24,28},{28,20},{20,12},{12,4},{4,0},{1,9},{9... | collective-permute-start | bytes 786440 | tf_op jit(solution)/shard_map/ppermute | solution.py:67
  59.4 1.4 %collective-permute-done.6.refs_7_ = bf16[256,512]{1,0:T(8,128)(2,1)S(1)} collective-permute-done((bf16[256,512]{1,0:T(8,128)(2,1)S(1)}, bf16[256,512]{1,0:T(8,128)(2,1)S(1)}, u32[]{:S(2)}, u32[]{:S(2)}) %collective-permute-start.6) | collective-permute-done | bytes 262176 | tf_op jit(solution)/shard_map/ppermute | solution.py:67
  60.9 2.1 %collective-permute-start.26 = (bf16[512,256]{1,0:T(8,128)(2,1)S(1)}, bf16[512,256]{1,0:T(8,128)(2,1)S(1)}, u32[]{:S(2)}, u32[]{:S(2)}) collective-permute-start(bf16[512,256]{1,0:T(8,128)(2,1)S(1)} %collective-permute-done.24.refs_1_), channel_id=1, source_target_pairs={{0,8},{8,16},{16,24},{24,28},{28,20},{20,12},{12,4},{4,0},{1,9},{9... | collective-permute-start | bytes 786440 | tf_op jit(solution)/shard_map/ppermute | solution.py:67
  63.9 6.9 %shard_map.65 = (bf16[512,512]{1,0:T(8,128)(2,1)}, bf16[512,512]{1,0:T(8,128)(2,1)}, f32[4,128,128]{2,1,0:T(8,128)}, bf16[4,128,128]{2,1,0:T(8,128)(2,1)}) custom-call(s32[2,8]{1,0:T(2,128)} %stack.103.starts, bf16[512,2048]{1,0:T(8,128)(2,1)} %tokens.2, bf16[256,512]{1,0:T(8,128)(2,1)} %refs_0_.4, bf16[256,512]{1,0:T(8,128)(2,1)} %copy-done.10, ...), custom_call_target="tpu_custom_call" | custom-call | flops 1 | bytes 30933248 | tf_op jit(solution)/shard_map/pallas_call | solution.py:23
  70.8 1.5 %collective-permute-start.16 = (bf16[4,128,128]{2,1,0:T(8,128)(2,1)}, bf16[4,128,128]{2,1,0:T(8,128)(2,1)S(1)}, u32[]{:S(2)}, u32[]{:S(2)}) collective-permute-start(bf16[4,128,128]{2,1,0:T(8,128)(2,1)} %get-tuple-element.25), channel_id=1, source_target_pairs={{0,12},{4,8},{8,4},{12,0},{16,28},{20,24},{24,20},{28,16},{1,13},{... | collective-permute-start | bytes 393224 | tf_op jit(solution)/shard_map/ppermute | solution.py:387
  72.8 1.2 %collective-permute-done.29.refs_6_ = bf16[512,256]{1,0:T(8,128)(2,1)S(1)} collective-permute-done((bf16[512,256]{1,0:T(8,128)(2,1)S(1)}, bf16[512,256]{1,0:T(8,128)(2,1)S(1)}, u32[]{:S(2)}, u32[]{:S(2)}) %collective-permute-start.29) | collective-permute-done | bytes 262176 | tf_op jit(solution)/shard_map/ppermute | solution.py:67
  74.4 1.6 %collective-permute-start.22 = (bf16[256,512]{1,0:T(8,128)(2,1)}, bf16[256,512]{1,0:T(8,128)(2,1)S(1)}, u32[]{:S(2)}, u32[]{:S(2)}) collective-permute-start(bf16[256,512]{1,0:T(8,128)(2,1)} %collective-permute-done.20.refs_4_), channel_id=1, source_target_pairs={{8,0},{16,8},{24,16},{28,24},{20,28},{12,20},{4,12},{0,4},{9,1},{1... | collective-permute-start | bytes 786440 | tf_op jit(solution)/shard_map/ppermute | solution.py:67
  76.4 0.8 collective-permute-done.16.refs_10_
  77.3 2.8 %collective-permute-start.28 = (bf16[512,256]{1,0:T(8,128)(2,1)S(1)}, bf16[512,256]{1,0:T(8,128)(2,1)S(1)}, u32[]{:S(2)}, u32[]{:S(2)}) collective-permute-start(bf16[512,256]{1,0:T(8,128)(2,1)S(1)} %collective-permute-done.26.refs_3_), channel_id=1, source_target_pairs={{0,8},{8,16},{16,24},{24,28},{28,20},{20,12},{12,4},{4,0},{1,9},{9... | collective-permute-start | bytes 786440 | tf_op jit(solution)/shard_map/ppermute | solution.py:67
  80.2 0.8 collective-permute-start.30
  81.0 1.0 convert_add_fusion
  82.0 2.0 %collective-permute-start.31 = (bf16[4,128,128]{2,1,0:T(8,128)(2,1)S(1)}, bf16[4,128,128]{2,1,0:T(8,128)(2,1)S(1)}, u32[]{:S(2)}, u32[]{:S(2)}) collective-permute-start(bf16[4,128,128]{2,1,0:T(8,128)(2,1)S(1)} %convert_add_fusion), channel_id=1, source_target_pairs={{0,16},{4,20},{8,24},{12,28},{16,0},{20,4},{24,8},{28,12},{1,17},{... | collective-permute-start | bytes 393224 | tf_op jit(solution)/shard_map/ppermute | solution.py:387
  84.2 2.5 %collective-permute-done.22.refs_6_ = bf16[256,512]{1,0:T(8,128)(2,1)S(1)} collective-permute-done((bf16[256,512]{1,0:T(8,128)(2,1)}, bf16[256,512]{1,0:T(8,128)(2,1)S(1)}, u32[]{:S(2)}, u32[]{:S(2)}) %collective-permute-start.22) | collective-permute-done | bytes 262176 | tf_op jit(solution)/shard_map/ppermute | solution.py:67
  86.7 0.7 copy-done.8
  87.5 7.3 %shard_map.66 = (bf16[512,512]{1,0:T(8,128)(2,1)}, f32[512,512]{1,0:T(8,128)}) custom-call(s32[2,8]{1,0:T(2,128)} %stack.103.starts, bf16[512,2048]{1,0:T(8,128)(2,1)} %tokens.2, bf16[512,512]{1,0:T(8,128)(2,1)} %get-tuple-element.27.keys, bf16[512,512]{1,0:T(8,128)(2,1)} %get-tuple-element.28.values, bf16[4,512,512]{2,1,0:T(8,128)(2,1)} %shard_map.64.mixing, ...), custom_call_target="tpu_custom_call" | custom-call | flops 1 | bytes 35651840 | tf_op jit(solution)/shard_map/pallas_call | solution.py:23
  94.8 1.2 %copy-done.2 = f32[512,512]{1,0:T(8,128)S(1)} copy-done((f32[512,512]{1,0:T(8,128)S(1)}, f32[512,512]{1,0:T(8,128)}, u32[]{:S(2)}) %copy-start.2) | copy-done | bytes 1048600
  96.1 1.0 copy-done.3
  97.1 4.5 %shard_map.67 = (bf16[512,512]{1,0:T(8,128)(2,1)S(1)}, bf16[512,512]{1,0:T(8,128)(2,1)S(1)}, bf16[512,512]{1,0:T(8,128)(2,1)S(1)}) custom-call(f32[3]{0:T(128)S(1)} %add_convert_fusion.2.upper, s32[2,8]{1,0:T(2,128)S(1)} %stack.88.starts, bf16[512,512]{1,0:T(8,128)(2,1)S(1)} %copy-done.3, f32[512,512]{1,0:T(8,128)S(1)} %copy-done.2, ...), custom_call_target="tpu_custom_call" | custom-call | flops 1 | bytes 23494960 | tf_op jit(solution)/shard_map/pallas_call | solution.py:23
  101.7 1.9 %collective-permute-done.32 = bf16[512,512]{1,0:T(8,128)(2,1)S(1)} collective-permute-done((bf16[512,512]{1,0:T(8,128)(2,1)S(1)}, bf16[512,512]{1,0:T(8,128)(2,1)S(1)}, u32[]{:S(2)}, u32[]{:S(2)}) %collective-permute-start.32) | collective-permute-done | bytes 524320 | tf_op jit(solution)/shard_map/ppermute | solution.py:414
  103.7 1.7 %collective-permute-start.34 = (bf16[512,512]{1,0:T(8,128)(2,1)S(1)}, bf16[512,512]{1,0:T(8,128)(2,1)S(1)}, u32[]{:S(2)}, u32[]{:S(2)}) collective-permute-start(bf16[512,512]{1,0:T(8,128)(2,1)S(1)} %add_convert_fusion.1), channel_id=1, source_target_pairs={{0,2},{1,3},{2,0},{3,1},{4,6},{5,7},{6,4},{7,5},{8,10},{9,11},{10,... | collective-permute-start | bytes 1572872 | tf_op jit(solution)/shard_map/ppermute | solution.py:414
  105.4 1.5 %shard_map.68 = (bf16[512,512]{1,0:T(8,128)(2,1)S(1)}, bf16[512,512]{1,0:T(8,128)(2,1)S(1)}) custom-call(s32[2,8]{1,0:T(2,128)S(1)} %stack.88.starts, bf16[512,512]{1,0:T(8,128)(2,1)S(1)} %get-tuple-element.36.attended, bf16[512,256]{1,0:T(8,128)(2,1)S(1)} %copy-done.1, bf16[512,256]{1,0:T(8,128)(2,1)S(1)} %collective-permute-done.24.refs_1_, ...), custom_call_target="tpu_custom_call" | custom-call | flops 1 | bytes 14680320 | tf_op jit(solution)/shard_map/pallas_call | solution.py:23
  107.1 10.7 %collective-permute-done.34 = bf16[512,512]{1,0:T(8,128)(2,1)S(1)} collective-permute-done((bf16[512,512]{1,0:T(8,128)(2,1)S(1)}, bf16[512,512]{1,0:T(8,128)(2,1)S(1)}, u32[]{:S(2)}, u32[]{:S(2)}) %collective-permute-start.34) | collective-permute-done | bytes 524320 | tf_op jit(solution)/shard_map/ppermute | solution.py:414
  117.7 1.0 add_convert_fusion
  (80 shorter events, 3.4 us)
Async XLA Ops:
  0.0 13.8 %copy-start.4 = (bf16[256,512]{1,0:T(8,128)(2,1)S(1)}, bf16[256,512]{1,0:T(8,128)(2,1)}, u32[]{:S(2)}) copy-start(bf16[256,512]{1,0:T(8,128)(2,1)} %refs_0_.5) | copy-start | bytes 786436
  0.0 27.2 %copy-start.1 = (bf16[512,256]{1,0:T(8,128)(2,1)S(1)}, bf16[512,256]{1,0:T(8,128)(2,1)}, u32[]{:S(2)}) copy-start(bf16[512,256]{1,0:T(8,128)(2,1)} %refs_0_.7) | copy-start | bytes 786436
  0.0 13.8 %collective-permute-start = (bf16[256,512]{1,0:T(8,128)(2,1)}, bf16[256,512]{1,0:T(8,128)(2,1)S(1)}, u32[]{:S(2)}, u32[]{:S(2)}) collective-permute-start(bf16[256,512]{1,0:T(8,128)(2,1)} %refs_0_.4), channel_id=1, source_target_pairs={{0,8},{8,16},{16,24},{24,28},{28,20},{20,12},{12,4},{4,0},{1,9},{9... | collective-permute-start | bytes 786440 | tf_op jit(solution)/shard_map/ppermute | solution.py:67
  3.0 10.9 %collective-permute-start.1 = (bf16[256,512]{1,0:T(8,128)(2,1)}, bf16[256,512]{1,0:T(8,128)(2,1)S(1)}, u32[]{:S(2)}, u32[]{:S(2)}) collective-permute-start(bf16[256,512]{1,0:T(8,128)(2,1)} %refs_0_.4), channel_id=1, source_target_pairs={{8,0},{16,8},{24,16},{28,24},{20,28},{12,20},{4,12},{0,4},{9,1},{1... | collective-permute-start | bytes 786440 | tf_op jit(solution)/shard_map/ppermute | solution.py:67
  3.0 12.9 %collective-permute-start.7 = (bf16[256,512]{1,0:T(8,128)(2,1)}, bf16[256,512]{1,0:T(8,128)(2,1)S(1)}, u32[]{:S(2)}, u32[]{:S(2)}) collective-permute-start(bf16[256,512]{1,0:T(8,128)(2,1)} %refs_8_.1), channel_id=1, source_target_pairs={{0,8},{8,16},{16,24},{24,28},{28,20},{20,12},{12,4},{4,0},{1,9},{9... | collective-permute-start | bytes 786440 | tf_op jit(solution)/shard_map/ppermute | solution.py:67
  5.1 13.0 %collective-permute-start.8 = (bf16[256,512]{1,0:T(8,128)(2,1)}, bf16[256,512]{1,0:T(8,128)(2,1)S(1)}, u32[]{:S(2)}, u32[]{:S(2)}) collective-permute-start(bf16[256,512]{1,0:T(8,128)(2,1)} %refs_8_.1), channel_id=1, source_target_pairs={{8,0},{16,8},{24,16},{28,24},{20,28},{12,20},{4,12},{0,4},{9,1},{1... | collective-permute-start | bytes 786440 | tf_op jit(solution)/shard_map/ppermute | solution.py:67
  5.1 16.5 %collective-permute-start.17 = (bf16[256,512]{1,0:T(8,128)(2,1)}, bf16[256,512]{1,0:T(8,128)(2,1)S(1)}, u32[]{:S(2)}, u32[]{:S(2)}) collective-permute-start(bf16[256,512]{1,0:T(8,128)(2,1)} %refs_0_.5), channel_id=1, source_target_pairs={{0,8},{8,16},{16,24},{24,28},{28,20},{20,12},{12,4},{4,0},{1,9},{9... | collective-permute-start | bytes 786440 | tf_op jit(solution)/shard_map/ppermute | solution.py:67
  13.8 50.1 %copy-start.10 = (bf16[256,512]{1,0:T(8,128)(2,1)}, bf16[256,512]{1,0:T(8,128)(2,1)S(1)}, u32[]{:S(2)}) copy-start(bf16[256,512]{1,0:T(8,128)(2,1)S(1)} %collective-permute-done.refs_1_) | copy-start | bytes 786436
  13.8 9.9 %collective-permute-start.18 = (bf16[256,512]{1,0:T(8,128)(2,1)S(1)}, bf16[256,512]{1,0:T(8,128)(2,1)S(1)}, u32[]{:S(2)}, u32[]{:S(2)}) collective-permute-start(bf16[256,512]{1,0:T(8,128)(2,1)S(1)} %copy-done.4), channel_id=1, source_target_pairs={{8,0},{16,8},{24,16},{28,24},{20,28},{12,20},{4,12},{0,4},{9,1},{1... | collective-permute-start | bytes 786440 | tf_op jit(solution)/shard_map/ppermute | solution.py:67
  13.9 50.0 %copy-start.11 = (bf16[256,512]{1,0:T(8,128)(2,1)}, bf16[256,512]{1,0:T(8,128)(2,1)S(1)}, u32[]{:S(2)}) copy-start(bf16[256,512]{1,0:T(8,128)(2,1)S(1)} %collective-permute-done.1.refs_2_) | copy-start | bytes 786436
  13.9 13.3 %collective-permute-start.2 = (bf16[256,512]{1,0:T(8,128)(2,1)S(1)}, bf16[256,512]{1,0:T(8,128)(2,1)S(1)}, u32[]{:S(2)}, u32[]{:S(2)}) collective-permute-start(bf16[256,512]{1,0:T(8,128)(2,1)S(1)} %collective-permute-done.refs_1_), channel_id=1, source_target_pairs={{0,8},{8,16},{16,24},{24,28},{28,20},{20,12},{12,4},{4,0},{1,9},{9... | collective-permute-start | bytes 786440 | tf_op jit(solution)/shard_map/ppermute | solution.py:67
  15.9 48.0 %copy-start.12 = (bf16[256,512]{1,0:T(8,128)(2,1)}, bf16[256,512]{1,0:T(8,128)(2,1)S(1)}, u32[]{:S(2)}) copy-start(bf16[256,512]{1,0:T(8,128)(2,1)S(1)} %collective-permute-done.7.refs_9_) | copy-start | bytes 786436
  15.9 13.4 %collective-permute-start.3 = (bf16[256,512]{1,0:T(8,128)(2,1)S(1)}, bf16[256,512]{1,0:T(8,128)(2,1)S(1)}, u32[]{:S(2)}, u32[]{:S(2)}) collective-permute-start(bf16[256,512]{1,0:T(8,128)(2,1)S(1)} %collective-permute-done.1.refs_2_), channel_id=1, source_target_pairs={{8,0},{16,8},{24,16},{28,24},{20,28},{12,20},{4,12},{0,4},{9,1},{1... | collective-permute-start | bytes 786440 | tf_op jit(solution)/shard_map/ppermute | solution.py:67
  18.1 45.8 %copy-start.13 = (bf16[256,512]{1,0:T(8,128)(2,1)}, bf16[256,512]{1,0:T(8,128)(2,1)S(1)}, u32[]{:S(2)}) copy-start(bf16[256,512]{1,0:T(8,128)(2,1)S(1)} %collective-permute-done.8.refs_10_) | copy-start | bytes 786436
  18.1 14.7 %collective-permute-start.9 = (bf16[256,512]{1,0:T(8,128)(2,1)S(1)}, bf16[256,512]{1,0:T(8,128)(2,1)S(1)}, u32[]{:S(2)}, u32[]{:S(2)}) collective-permute-start(bf16[256,512]{1,0:T(8,128)(2,1)S(1)} %collective-permute-done.7.refs_9_), channel_id=1, source_target_pairs={{0,8},{8,16},{16,24},{24,28},{28,20},{20,12},{12,4},{4,0},{1,9},{9... | collective-permute-start | bytes 786440 | tf_op jit(solution)/shard_map/ppermute | solution.py:67
  21.5 49.3 %copy-start.5 = (bf16[256,512]{1,0:T(8,128)(2,1)}, bf16[256,512]{1,0:T(8,128)(2,1)S(1)}, u32[]{:S(2)}) copy-start(bf16[256,512]{1,0:T(8,128)(2,1)S(1)} %collective-permute-done.17.refs_1_) | copy-start | bytes 786436
  21.6 13.4 %collective-permute-start.10 = (bf16[256,512]{1,0:T(8,128)(2,1)S(1)}, bf16[256,512]{1,0:T(8,128)(2,1)S(1)}, u32[]{:S(2)}, u32[]{:S(2)}) collective-permute-start(bf16[256,512]{1,0:T(8,128)(2,1)S(1)} %collective-permute-done.8.refs_10_), channel_id=1, source_target_pairs={{8,0},{16,8},{24,16},{28,24},{20,28},{12,20},{4,12},{0,4},{9,1},{1... | collective-permute-start | bytes 786440 | tf_op jit(solution)/shard_map/ppermute | solution.py:67
  23.7 47.1 %copy-start.6 = (bf16[256,512]{1,0:T(8,128)(2,1)}, bf16[256,512]{1,0:T(8,128)(2,1)S(1)}, u32[]{:S(2)}) copy-start(bf16[256,512]{1,0:T(8,128)(2,1)S(1)} %collective-permute-done.18.refs_2_) | copy-start | bytes 786436
  23.7 14.7 %collective-permute-start.19 = (bf16[256,512]{1,0:T(8,128)(2,1)S(1)}, bf16[256,512]{1,0:T(8,128)(2,1)S(1)}, u32[]{:S(2)}, u32[]{:S(2)}) collective-permute-start(bf16[256,512]{1,0:T(8,128)(2,1)S(1)} %collective-permute-done.17.refs_1_), channel_id=1, source_target_pairs={{0,8},{8,16},{16,24},{24,28},{28,20},{20,12},{12,4},{4,0},{1,9},{9... | collective-permute-start | bytes 786440 | tf_op jit(solution)/shard_map/ppermute | solution.py:67
  27.2 26.6 %copy-start.14 = (bf16[256,512]{1,0:T(8,128)(2,1)}, bf16[256,512]{1,0:T(8,128)(2,1)S(1)}, u32[]{:S(2)}) copy-start(bf16[256,512]{1,0:T(8,128)(2,1)S(1)} %collective-permute-done.2.refs_3_) | copy-start | bytes 786436
  27.2 13.4 %collective-permute-start.25 = (bf16[512,256]{1,0:T(8,128)(2,1)S(1)}, bf16[512,256]{1,0:T(8,128)(2,1)S(1)}, u32[]{:S(2)}, u32[]{:S(2)}) collective-permute-start(bf16[512,256]{1,0:T(8,128)(2,1)S(1)} %copy-done.1), channel_id=1, source_target_pairs={{8,0},{16,8},{24,16},{28,24},{20,28},{12,20},{4,12},{0,4},{9,1},{1... | collective-permute-start | bytes 786440 | tf_op jit(solution)/shard_map/ppermute | solution.py:67
  29.3 30.1 %copy-start.15 = (bf16[256,512]{1,0:T(8,128)(2,1)}, bf16[256,512]{1,0:T(8,128)(2,1)S(1)}, u32[]{:S(2)}) copy-start(bf16[256,512]{1,0:T(8,128)(2,1)S(1)} %collective-permute-done.3.refs_4_) | copy-start | bytes 786436
  29.3 14.7 %collective-permute-start.24 = (bf16[512,256]{1,0:T(8,128)(2,1)S(1)}, bf16[512,256]{1,0:T(8,128)(2,1)S(1)}, u32[]{:S(2)}, u32[]{:S(2)}) collective-permute-start(bf16[512,256]{1,0:T(8,128)(2,1)S(1)} %copy-done.1), channel_id=1, source_target_pairs={{0,8},{8,16},{16,24},{24,28},{28,20},{20,12},{12,4},{4,0},{1,9},{9... | collective-permute-start | bytes 786440 | tf_op jit(solution)/shard_map/ppermute | solution.py:67
  32.8 28.1 %copy-start.16 = (bf16[256,512]{1,0:T(8,128)(2,1)}, bf16[256,512]{1,0:T(8,128)(2,1)S(1)}, u32[]{:S(2)}) copy-start(bf16[256,512]{1,0:T(8,128)(2,1)S(1)} %collective-permute-done.9.refs_11_) | copy-start | bytes 786436
  32.8 16.9 %collective-permute-start.4 = (bf16[256,512]{1,0:T(8,128)(2,1)S(1)}, bf16[256,512]{1,0:T(8,128)(2,1)S(1)}, u32[]{:S(2)}, u32[]{:S(2)}) collective-permute-start(bf16[256,512]{1,0:T(8,128)(2,1)S(1)} %collective-permute-done.2.refs_3_), channel_id=1, source_target_pairs={{0,8},{8,16},{16,24},{24,28},{28,20},{20,12},{12,4},{4,0},{1,9},{9... | collective-permute-start | bytes 786440 | tf_op jit(solution)/shard_map/ppermute | solution.py:67
  34.9 28.1 %copy-start.17 = (bf16[256,512]{1,0:T(8,128)(2,1)}, bf16[256,512]{1,0:T(8,128)(2,1)S(1)}, u32[]{:S(2)}) copy-start(bf16[256,512]{1,0:T(8,128)(2,1)S(1)} %collective-permute-done.10.refs_12_) | copy-start | bytes 786436
  34.9 16.8 %collective-permute-start.12 = (bf16[256,512]{1,0:T(8,128)(2,1)S(1)}, bf16[256,512]{1,0:T(8,128)(2,1)}, u32[]{:S(2)}, u32[]{:S(2)}) collective-permute-start(bf16[256,512]{1,0:T(8,128)(2,1)S(1)} %collective-permute-done.10.refs_12_), channel_id=1, source_target_pairs={{8,0},{16,8},{24,16},{28,24},{20,28},{12,20},{4,12},{0,4},{9,1},{1... | collective-permute-start | bytes 786440 | tf_op jit(solution)/shard_map/ppermute | solution.py:67
  38.4 32.4 %copy-start.7 = (bf16[256,512]{1,0:T(8,128)(2,1)}, bf16[256,512]{1,0:T(8,128)(2,1)S(1)}, u32[]{:S(2)}) copy-start(bf16[256,512]{1,0:T(8,128)(2,1)S(1)} %collective-permute-done.19.refs_3_) | copy-start | bytes 786436
  38.4 13.4 %collective-permute-start.5 = (bf16[256,512]{1,0:T(8,128)(2,1)S(1)}, bf16[256,512]{1,0:T(8,128)(2,1)S(1)}, u32[]{:S(2)}, u32[]{:S(2)}) collective-permute-start(bf16[256,512]{1,0:T(8,128)(2,1)S(1)} %collective-permute-done.3.refs_4_), channel_id=1, source_target_pairs={{8,0},{16,8},{24,16},{28,24},{20,28},{12,20},{4,12},{0,4},{9,1},{1... | collective-permute-start | bytes 786440 | tf_op jit(solution)/shard_map/ppermute | solution.py:67
  40.6 16.9 %collective-permute-start.27 = (bf16[512,256]{1,0:T(8,128)(2,1)S(1)}, bf16[512,256]{1,0:T(8,128)(2,1)S(1)}, u32[]{:S(2)}, u32[]{:S(2)}) collective-permute-start(bf16[512,256]{1,0:T(8,128)(2,1)S(1)} %collective-permute-done.25.refs_2_), channel_id=1, source_target_pairs={{8,0},{16,8},{24,16},{28,24},{20,28},{12,20},{4,12},{0,4},{9,1},{1... | collective-permute-start | bytes 786440 | tf_op jit(solution)/shard_map/ppermute | solution.py:67
  44.0 13.4 %collective-permute-start.11 = (bf16[256,512]{1,0:T(8,128)(2,1)S(1)}, bf16[256,512]{1,0:T(8,128)(2,1)S(1)}, u32[]{:S(2)}, u32[]{:S(2)}) collective-permute-start(bf16[256,512]{1,0:T(8,128)(2,1)S(1)} %collective-permute-done.9.refs_11_), channel_id=1, source_target_pairs={{0,8},{8,16},{16,24},{24,28},{28,20},{20,12},{12,4},{4,0},{1,9},{9... | collective-permute-start | bytes 786440 | tf_op jit(solution)/shard_map/ppermute | solution.py:67
  49.6 11.2 %collective-permute-start.6 = (bf16[256,512]{1,0:T(8,128)(2,1)S(1)}, bf16[256,512]{1,0:T(8,128)(2,1)S(1)}, u32[]{:S(2)}, u32[]{:S(2)}) collective-permute-start(bf16[256,512]{1,0:T(8,128)(2,1)S(1)} %collective-permute-done.4.refs_5_), channel_id=1, source_target_pairs={{0,8},{8,16},{16,24},{24,28},{28,20},{20,12},{12,4},{4,0},{1,9},{9... | collective-permute-start | bytes 786440 | tf_op jit(solution)/shard_map/ppermute | solution.py:67
  51.8 12.1 %collective-permute-start.13 = (bf16[256,512]{1,0:T(8,128)(2,1)}, bf16[256,512]{1,0:T(8,128)(2,1)}, u32[]{:S(2)}, u32[]{:S(2)}) collective-permute-start(bf16[256,512]{1,0:T(8,128)(2,1)} %collective-permute-done.12.refs_14_), channel_id=1, source_target_pairs={{8,0},{16,8},{24,16},{28,24},{20,28},{12,20},{4,12},{0,4},{9,1},{1... | collective-permute-start | bytes 786440 | tf_op jit(solution)/shard_map/ppermute | solution.py:67
  51.8 20.6 %collective-permute-start.20 = (bf16[256,512]{1,0:T(8,128)(2,1)S(1)}, bf16[256,512]{1,0:T(8,128)(2,1)}, u32[]{:S(2)}, u32[]{:S(2)}) collective-permute-start(bf16[256,512]{1,0:T(8,128)(2,1)S(1)} %collective-permute-done.18.refs_2_), channel_id=1, source_target_pairs={{8,0},{16,8},{24,16},{28,24},{20,28},{12,20},{4,12},{0,4},{9,1},{1... | collective-permute-start | bytes 786440 | tf_op jit(solution)/shard_map/ppermute | solution.py:67
  57.4 16.6 %collective-permute-start.29 = (bf16[512,256]{1,0:T(8,128)(2,1)S(1)}, bf16[512,256]{1,0:T(8,128)(2,1)S(1)}, u32[]{:S(2)}, u32[]{:S(2)}) collective-permute-start(bf16[512,256]{1,0:T(8,128)(2,1)S(1)} %collective-permute-done.27.refs_4_), channel_id=1, source_target_pairs={{8,0},{16,8},{24,16},{28,24},{20,28},{12,20},{4,12},{0,4},{9,1},{1... | collective-permute-start | bytes 786440 | tf_op jit(solution)/shard_map/ppermute | solution.py:67
  57.4 17.0 %collective-permute-start.21 = (bf16[256,512]{1,0:T(8,128)(2,1)S(1)}, bf16[256,512]{1,0:T(8,128)(2,1)}, u32[]{:S(2)}, u32[]{:S(2)}) collective-permute-start(bf16[256,512]{1,0:T(8,128)(2,1)S(1)} %collective-permute-done.19.refs_3_), channel_id=1, source_target_pairs={{0,8},{8,16},{16,24},{24,28},{28,20},{20,12},{12,4},{4,0},{1,9},{9... | collective-permute-start | bytes 786440 | tf_op jit(solution)/shard_map/ppermute | solution.py:67
  60.9 15.2 %collective-permute-start.26 = (bf16[512,256]{1,0:T(8,128)(2,1)S(1)}, bf16[512,256]{1,0:T(8,128)(2,1)S(1)}, u32[]{:S(2)}, u32[]{:S(2)}) collective-permute-start(bf16[512,256]{1,0:T(8,128)(2,1)S(1)} %collective-permute-done.24.refs_1_), channel_id=1, source_target_pairs={{0,8},{8,16},{16,24},{24,28},{28,20},{20,12},{12,4},{4,0},{1,9},{9... | collective-permute-start | bytes 786440 | tf_op jit(solution)/shard_map/ppermute | solution.py:67
  70.8 6.4 %collective-permute-start.16 = (bf16[4,128,128]{2,1,0:T(8,128)(2,1)}, bf16[4,128,128]{2,1,0:T(8,128)(2,1)S(1)}, u32[]{:S(2)}, u32[]{:S(2)}) collective-permute-start(bf16[4,128,128]{2,1,0:T(8,128)(2,1)} %get-tuple-element.25), channel_id=1, source_target_pairs={{0,12},{4,8},{8,4},{12,0},{16,28},{20,24},{24,20},{28,16},{1,13},{... | collective-permute-start | bytes 393224 | tf_op jit(solution)/shard_map/ppermute | solution.py:387
  72.4 7.9 %collective-permute-start.15 = (bf16[4,128,128]{2,1,0:T(8,128)(2,1)}, bf16[4,128,128]{2,1,0:T(8,128)(2,1)S(1)}, u32[]{:S(2)}, u32[]{:S(2)}) collective-permute-start(bf16[4,128,128]{2,1,0:T(8,128)(2,1)} %get-tuple-element.25), channel_id=1, source_target_pairs={{0,8},{4,12},{8,0},{12,4},{16,24},{20,28},{24,16},{28,20},{1,9},{5... | collective-permute-start | bytes 393224 | tf_op jit(solution)/shard_map/ppermute | solution.py:387
  74.0 7.0 %collective-permute-start.14 = (bf16[4,128,128]{2,1,0:T(8,128)(2,1)}, bf16[4,128,128]{2,1,0:T(8,128)(2,1)S(1)}, u32[]{:S(2)}, u32[]{:S(2)}) collective-permute-start(bf16[4,128,128]{2,1,0:T(8,128)(2,1)} %get-tuple-element.25), channel_id=1, source_target_pairs={{0,4},{4,0},{8,12},{12,8},{16,20},{20,16},{24,28},{28,24},{1,5},{5... | collective-permute-start | bytes 393224 | tf_op jit(solution)/shard_map/ppermute | solution.py:387
  74.4 12.3 %collective-permute-start.22 = (bf16[256,512]{1,0:T(8,128)(2,1)}, bf16[256,512]{1,0:T(8,128)(2,1)S(1)}, u32[]{:S(2)}, u32[]{:S(2)}) collective-permute-start(bf16[256,512]{1,0:T(8,128)(2,1)} %collective-permute-done.20.refs_4_), channel_id=1, source_target_pairs={{8,0},{16,8},{24,16},{28,24},{20,28},{12,20},{4,12},{0,4},{9,1},{1... | collective-permute-start | bytes 786440 | tf_op jit(solution)/shard_map/ppermute | solution.py:67
  76.1 10.6 %collective-permute-start.23 = (bf16[256,512]{1,0:T(8,128)(2,1)}, bf16[256,512]{1,0:T(8,128)(2,1)S(1)}, u32[]{:S(2)}, u32[]{:S(2)}) collective-permute-start(bf16[256,512]{1,0:T(8,128)(2,1)} %collective-permute-done.21.refs_5_), channel_id=1, source_target_pairs={{0,8},{8,16},{16,24},{24,28},{28,20},{20,12},{12,4},{4,0},{1,9},{9... | collective-permute-start | bytes 786440 | tf_op jit(solution)/shard_map/ppermute | solution.py:67
  77.3 17.5 %collective-permute-start.28 = (bf16[512,256]{1,0:T(8,128)(2,1)S(1)}, bf16[512,256]{1,0:T(8,128)(2,1)S(1)}, u32[]{:S(2)}, u32[]{:S(2)}) collective-permute-start(bf16[512,256]{1,0:T(8,128)(2,1)S(1)} %collective-permute-done.26.refs_3_), channel_id=1, source_target_pairs={{0,8},{8,16},{16,24},{24,28},{28,20},{20,12},{12,4},{4,0},{1,9},{9... | collective-permute-start | bytes 786440 | tf_op jit(solution)/shard_map/ppermute | solution.py:67
  80.2 14.6 %collective-permute-start.30 = (bf16[512,256]{1,0:T(8,128)(2,1)S(1)}, bf16[512,256]{1,0:T(8,128)(2,1)S(1)}, u32[]{:S(2)}, u32[]{:S(2)}) collective-permute-start(bf16[512,256]{1,0:T(8,128)(2,1)S(1)} %collective-permute-done.29.refs_6_), channel_id=1, source_target_pairs={{8,0},{16,8},{24,16},{28,24},{20,28},{12,20},{4,12},{0,4},{9,1},{1... | collective-permute-start | bytes 786440 | tf_op jit(solution)/shard_map/ppermute | solution.py:67
  82.0 12.8 %collective-permute-start.31 = (bf16[4,128,128]{2,1,0:T(8,128)(2,1)S(1)}, bf16[4,128,128]{2,1,0:T(8,128)(2,1)S(1)}, u32[]{:S(2)}, u32[]{:S(2)}) collective-permute-start(bf16[4,128,128]{2,1,0:T(8,128)(2,1)S(1)} %convert_add_fusion), channel_id=1, source_target_pairs={{0,16},{4,20},{8,24},{12,28},{16,0},{20,4},{24,8},{28,12},{1,17},{... | collective-permute-start | bytes 393224 | tf_op jit(solution)/shard_map/ppermute | solution.py:387
  101.6 2.0 %collective-permute-start.32 = (bf16[512,512]{1,0:T(8,128)(2,1)S(1)}, bf16[512,512]{1,0:T(8,128)(2,1)S(1)}, u32[]{:S(2)}, u32[]{:S(2)}) collective-permute-start(bf16[512,512]{1,0:T(8,128)(2,1)S(1)} %get-tuple-element.35), channel_id=1, source_target_pairs={{0,1},{1,0},{2,3},{3,2},{4,5},{5,4},{6,7},{7,6},{8,9},{9,8},{10,11... | collective-permute-start | bytes 1572872 | tf_op jit(solution)/shard_map/ppermute | solution.py:414
  103.7 14.0 %collective-permute-start.34 = (bf16[512,512]{1,0:T(8,128)(2,1)S(1)}, bf16[512,512]{1,0:T(8,128)(2,1)S(1)}, u32[]{:S(2)}, u32[]{:S(2)}) collective-permute-start(bf16[512,512]{1,0:T(8,128)(2,1)S(1)} %add_convert_fusion.1), channel_id=1, source_target_pairs={{0,2},{1,3},{2,0},{3,1},{4,6},{5,7},{6,4},{7,5},{8,10},{9,11},{10,... | collective-permute-start | bytes 1572872 | tf_op jit(solution)/shard_map/ppermute | solution.py:414
  107.0 10.7 %collective-permute-start.33 = (bf16[512,512]{1,0:T(8,128)(2,1)S(1)}, bf16[512,512]{1,0:T(8,128)(2,1)S(1)}, u32[]{:S(2)}, u32[]{:S(2)}) collective-permute-start(bf16[512,512]{1,0:T(8,128)(2,1)S(1)} %get-tuple-element.38), channel_id=1, source_target_pairs={{0,1},{1,0},{2,3},{3,2},{4,5},{5,4},{6,7},{7,6},{8,9},{9,8},{10,11... | collective-permute-start | bytes 1572872 | tf_op jit(solution)/shard_map/ppermute | solution.py:414
  (9 other events, 43.4 us)
